TPU v7x, 256 devices: a whole 4x4x8 slice. The times are simulated.
256 devices in a mesh: dp: 4 (over x), ctx: 8 (over y, core), tp: 8 (over z).
Axes of the slice: x: 4, y: 4, z: 8, core: 2. Of those that a mesh axis runs over, the one named last changes fastest.
Arguments:
- hidden: bfloat16 [4, 2048, 8192], P('dp', ('ctx', 'tp')), may hold values from -6 to 6
- key_weight: bfloat16 [8192, 1024], P(None, 'tp'), may hold values from -0.0625 to 0.0625
- value_weight: bfloat16 [8192, 1024], P(None, 'tp'), may hold values from -0.0625 to 0.0625
- queries: bfloat16 [4, 2048, 8192], P('dp', 'ctx', 'tp'), may hold values from -200 to 200
- out_grad: bfloat16 [4, 2048, 8192], P('dp', 'ctx', 'tp'), may hold values from -6 to 6
- segment_ids: int32 [4, 2048], P('dp', 'ctx'), may hold values from 0 to 7, never falling along the last dimension, each value on 1 to 1024 neighbouring positions
Outputs:
- attended: bfloat16 [4, 2048, 8192], P('dp', 'ctx', 'tp')
- query_grad: bfloat16 [4, 2048, 8192], P('dp', 'ctx', 'tp')
- hidden_grad: bfloat16 [4, 2048, 8192], P('dp', ('ctx', 'tp'))
- key_weight_grad: float32 [8192, 1024], P(('dp', 'ctx'), 'tp')
- value_weight_grad: float32 [8192, 1024], P(('dp', 'ctx'), 'tp')
Inputs may be any that keep to these rules, and one draw needn't show every extreme that they name: `segment_ids`: document numbers never fall along a bin, each document holds 1 to 1024 tokens, and one holds exactly 1024.
All inputs are finite; a program needn't handle non-finite values.
Results may differ from a plain program's by a relative error of at most 0.03.
The roundings to bfloat16 on the way count: a program that leaves them out, or rounds other values in their place, can miss the bound.
Values may be sent and summed in bfloat16 or wider, within the bound.
No kernel may reach another device: no remote copies, remote signals or barrier semaphores. Data moves between devices by JAX's collectives and lax.ppermute only.
A program may use at most 128 MiB of HBM per device.

v0:
```python
import math

import jax
import jax.numpy as jnp
from jax import lax
from jax.sharding import PartitionSpec as P

D = 8192
HQ = 64
KVH = 8
HD = 128


def on_device(hidden, key_weight, value_weight, queries, out_grad, segment_ids):
    scale = 1.0 / math.sqrt(HD)
    group = HQ // KVH
    kv_cols = key_weight.shape[1]
    kv_local = kv_cols // HD
    rows = queries.shape[1]
    x_count = hidden.shape[1]
    gathered = lax.all_gather(hidden[0], "tp", axis=0, tiled=True)
    weights = jnp.concatenate([key_weight, value_weight], axis=1)
    projected = jnp.dot(gathered, weights, preferred_element_type=jnp.float32)
    keys = projected[:, :kv_cols].astype(jnp.bfloat16)
    values = projected[:, kv_cols:].astype(jnp.bfloat16)
    own_seg = segment_ids[0].reshape(rows, 1)
    all_keys, all_values, all_seg = (
        lax.all_gather(keys, "ctx", axis=0, tiled=True),
        lax.all_gather(values, "ctx", axis=0, tiled=True),
        lax.all_gather(own_seg, "ctx", axis=0, tiled=True),
    )
    total = all_keys.shape[0]
    first = lax.axis_index("ctx") * rows
    query_place = first + jnp.arange(rows)
    key_place = jnp.arange(total)
    mask = (own_seg == all_seg.reshape(1, total)) & (key_place[None, :] <= query_place[:, None])
    query_heads = queries[0].reshape(rows, kv_local, group, HD)
    grad_heads = out_grad[0].reshape(rows, kv_local, group, HD)
    key_heads = all_keys.reshape(total, kv_local, HD)
    value_heads = all_values.reshape(total, kv_local, HD)
    scores = (
        jnp.einsum("qhgd,khd->hgqk", query_heads, key_heads, preferred_element_type=jnp.float32)
        * scale
    )
    scores = jnp.where(mask[None, None], scores, -jnp.inf)
    top = jnp.max(scores, axis=-1, keepdims=True)
    expd = jnp.exp(scores - top)
    prob = expd / jnp.sum(expd, axis=-1, keepdims=True)
    prob_b = prob.astype(jnp.bfloat16)
    attended = jnp.einsum(
        "hgqk,khd->qhgd", prob_b, value_heads, preferred_element_type=jnp.float32
    ).astype(jnp.bfloat16)
    delta = jnp.sum(grad_heads.astype(jnp.float32) * attended.astype(jnp.float32), axis=-1)
    delta = jnp.transpose(delta, (1, 2, 0))
    dprob = jnp.einsum(
        "qhgd,khd->hgqk", grad_heads, value_heads, preferred_element_type=jnp.float32
    )
    dscore_b = (prob * (dprob - delta[..., None])).astype(jnp.bfloat16)
    query_grad = (
        jnp.einsum("hgqk,khd->qhgd", dscore_b, key_heads, preferred_element_type=jnp.float32)
        * scale
    ).astype(jnp.bfloat16)
    key_part = (
        jnp.einsum("hgqk,qhgd->khd", dscore_b, query_heads, preferred_element_type=jnp.float32)
        * scale
    )
    value_part = jnp.einsum(
        "hgqk,qhgd->khd", prob_b, grad_heads, preferred_element_type=jnp.float32
    )
    kv_grads = lax.psum_scatter(
        jnp.concatenate(
            [
                key_part.reshape(lax.axis_size("ctx") * rows, kv_cols),
                value_part.reshape(lax.axis_size("ctx") * rows, kv_cols),
            ],
            axis=1,
        ),
        "ctx",
        scatter_dimension=0,
        tiled=True,
    ).astype(jnp.bfloat16)
    hidden_grad = lax.psum_scatter(
        lax.dot_general(
            kv_grads, weights, (((1,), (1,)), ((), ())), preferred_element_type=jnp.float32
        ),
        "tp",
        scatter_dimension=0,
        tiled=True,
    ).astype(jnp.bfloat16)
    summed = lax.psum_scatter(
        lax.dot_general(
            gathered, kv_grads, (((0,), (0,)), ((), ())), preferred_element_type=jnp.float32
        ),
        ("dp", "ctx"),
        scatter_dimension=0,
        tiled=True,
    )
    return (
        attended.reshape(1, rows, kv_local * group * HD),
        query_grad.reshape(1, rows, kv_local * group * HD),
        hidden_grad.reshape(1, x_count, D),
        summed[:, :kv_cols],
        summed[:, kv_cols:],
    )


def solution(mesh):
    in_specs = (
        P("dp", ("ctx", "tp"), None),
        P(None, "tp"),
        P(None, "tp"),
        P("dp", "ctx", "tp"),
        P("dp", "ctx", "tp"),
        P("dp", "ctx"),
    )
    out_specs = (
        P("dp", "ctx", "tp"),
        P("dp", "ctx", "tp"),
        P("dp", ("ctx", "tp"), None),
        P(("dp", "ctx"), "tp"),
        P(("dp", "ctx"), "tp"),
    )
    return jax.shard_map(
        on_device, mesh=mesh, in_specs=in_specs, out_specs=out_specs, check_vma=False
    )
```

profile of v0, /device:TPU:2, one launch (start us, length us, event | category | flops | bytes accessed | tf_op | source)
XLA Modules:
  0.0 395.9 jit_solution(16850897480752182110)
XLA Ops:
  7.2 0.0 all-gather.4.cloned.1.call-start
  7.2 0.7 all-gather.4.cloned.1.call-update
  7.9 0.0 reduce-scatter.4.cloned.1.call-start
  7.9 1.2 copy.16
  9.2 2.0 copy.35
  11.2 1.2 copy.34
  12.5 11.1 %all-gather.1 = s32[1,2048]{1,0:T(1,128)S(1)} all-gather(s32[1,256]{1,0:T(1,128)} %param.11), channel_id=3, replica_groups=mesh['dp'=4,'ctx'=8,'tp'=8] {'ctx'}, dimensions={1}, use_global_device_ids=true | all-gather | bytes 9216 | tf_op jit(solution)/shard_map/all_gather | solution.py:30
  23.6 1.2 fusion.18
  24.8 3.1 constant_dynamic-update-slice_fusion.1
  27.8 3.2 constant_dynamic-update-slice_fusion
  31.0 36.6 %all-gather.4.cloned.1.call-done = bf16[1,256,8192]{2,1,0:T(8,128)(2,1)} async-done(((bf16[1,32,8192]{2,1,0:T(8,128)(2,1)}), bf16[1,256,8192]{2,1,0:T(8,128)(2,1)}) %all-gather.4.cloned.1.call-update) | async-done | bytes 4194320 | tf_op jit(solution)/shard_map/all_gather | solution.py:21
  67.6 4.8 %fusion.26 = bf16[256,256]{0,1:T(8,128)(2,1)S(1)} fusion(bf16[8192,256]{1,0:T(8,128)(2,1)} %constant_dynamic-update-slice_fusion, bf16[1,256,8192]{2,1,0:T(8,128)(2,1)} %all-gather.4.cloned.1.call-done), kind=kOutput, calls=%fused_computation.28 | convolution fusion | flops 1073807360 | bytes 8519680 | tf_op jit(solution)/shard_map/dot_general | solution.py:23
  72.4 13.5 %all_gather.15 = bf16[2048,128]{0,1:T(8,128)(2,1)S(1)} all-gather(bf16[256,128]{0,1:T(8,128)(2,1)S(1)} %get-tuple-element.12), channel_id=1, replica_groups=mesh['dp'=4,'ctx'=8,'tp'=8] {'ctx'}, dimensions={0}, use_global_device_ids=true | all-gather | bytes 589824 | tf_op jit(solution)/shard_map/all_gather | solution.py:28
  85.8 14.4 %all_gather.13 = bf16[2048,128]{0,1:T(8,128)(2,1)} all-gather(bf16[256,128]{0,1:T(8,128)(2,1)S(1)} %get-tuple-element.13), channel_id=1, replica_groups=mesh['dp'=4,'ctx'=8,'tp'=8] {'ctx'}, dimensions={0}, use_global_device_ids=true | all-gather | bytes 589824 | tf_op jit(solution)/shard_map/all_gather | solution.py:29
  100.2 7.2 %fusion.4 = (f32[8,256]{1,0:T(8,128)S(1)}, f32[2048,256,8]{1,0,2:T(8,128)}) fusion(pred[256,2048]{0,1:T(8,128)(4,1)S(1)} %fusion.18, bf16[256,8,128]{0,2,1:T(8,128)(2,1)S(1)} %bitcast.111, bf16[2048,128]{0,1:T(8,128)(2,1)S(1)} %all_gather.15), kind=kOutput, calls=%fused_computation.7 | convolution fusion | flops 1086322688 | bytes 18358272 | tf_op jit(solution)/shard_map/qhgd,khd->hgqk/dot_general | solution.py:42
  107.4 9.3 %fusion.3 = f32[8,256]{1,0:T(8,128)S(1)} fusion(f32[2048,256,8]{1,0,2:T(8,128)} %get-tuple-element.15, f32[8,256]{1,0:T(8,128)S(1)} %get-tuple-element.14, pred[256,2048]{0,1:T(8,128)(4,1)S(1)} %fusion.18), kind=kLoop, calls=%fused_computation.6 | loop fusion | flops 16775168 | bytes 17317888 | tf_op jit(solution)/shard_map/reduce_sum | solution.py:48
  116.7 0.0 copy-start
  116.7 0.0 copy-start.3
  116.7 9.5 %fusion.14 = f32[2048,128]{0,1:T(8,128)} fusion(bf16[256,8,128]{0,2,1:T(8,128)(2,1)} %bitcast.116, f32[8,256]{1,0:T(8,128)S(1)} %fusion.3, f32[8,256]{1,0:T(8,128)S(1)} %get-tuple-element.14, f32[2048,256,8]{1,0,2:T(8,128)} %get-tuple-element.15, pred[256,2048]{0,1:T(8,128)(4,1)S(1)} %fusion.18), kind=kOutput, calls=%fused_computation.18 | convolution fusion | flops 1094713344 | bytes 18890752 | tf_op jit(solution)/shard_map/hgqk,qhgd->khd/dot_general | solution.py:67
  126.1 1.6 copy-done
  127.7 0.0 copy-done.3
  127.8 5.5 %multiply_reduce_fusion = (f32[256,8]{0,1:T(8,128)S(1)}, bf16[128,8,256]{2,0,1:T(8,128)(2,1)}) fusion(f32[256,1,8,128]{0,3,2,1:T(8,128)S(1)} %bitcast.114, f32[8,256]{1,0:T(8,128)S(1)} %fusion.3, f32[8,256]{1,0:T(8,128)S(1)} %get-tuple-element.14, f32[2048,256,8]{1,0,2:T(8,128)S(1)} %copy-done, pred[256,2048]{0,1:T(8,128)(4,1)S(1)} %fusion.18, ...), kind=kOutput, calls=%fused_computation.29 | convolution fusion | flops 1095759872 | bytes 19423232 | tf_op jit(solution)/shard_map/hgqk,khd->qhgd/dot_general | solution.py:50
  133.3 8.8 %fusion.5 = bf16[8,256,2048]{1,2,0:T(8,128)(2,1)} fusion(f32[8,256]{1,0:T(8,128)S(1)} %bitcast.120, f32[8,256]{1,0:T(8,128)S(1)} %fusion.3, f32[8,256]{1,0:T(8,128)S(1)} %get-tuple-element.14, f32[2048,256,8]{1,0,2:T(8,128)S(1)} %copy-done, pred[256,2048]{0,1:T(8,128)(4,1)S(1)} %fusion.18, bf16[256,8,128]{0,2,1:T(8,128)(2,1)} %bitcast.117, ...), kind=kOutput, calls=%fused_computation.9 | convolution fusion | flops 1103101952 | bytes 26763264 | tf_op jit(solution)/shard_map/qhgd,khd->hgqk/dot_general | solution.py:55
  142.1 0.0 copy-start.2
  142.1 6.3 %fusion.17 = f32[2048,128]{0,1:T(8,128)S(1)} fusion(bf16[8,256,2048]{1,2,0:T(8,128)(2,1)} %fusion.5, bf16[256,8,128]{0,2,1:T(8,128)(2,1)S(1)} %bitcast.112), kind=kOutput, calls=%fused_computation.20 | convolution fusion | flops 1074003968 | bytes 9961472 | tf_op jit(solution)/shard_map/hgqk,qhgd->khd/dot_general | solution.py:64
  148.4 0.0 copy-done.2
  148.4 1.5 pad_maximum_fusion
  149.9 0.0 reduce-scatter.4.cloned.1.call-update
  149.9 0.0 reduce-scatter.8.cloned.1.call-start
  149.9 34.3 %reduce-scatter.4.cloned.1.call-done = f32[256,256]{0,1:T(8,128)} async-done(((f32[2048,256]{0,1:T(8,128)}), f32[256,256]{0,1:T(8,128)}) %reduce-scatter.4.cloned.1.call-update) | async-done | bytes 262160 | tf_op jit(solution)/shard_map/reduce_scatter | solution.py:70
  184.3 0.0 copy-start.1
  184.3 6.8 %convolution_bitcast_fusion = f32[8192,256]{0,1:T(8,128)} fusion(bf16[1,256,8192]{2,1,0:T(8,128)(2,1)} %all-gather.4.cloned.1.call-done, f32[256,256]{0,1:T(8,128)} %reduce-scatter.4.cloned.1.call-done), kind=kOutput, calls=%fused_computation.8 | convolution fusion | flops 1073807360 | bytes 12845056 | tf_op jit(solution)/shard_map/dot_general | solution.py:91
  191.1 0.0 reduce-scatter.8.cloned.1.call-update
  191.1 0.0 copy-start.4
  191.1 0.0 reduce-scatter.6.cloned.1.call-start
  191.1 0.0 copy-done.1
  191.1 6.8 %fusion.35 = f32[256,8192]{1,0:T(8,128)} fusion(bf16[8192,256]{1,0:T(8,128)(2,1)} %constant_dynamic-update-slice_fusion, f32[256,256]{0,1:T(8,128)S(1)} %copy-done.1), kind=kOutput, calls=%fused_computation.37 | convolution fusion | flops 1073807360 | bytes 12845056 | tf_op jit(solution)/shard_map/dot_general | solution.py:83
  197.9 0.0 reduce-scatter.6.cloned.1.call-update
  197.9 0.0 copy-done.4
  198.0 1.0 copy.22
  199.0 4.9 %fusion.19 = bf16[128,8,256]{2,0,1:T(8,128)(2,1)S(1)} fusion(bf16[8,256,2048]{1,2,0:T(8,128)(2,1)} %fusion.5, bf16[2048,128]{0,1:T(8,128)(2,1)S(1)} %all_gather.15), kind=kOutput, calls=%fused_computation.25 | convolution fusion | flops 1074266112 | bytes 9437184 | tf_op jit(solution)/shard_map/hgqk,khd->qhgd/dot_general | solution.py:60
  203.8 1.0 copy.23
  204.8 85.2 %reduce-scatter.8.cloned.1.call-done = f32[256,256]{0,1:T(8,128)} async-done(((f32[8192,256]{0,1:T(8,128)}), f32[256,256]{0,1:T(8,128)}) %reduce-scatter.8.cloned.1.call-update) | async-done | bytes 262160 | tf_op jit(solution)/shard_map/reduce_scatter | solution.py:90
  290.1 1.0 fusion.39
  291.1 0.8 copy.24
  291.8 0.8 copy.25
  292.6 94.7 %reduce-scatter.6.cloned.1.call-done = f32[32,8192]{1,0:T(8,128)} async-done(((f32[256,8192]{1,0:T(8,128)}), f32[32,8192]{1,0:T(8,128)}) %reduce-scatter.6.cloned.1.call-update) | async-done | bytes 1048592 | tf_op jit(solution)/shard_map/reduce_scatter | solution.py:82
  387.3 2.1 convert_bitcast_fusion
  (2 shorter events, 0.0 us)
Async XLA Ops:
  7.2 60.4 %all-gather.4.cloned.1.call-start = ((), (), s32[]{:S(2)}) async-start(), calls=%async_computation.6 | async-start | bytes 4718592 | tf_op jit(solution)/shard_map/all_gather | solution.py:21
  7.9 176.4 %reduce-scatter.4.cloned.1.call-start = ((), (), s32[]{:S(2)}) async-start(), calls=%async_computation.3 | async-start | bytes 2359296 | tf_op jit(solution)/shard_map/reduce_scatter | solution.py:70
  116.7 11.1 %copy-start = (f32[2048,256,8]{1,0,2:T(8,128)S(1)}, f32[2048,256,8]{1,0,2:T(8,128)}, u32[]{:S(2)}) copy-start(f32[2048,256,8]{1,0,2:T(8,128)} %get-tuple-element.15) | copy-start | bytes 50331652
  116.7 11.1 %copy-start.3 = (bf16[2048,128]{0,1:T(8,128)(2,1)S(1)}, bf16[2048,128]{0,1:T(8,128)(2,1)}, u32[]{:S(2)}) copy-start(bf16[2048,128]{0,1:T(8,128)(2,1)} %all_gather.13) | copy-start | bytes 1572868
  142.1 6.3 %copy-start.2 = (f32[2048,128]{0,1:T(8,128)S(1)}, f32[2048,128]{0,1:T(8,128)}, u32[]{:S(2)}) copy-start(f32[2048,128]{0,1:T(8,128)} %fusion.14) | copy-start | bytes 3145732
  149.9 140.2 %reduce-scatter.8.cloned.1.call-start = ((), (), s32[]{:S(2)}) async-start(), calls=%async_computation.5 | async-start | bytes 8650752 | tf_op jit(solution)/shard_map/reduce_scatter | solution.py:90
  184.3 6.9 %copy-start.1 = (f32[256,256]{0,1:T(8,128)S(1)}, f32[256,256]{0,1:T(8,128)}, u32[]{:S(2)}) copy-start(f32[256,256]{0,1:T(8,128)} %reduce-scatter.4.cloned.1.call-done) | copy-start | bytes 786436
  191.1 6.9 %copy-start.4 = (bf16[128,8,256]{2,0,1:T(8,128)(2,1)S(1)}, bf16[128,8,256]{2,0,1:T(8,128)(2,1)}, u32[]{:S(2)}) copy-start(bf16[128,8,256]{2,0,1:T(8,128)(2,1)} %get-tuple-element.17) | copy-start | bytes 1572868
  191.1 196.2 %reduce-scatter.6.cloned.1.call-start = ((), (), s32[]{:S(2)}) async-start(), calls=%async_computation.4 | async-start | bytes 9437184 | tf_op jit(solution)/shard_map/reduce_scatter | solution.py:82
Sparse Core Ops, SparseCore 0:
  9.8 57.7 all-gather.3
  150.0 34.1 reduce-scatter.3
  191.2 98.8 reduce-scatter.7
  292.6 94.6 reduce-scatter.5
where the time goes:
time: 397 us; the launch traced here: 396 us
  waiting for transfers between devices  252 us (63%)
  matrix products  60.5 us (15%)
  blocking collectives  38.9 us (10%)
  local copies, waits for them, and re-layouts  16.9 us (4%)
  other arithmetic  14 us (4%)
  between operations  13.9 us (4%)
    reduce_scatter x1, waiting for transfers between devices, on_device(): lax.psum_scatter(lax.dot_general(kv_grads, weights, (((1,), (1,)), ((), (...  94.7 us
    reduce_scatter x1, waiting for transfers between devices, on_device(): lax.psum_scatter(lax.dot_general(gathered, kv_grads, (((0,), (0,)), ((),...  85.2 us
    all_gather x1, waiting for transfers between devices, on_device(): gathered = lax.all_gather(hidden[0], 'tp', axis=0, tiled=True)  36.6 us
    reduce_scatter x1, waiting for transfers between devices, on_device(): lax.psum_scatter(jnp.concatenate([key_part.reshape(lax.axis_size('ctx') *...  34.3 us
    all_gather x1, blocking collectives, on_device(): lax.all_gather(values, 'ctx', axis=0, tiled=True)  14.4 us
    all_gather x1, blocking collectives, on_device(): lax.all_gather(keys, 'ctx', axis=0, tiled=True)  13.5 us
    all_gather x1, blocking collectives, on_device(): lax.all_gather(own_seg, 'ctx', axis=0, tiled=True)  11.1 us
    dot_general x1, matrix products, on_device(): jnp.einsum('hgqk,qhgd->khd', prob_b, grad_heads, preferred_element_type=j...  9.45 us
  transfers between devices with their start and end apart: 4, of which 4 were waited for; matrix products, arithmetic and copies ran while one was open for 7% of the time, Pallas kernels for 0%

commit v1 on v0

v1 whole, which is shorter than its diff:
```python
import functools
import math

import jax
import jax.numpy as jnp
from jax import lax
from jax.experimental import pallas as pl
from jax.experimental.pallas import tpu as pltpu
from jax.sharding import Mesh, PartitionSpec as P

HD = 128
SLOTS = 5
NEG = -1e30
F32 = jnp.float32
BF16 = jnp.bfloat16


def attention_kernel(thr_ref, kv0, kv1, kv2, kv3, kv4, q_ref, do_ref,
                     att_ref, dq_ref, dkv_ref, k_all, v_all, kt_all, vt_all, s_ref, pb_ref):
    rows = q_ref.shape[0]
    scale = 1.0 / math.sqrt(HD)
    log2e = math.log2(math.e)
    head = pl.program_id(0)

    @pl.when(head == 0)
    def _():
        for j, kv in enumerate((kv0, kv1, kv2, kv3, kv4)):
            here = pl.ds(j * rows, rows)
            k = kv[:, :HD]
            v = kv[:, HD:]
            k_all[here, :] = k
            v_all[here, :] = v
            kt_all[:, here] = k.T
            vt_all[:, here] = v.T
        dkv_ref[...] = jnp.zeros_like(dkv_ref)

    q = q_ref[...]
    do = do_ref[...]
    top = jnp.full((1, rows), NEG, F32)
    place = lax.broadcasted_iota(jnp.int32, (rows, rows), 0)
    for j in range(SLOTS):
        here = pl.ds(j * rows, rows)
        s = lax.dot_general(k_all[here, :], q, (((1,), (1,)), ((), ())), preferred_element_type=F32)
        mask = place >= thr_ref[j:j + 1, :]
        if j == 0:
            mask = mask & (place <= lax.broadcasted_iota(jnp.int32, (rows, rows), 1))
        s = jnp.where(mask, s, NEG)
        s_ref[here, :] = s
        top = jnp.maximum(top, jnp.max(s, axis=0, keepdims=True))
    total = jnp.zeros((1, rows), F32)
    for j in range(SLOTS):
        here = pl.ds(j * rows, rows)
        e = jnp.exp2((s_ref[here, :] - top) * (scale * log2e))
        s_ref[here, :] = e
        total = total + jnp.sum(e, axis=0, keepdims=True)
    inv = 1.0 / total
    out_t = jnp.zeros((HD, rows), F32)
    for j in range(SLOTS):
        here = pl.ds(j * rows, rows)
        prob = s_ref[here, :] * inv
        s_ref[here, :] = prob
        prob_b = prob.astype(BF16)
        pb_ref[here, :] = prob_b
        out_t = out_t + jnp.dot(vt_all[:, here], prob_b, preferred_element_type=F32)
    out_b = out_t.astype(BF16)
    att_ref[...] = out_b.T
    delta = jnp.sum(do.T.astype(F32) * out_b.astype(F32), axis=0, keepdims=True)
    dq_t = jnp.zeros((HD, rows), F32)
    for j in range(SLOTS):
        here = pl.ds(j * rows, rows)
        dp = lax.dot_general(v_all[here, :], do, (((1,), (1,)), ((), ())), preferred_element_type=F32)
        ds = (s_ref[here, :] * (dp - delta)).astype(BF16)
        dq_t = dq_t + jnp.dot(kt_all[:, here], ds, preferred_element_type=F32)
        dkv_ref[here, :HD] += jnp.dot(ds, q, preferred_element_type=F32)
        dkv_ref[here, HD:] += jnp.dot(pb_ref[here, :], do, preferred_element_type=F32)
    dq_ref[...] = (dq_t * scale).astype(BF16).T

    @pl.when(head == pl.num_programs(0) - 1)
    def _():
        dkv_ref[:, :HD] = dkv_ref[:, :HD] * scale


def attention(thr, slots, q, do):
    rows, width = q.shape
    heads = width // HD
    whole = lambda h: (0, 0)
    return pl.pallas_call(
        attention_kernel,
        grid=(heads,),
        in_specs=[pl.BlockSpec(thr.shape, whole)]
        + [pl.BlockSpec((rows, 2 * HD), whole)] * SLOTS
        + [pl.BlockSpec((rows, HD), lambda h: (0, h))] * 2,
        out_specs=[
            pl.BlockSpec((rows, HD), lambda h: (0, h)),
            pl.BlockSpec((rows, HD), lambda h: (0, h)),
            pl.BlockSpec((SLOTS * rows, 2 * HD), whole),
        ],
        out_shape=[
            jax.ShapeDtypeStruct((rows, width), BF16),
            jax.ShapeDtypeStruct((rows, width), BF16),
            jax.ShapeDtypeStruct((SLOTS * rows, 2 * HD), F32),
        ],
        scratch_shapes=[
            pltpu.VMEM((SLOTS * rows, HD), BF16),
            pltpu.VMEM((SLOTS * rows, HD), BF16),
            pltpu.VMEM((HD, SLOTS * rows), BF16),
            pltpu.VMEM((HD, SLOTS * rows), BF16),
            pltpu.VMEM((SLOTS * rows, rows), F32),
            pltpu.VMEM((SLOTS * rows, rows), BF16),
        ],
        compiler_params=pltpu.CompilerParams(
            dimension_semantics=("arbitrary",), vmem_limit_bytes=40 * 1024 * 1024
        ),
        cost_estimate=pl.CostEstimate(
            flops=12 * SLOTS * rows * width * rows, bytes_accessed=6 * 1024 * 1024,
            transcendentals=SLOTS * rows * rows * heads,
        ),
    )(thr, *slots, q, do)


def on_device(hidden, key_weight, value_weight, queries, out_grad, segment_ids):
    rows = queries.shape[1]
    width = hidden.shape[2]
    x_count = hidden.shape[1]
    ny = lax.axis_size("y")
    chips = lax.axis_size("dp") * ny
    y = lax.axis_index("y")
    core = lax.axis_index("core")
    swap = [(0, 1), (1, 0)]

    gathered = lax.all_gather(hidden[0], "tp", axis=0, tiled=True)
    weights = jnp.concatenate([key_weight, value_weight], axis=1)

    all_seg = lax.all_gather(segment_ids[0], ("y", "core"), axis=0, tiled=True)
    starts = jnp.sum(
        (all_seg[None, :] < segment_ids[0][:, None]).astype(jnp.int32), axis=1
    ) - (2 * y + core) * rows
    back3 = jnp.where(core == 0, 1, 3) * rows
    back4 = jnp.where(core == 0, 3, 1) * rows
    backs = jnp.stack([jnp.int32(0), jnp.int32(2 * rows), jnp.int32(4 * rows), back3, back4])
    thr = starts[None, :] + jnp.concatenate([backs, jnp.zeros((3,), jnp.int32)])[:, None]

    kv = jnp.dot(gathered, weights, preferred_element_type=F32).astype(BF16)

    down1 = [(i, i + 1) for i in range(ny - 1)]
    down2 = [(i, i + 2) for i in range(ny - 2)]
    kv1 = lax.ppermute(kv, "y", down1)
    kv2 = lax.ppermute(kv, "y", down2)
    near = lax.ppermute(kv, "core", [(0, 1)])
    kv3 = lax.ppermute(kv1, "core", swap)
    far = lax.ppermute(kv2, "core", [(1, 0)])
    kv4 = jnp.where(core == 0, far, near)

    att, dq, dkv = attention(thr, (kv, kv1, kv2, kv3, kv4), queries[0], out_grad[0])

    cols = gathered.reshape(rows, chips, 2, width // (2 * chips))
    mine = jnp.where(core == 0, cols[:, :, 0], cols[:, :, 1])
    theirs = jnp.where(core == 0, cols[:, :, 1], cols[:, :, 0])
    other = lax.ppermute(theirs, "core", swap)

    part = dkv.reshape(SLOTS, rows, 2 * HD)
    up1 = [(i + 1, i) for i in range(ny - 1)]
    up2 = [(i + 2, i) for i in range(ny - 2)]
    got3 = lax.ppermute(part[3], "core", swap)
    got4 = lax.ppermute(part[4], "core", swap)
    own = part[0] + jnp.where(core == 0, got4, 0.0)
    send1 = (part[1] + got3).astype(BF16)
    send2 = (part[2] + jnp.where(core == 0, 0.0, got4)).astype(BF16)
    got1 = lax.ppermute(send1, "y", up1)
    got2 = lax.ppermute(send2, "y", up2)
    grads = (own + got1.astype(F32) + got2.astype(F32)).astype(BF16)

    spread = lax.dot_general(
        grads, weights, (((1,), (1,)), ((), ())), preferred_element_type=F32
    ).astype(BF16)
    hidden_grad = lax.psum_scatter(spread, "tp", scatter_dimension=0, tiled=True)

    other_grads = lax.ppermute(grads, "core", swap)
    contract = (((0,), (0,)), ((), ()))
    half = lax.dot_general(
        grads, mine.reshape(rows, -1), contract, preferred_element_type=F32
    ) + lax.dot_general(
        other_grads, other.reshape(rows, -1), contract, preferred_element_type=F32
    )
    blocks = jnp.transpose(half.astype(BF16).reshape(2 * HD, chips, -1), (1, 0, 2))
    blocks = lax.all_to_all(blocks, ("dp", "y"), 0, 0, tiled=True)
    summed = jnp.sum(blocks.astype(F32), axis=0).T
    return (
        att[None],
        dq[None],
        hidden_grad.reshape(1, x_count, width),
        summed[:, :HD],
        summed[:, HD:],
    )


def solution(mesh):
    fine = Mesh(
        mesh.devices.reshape(mesh.shape["dp"], mesh.shape["ctx"] // 2, 2, mesh.shape["tp"]),
        ("dp", "y", "core", "tp"),
    )
    ctx = ("y", "core")
    in_specs = (
        P("dp", ("y", "core", "tp"), None),
        P(None, "tp"),
        P(None, "tp"),
        P("dp", ctx, "tp"),
        P("dp", ctx, "tp"),
        P("dp", ctx),
    )
    out_specs = (
        P("dp", ctx, "tp"),
        P("dp", ctx, "tp"),
        P("dp", ("y", "core", "tp"), None),
        P(("dp", "y", "core"), "tp"),
        P(("dp", "y", "core"), "tp"),
    )
    return jax.shard_map(
        on_device, mesh=fine, in_specs=in_specs, out_specs=out_specs, check_vma=False
    )
```

time: 397 us -> 187 us (0.47)
  waiting for transfers between devices: 252 us -> 56.6 us
  matrix products: 60.5 us -> 11.6 us
  Pallas kernels: 0 us -> 18.5 us
  starting transfers between devices: 0.16 us -> 14.6 us
  other arithmetic: 14 us -> 5.39 us
  blocking collectives: 38.9 us -> 46.7 us
    reduce_scatter x3 -> x1, waiting for transfers between devices: 214 us -> 0.01 us  [on_device(): lax.psum_scatter(spread, 'tp', scatter_dimension=0, tiled=True)]
    dot_general x9 -> x4, matrix products: 60.5 us -> 11.6 us  [the longest x1 5.44 us: on_device(): lax.dot_general(grads, weights, (((1,), (1,)), ((), ())), preferred_eleme...]
    all_to_all x0 -> x1, blocking collectives: none -> 35.7 us  [on_device(): blocks = lax.all_to_all(blocks, ('dp', 'y'), 0, 0, tiled=True)]
    all_gather x3 -> x1, blocking collectives: 38.9 us -> 11 us  [on_device(): all_seg = lax.all_gather(segment_ids[0], ('y', 'core'), axis=0, tiled=True)]
    pallas_call x0 -> x1, Pallas kernels: none -> 18.5 us  [attention(): pl.pallas_call(attention_kernel, grid=(heads,), in_specs=[pl.BlockSpec(th...]
    ppermute x0 -> x11, starting transfers between devices: none -> 14.5 us  [the longest x1 4.92 us: on_device(): kv2 = lax.ppermute(kv, 'y', down2)]
    ppermute x0 -> x11, waiting for transfers between devices: none -> 13.3 us  [the longest x1 6.57 us: on_device(): got2 = lax.ppermute(send2, 'y', up2)]
    reduce_sum x1 -> x2, other arithmetic: 9.25 us -> 1.31 us  [the longest x1 1.03 us: on_device(): jnp.sum((all_seg[None, :] < segment_ids[0][:, None]).astype(jnp.int32), a...]
  transfers between devices with their start and end apart: 4 -> 13, of which waited for: 4 -> 8; matrix products, arithmetic and copies ran while one was open for 7% -> 13% of each run, Pallas kernels for 0% -> 0%
where the time goes in v1:
time: 187 us; the launch traced here: 186 us
  waiting for transfers between devices  56.6 us (30%)
  blocking collectives  46.7 us (25%)
  Pallas kernels  18.5 us (10%)
  local copies, waits for them, and re-layouts  18.1 us (10%)
  starting transfers between devices  14.6 us (8%)
  between operations  14.2 us (8%)
  matrix products  11.6 us (6%)
  other arithmetic  5.39 us (3%)
    all_gather x1, waiting for transfers between devices, on_device(): gathered = lax.all_gather(hidden[0], 'tp', axis=0, tiled=True)  42.6 us
    all_to_all x1, blocking collectives, on_device(): blocks = lax.all_to_all(blocks, ('dp', 'y'), 0, 0, tiled=True)  35.7 us
    pallas_call x1, Pallas kernels, attention(): pl.pallas_call(attention_kernel, grid=(heads,), in_specs=[pl.BlockSpec(th...  18.5 us
    all_gather x1, blocking collectives, on_device(): all_seg = lax.all_gather(segment_ids[0], ('y', 'core'), axis=0, tiled=True)  11 us
    unnamed x12, local copies, waits for them, and re-layouts  6.65 us
    ppermute x1, waiting for transfers between devices, on_device(): got2 = lax.ppermute(send2, 'y', up2)  6.57 us
    all_gather x1, local copies, waits for them, and re-layouts, on_device(): gathered = lax.all_gather(hidden[0], 'tp', axis=0, tiled=True)  6.39 us
    dot_general x1, matrix products, on_device(): lax.dot_general(grads, weights, (((1,), (1,)), ((), ())), preferred_eleme...  5.44 us
  transfers between devices with their start and end apart: 13, of which 8 were waited for; matrix products, arithmetic and copies ran while one was open for 13% of the time, Pallas kernels for 0%

profile of v1, /device:TPU:2, one launch (start us, length us, event | category | flops | bytes accessed | tf_op | source)
XLA Modules:
  0.0 185.7 jit_solution(16835530041321598334)
XLA Ops:
  7.2 0.0 all-gather.4.cloned.1.call-start
  7.2 0.7 all-gather.4.cloned.1.call-update
  7.9 0.0 reduce-scatter.2.cloned.1.call-start
  8.0 0.1 concatenate.6
  8.1 11.0 %all-gather = s32[1,2048]{1,0:T(1,128)S(1)} all-gather(s32[1,256]{1,0:T(1,128)} %param.11), channel_id=2, replica_groups=mesh['dp'=4,'y'=4,'core'=2,'tp'=8] {'y','core'}, dimensions={1}, use_global_device_ids=true | all-gather | bytes 9216 | tf_op jit(solution)/shard_map/all_gather | solution.py:134
  19.1 1.0 convert_reduce_fusion.1
  20.1 0.0 copy-start.3
  20.1 3.3 %constant_dynamic-update-slice_fusion.1 = bf16[8192,256]{1,0:T(8,128)(2,1)} fusion(bf16[8192,128]{1,0:T(8,128)(2,1)} %param.7), kind=kLoop, calls=%fused_computation.17 | loop fusion | bytes 4194304
  23.5 1.5 constant_dynamic-update-slice_fusion
  25.0 42.6 %all-gather.4.cloned.1.call-done = bf16[1,256,8192]{2,1,0:T(8,128)(2,1)} async-done(((bf16[1,32,8192]{2,1,0:T(8,128)(2,1)}), bf16[1,256,8192]{2,1,0:T(8,128)(2,1)}) %all-gather.4.cloned.1.call-update) | async-done | bytes 4194320 | tf_op jit(solution)/shard_map/all_gather | solution.py:131
  67.6 4.7 %fusion.6.kv0 = bf16[256,256]{1,0:T(8,128)(2,1)S(1)} fusion(bf16[8192,256]{1,0:T(8,128)(2,1)} %constant_dynamic-update-slice_fusion, bf16[1,256,8192]{2,1,0:T(8,128)(2,1)} %all-gather.4.cloned.1.call-done), kind=kOutput, calls=%fused_computation.11 | convolution fusion | flops 1073807360 | bytes 8519680 | tf_op jit(solution)/shard_map/dot_general | solution.py:143
  72.3 4.9 %collective-permute-start.1 = (bf16[256,256]{1,0:T(8,128)(2,1)S(1)}, bf16[256,256]{1,0:T(8,128)(2,1)S(1)}, u32[]{:S(2)}, u32[]{:S(2)}) collective-permute-start(bf16[256,256]{1,0:T(8,128)(2,1)S(1)} %fusion.6.kv0), channel_id=1, source_target_pairs={{0,32},{16,48},{1,33},{17,49},{2,34},{18,50},{3,35},{19,51},{4,36}... | collective-permute-start | bytes 393224 | tf_op jit(solution)/shard_map/ppermute | solution.py:148
  77.3 2.5 %collective-permute-start = (bf16[256,256]{1,0:T(8,128)(2,1)S(1)}, bf16[256,256]{1,0:T(8,128)(2,1)S(1)}, u32[]{:S(2)}, u32[]{:S(2)}) collective-permute-start(bf16[256,256]{1,0:T(8,128)(2,1)S(1)} %fusion.6.kv0), channel_id=1, source_target_pairs={{0,16},{16,32},{32,48},{1,17},{17,33},{33,49},{2,18},{18,34},{34,5... | collective-permute-start | bytes 393224 | tf_op jit(solution)/shard_map/ppermute | solution.py:147
  79.8 1.3 collective-permute-start.4
  81.1 0.0 collective-permute-done.1.kv2
  81.1 1.3 collective-permute-start.3
  82.4 0.1 broadcast_add_fusion.thr_ref
  82.4 0.3 collective-permute-done.kv1
  82.8 0.8 collective-permute-start.2
  83.6 0.0 collective-permute-done.4
  83.6 0.7 collective-permute-done.3
  84.3 0.3 collective-permute-done.2.kv3
  84.6 18.5 %shard_map.101 = (bf16[256,1024]{1,0:T(8,128)(2,1)}, bf16[256,1024]{1,0:T(8,128)(2,1)}, f32[1280,256]{1,0:T(8,128)S(1)}) custom-call(s32[8,256]{1,0:T(8,128)S(1)} %broadcast_add_fusion.thr_ref, bf16[256,256]{1,0:T(8,128)(2,1)S(1)} %fusion.6.kv0, bf16[256,256]{1,0:T(8,128)(2,1)S(1)} %collective-permute-done.kv1, ...), custom_call_target="tpu_custom_call" | custom-call | flops 4026531840 | bytes 6291456 | tf_op jit(solution)/shard_map/pallas_call | solution.py:87
  103.1 0.5 collective-permute-start.6
  103.6 0.1 collective-permute-start.5
  103.7 1.0 collective-permute-done.6
  104.7 0.4 collective-permute-done.5
  105.1 0.1 add_convert_fusion.2
  105.2 1.3 collective-permute-start.8
  106.5 1.3 collective-permute-start.7
  107.8 6.6 %collective-permute-done.8 = bf16[256,256]{1,0:T(8,128)(2,1)S(1)} collective-permute-done((bf16[256,256]{1,0:T(8,128)(2,1)S(1)}, bf16[256,256]{1,0:T(8,128)(2,1)S(1)}, u32[]{:S(2)}, u32[]{:S(2)}) %collective-permute-start.8) | collective-permute-done | bytes 131104 | tf_op jit(solution)/shard_map/ppermute | solution.py:170
  114.4 0.1 add_convert_fusion
  114.4 5.4 %convolution_convert_fusion = bf16[256,8192]{1,0:T(8,128)(2,1)} fusion(bf16[256,256]{1,0:T(8,128)(2,1)S(1)} %add_convert_fusion, bf16[8192,256]{1,0:T(8,128)(2,1)} %constant_dynamic-update-slice_fusion), kind=kOutput, calls=%fused_computation | convolution fusion | flops 1075838976 | bytes 8519680 | tf_op jit(solution)/shard_map/dot_general | solution.py:173
  119.9 0.0 reduce-scatter.2.cloned.1.call-update
  119.9 6.4 %copy.25 = bf16[1,256,8192]{1,2,0:T(8,128)(2,1)} copy(bf16[1,256,8192]{2,1,0:T(8,128)(2,1)} %all-gather.4.cloned.1.call-done) | data formatting | bytes 8388608 | tf_op jit(solution)/shard_map/all_gather | solution.py:131
  126.3 3.8 %broadcast_select_fusion.1 = (bf16[256,16,1,256]{0,3,2,1:T(8,128)(2,1)}, bf16[256,16,1,256]{0,3,2,1:T(8,128)(2,1)S(1)}) fusion(pred[]{:T(512)S(6)} %eq.2, bf16[256,16,2,256]{0,3,2,1:T(8,128)(2,1)} %bitcast.40), kind=kLoop, calls=%fused_computation.9 | loop fusion | flops 2097152 | bytes 8388609 | tf_op jit(solution)/shard_map/jit(_where)/select_n | solution.py:157
  130.1 3.2 %copy.26 = bf16[256,16,1,256]{3,1,0,2:T(8,128)(2,1)} copy(bf16[256,16,1,256]{0,3,2,1:T(8,128)(2,1)S(1)} %get-tuple-element.22) | data formatting | bytes 4194304 | tf_op jit(solution)/shard_map/jit(_where)/select_n | solution.py:158
  133.3 0.5 collective-permute-start.9
  133.8 4.0 %collective-permute-done.10 = bf16[256,16,256]{2,1,0:T(8,128)(2,1)S(1)} collective-permute-done((bf16[256,16,256]{2,1,0:T(8,128)(2,1)}, bf16[256,16,256]{2,1,0:T(8,128)(2,1)S(1)}, u32[]{:S(2)}, u32[]{:S(2)}) %collective-permute-start.10) | collective-permute-done | bytes 2097184 | tf_op jit(solution)/shard_map/ppermute | solution.py:159
  137.9 0.9 copy.34
  138.8 0.7 fusion.11
  139.6 0.9 copy-done.2
  140.4 0.8 fusion
  141.2 0.2 copy.36
  141.4 35.7 %all_to_all.5 = bf16[16,256,256]{2,1,0:T(8,128)(2,1)S(1)} all-to-all(bf16[16,256,256]{2,1,0:T(8,128)(2,1)S(1)} %bitcast.42), channel_id=1, replica_groups=mesh['dp'=4,'y'=4,'core'=2,'tp'=8] {'dp','y'}, dimensions={0} | all-to-all | bytes 4194304 | tf_op jit(solution)/shard_map/all_to_all | solution.py:186
  177.1 0.3 convert_reduce_fusion
  177.4 0.8 copy.29
  178.1 0.8 copy.30
  (15 shorter events, 0.1 us)
Async XLA Ops:
  7.2 60.4 %all-gather.4.cloned.1.call-start = ((), (), s32[]{:S(2)}) async-start(), calls=%async_computation.3 | async-start | bytes 4718592 | tf_op jit(solution)/shard_map/all_gather | solution.py:131
  7.9 171.0 %reduce-scatter.2.cloned.1.call-start = ((), (), s32[]{:S(2)}) async-start(), calls=%async_computation.2 | async-start | bytes 4718592 | tf_op jit(solution)/shard_map/reduce_scatter | solution.py:176
  20.1 3.3 %copy-start.3 = (bf16[8192,128]{1,0:T(8,128)(2,1)S(1)}, bf16[8192,128]{1,0:T(8,128)(2,1)}, u32[]{:S(2)}) copy-start(bf16[8192,128]{1,0:T(8,128)(2,1)} %param.8) | copy-start | bytes 6291460
  25.0 59.6 %copy-start = (bf16[1,256,1024]{2,1,0:T(8,128)(2,1)S(1)}, bf16[1,256,1024]{2,1,0:T(8,128)(2,1)}, u32[]{:S(2)}) copy-start(bf16[1,256,1024]{2,1,0:T(8,128)(2,1)} %param.9) | copy-start | bytes 1572868
  25.0 59.6 %copy-start.1 = (bf16[1,256,1024]{2,1,0:T(8,128)(2,1)S(1)}, bf16[1,256,1024]{2,1,0:T(8,128)(2,1)}, u32[]{:S(2)}) copy-start(bf16[1,256,1024]{2,1,0:T(8,128)(2,1)} %param.10) | copy-start | bytes 1572868
  72.3 8.8 %collective-permute-start.1 = (bf16[256,256]{1,0:T(8,128)(2,1)S(1)}, bf16[256,256]{1,0:T(8,128)(2,1)S(1)}, u32[]{:S(2)}, u32[]{:S(2)}) collective-permute-start(bf16[256,256]{1,0:T(8,128)(2,1)S(1)} %fusion.6.kv0), channel_id=1, source_target_pairs={{0,32},{16,48},{1,33},{17,49},{2,34},{18,50},{3,35},{19,51},{4,36}... | collective-permute-start | bytes 393224 | tf_op jit(solution)/shard_map/ppermute | solution.py:148
  77.3 5.5 %collective-permute-start = (bf16[256,256]{1,0:T(8,128)(2,1)S(1)}, bf16[256,256]{1,0:T(8,128)(2,1)S(1)}, u32[]{:S(2)}, u32[]{:S(2)}) collective-permute-start(bf16[256,256]{1,0:T(8,128)(2,1)S(1)} %fusion.6.kv0), channel_id=1, source_target_pairs={{0,16},{16,32},{32,48},{1,17},{17,33},{33,49},{2,18},{18,34},{34,5... | collective-permute-start | bytes 393224 | tf_op jit(solution)/shard_map/ppermute | solution.py:147
  79.8 3.9 %collective-permute-start.4 = (bf16[256,256]{1,0:T(8,128)(2,1)S(1)}, bf16[256,256]{1,0:T(8,128)(2,1)S(1)}, u32[]{:S(2)}, u32[]{:S(2)}) collective-permute-start(bf16[256,256]{1,0:T(8,128)(2,1)S(1)} %fusion.6.kv0), channel_id=1, source_target_pairs={{0,8},{1,9},{2,10},{3,11},{4,12},{5,13},{6,14},{7,15},{16,24},{17,... | collective-permute-start | bytes 393224 | tf_op jit(solution)/shard_map/ppermute | solution.py:149
  81.1 3.2 %collective-permute-start.3 = (bf16[256,256]{1,0:T(8,128)(2,1)S(1)}, bf16[256,256]{1,0:T(8,128)(2,1)S(1)}, u32[]{:S(2)}, u32[]{:S(2)}) collective-permute-start(bf16[256,256]{1,0:T(8,128)(2,1)S(1)} %collective-permute-done.1.kv2), channel_id=1, source_target_pairs={{8,0},{9,1},{10,2},{11,3},{12,4},{13,5},{14,6},{15,7},{24,16},{25,... | collective-permute-start | bytes 393224 | tf_op jit(solution)/shard_map/ppermute | solution.py:151
  82.8 1.8 collective-permute-start.2
  103.1 1.6 collective-permute-start.6
  103.6 1.5 collective-permute-start.5
  105.2 9.2 %collective-permute-start.8 = (bf16[256,256]{1,0:T(8,128)(2,1)S(1)}, bf16[256,256]{1,0:T(8,128)(2,1)S(1)}, u32[]{:S(2)}, u32[]{:S(2)}) collective-permute-start(bf16[256,256]{1,0:T(8,128)(2,1)S(1)} %get-tuple-element.24), channel_id=1, source_target_pairs={{32,0},{48,16},{33,1},{49,17},{34,2},{50,18},{35,3},{51,19},{36,4}... | collective-permute-start | bytes 393224 | tf_op jit(solution)/shard_map/ppermute | solution.py:170
  106.5 7.9 %collective-permute-start.7 = (bf16[256,256]{1,0:T(8,128)(2,1)S(1)}, bf16[256,256]{1,0:T(8,128)(2,1)S(1)}, u32[]{:S(2)}, u32[]{:S(2)}) collective-permute-start(bf16[256,256]{1,0:T(8,128)(2,1)S(1)} %get-tuple-element.23), channel_id=1, source_target_pairs={{16,0},{32,16},{48,32},{17,1},{33,17},{49,33},{18,2},{34,18},{50,3... | collective-permute-start | bytes 393224 | tf_op jit(solution)/shard_map/ppermute | solution.py:169
  133.3 4.6 %collective-permute-start.10 = (bf16[256,16,256]{2,1,0:T(8,128)(2,1)}, bf16[256,16,256]{2,1,0:T(8,128)(2,1)S(1)}, u32[]{:S(2)}, u32[]{:S(2)}) collective-permute-start(bf16[256,16,256]{2,1,0:T(8,128)(2,1)} %bitcast.45), channel_id=1, source_target_pairs={{0,8},{8,0},{1,9},{9,1},{2,10},{10,2},{3,11},{11,3},{4,12},{12,4},... | collective-permute-start | bytes 6291464 | tf_op jit(solution)/shard_map/ppermute | solution.py:159
  133.3 5.5 %collective-permute-start.9 = (bf16[256,256]{1,0:T(8,128)(2,1)S(1)}, bf16[256,256]{1,0:T(8,128)(2,1)S(1)}, u32[]{:S(2)}, u32[]{:S(2)}) collective-permute-start(bf16[256,256]{1,0:T(8,128)(2,1)S(1)} %add_convert_fusion), channel_id=1, source_target_pairs={{0,8},{8,0},{1,9},{9,1},{2,10},{10,2},{3,11},{11,3},{4,12},{12,4},... | collective-permute-start | bytes 393224 | tf_op jit(solution)/shard_map/ppermute | solution.py:178
  138.8 1.6 copy-start.2
Sparse Core Ops, SparseCore 0:
  9.8 57.7 all-gather.3
  120.0 56.1 reduce-scatter.1

commit v2 on v1

v2 whole, which is shorter than its diff:
```python
import functools
import math

import jax
import jax.numpy as jnp
from jax import lax
from jax.experimental import pallas as pl
from jax.experimental.pallas import tpu as pltpu
from jax.sharding import Mesh, PartitionSpec as P

HD = 128
SLOTS = 5
PAIR = 2
EARLY = [(s, h) for s in (0, 1, 7, 2, 6) for h in (0, 1)] + [(3, 0), (5, 1)]
LATE = [(3, 1), (5, 0), (4, 0), (4, 1)]
NEG = -1e30
MIB = 1024 * 1024
VMEM = 56 * MIB
F32 = jnp.float32
BF16 = jnp.bfloat16


def attention_kernel(place_ref, kv0, kv1, kv2, kv3, near, far, q_ref, do_ref,
                     att_ref, dq_ref, p0, p1, p2, p34,
                     k_all, v_all, kt_all, vt_all, s_ref, pb_ref, ds_ref, dkv_ref, thr_ref):
    rows = q_ref.shape[0]
    scale = 1.0 / math.sqrt(HD)
    log2e = math.log2(math.e)
    step = pl.program_id(0)
    heads = range(PAIR)
    spans = [pl.ds(j * rows, rows) for j in range(SLOTS)]

    @pl.when(step == 0)
    def _():
        blocks = (kv0[...], kv1[...], kv2[...], kv3[...], near[...] + far[...])
        documents = [kv[rows:, :].astype(F32) for kv in blocks]
        start = jnp.full((1, rows), (1 - SLOTS) * rows, jnp.int32)
        for doc in documents:
            earlier = doc.T[:, :1] < documents[0][:1, :]
            start = start + jnp.sum(earlier.astype(jnp.int32), axis=0, keepdims=True)
        core = place_ref[2]
        for j, back in enumerate((0, 2, 4, 1 + 2 * core, 3 - 2 * core)):
            thr_ref[j:j + 1, :] = start + back * rows
        for here, kv in zip(spans, blocks):
            k = kv[:rows, :HD]
            v = kv[:rows, HD:]
            k_all[here, :] = k
            v_all[here, :] = v
            kt_all[:, here] = k.T
            vt_all[:, here] = v.T
        dkv_ref[...] = jnp.zeros_like(dkv_ref)

    q = [q_ref[:, h * HD:(h + 1) * HD] for h in heads]
    do = [do_ref[:, h * HD:(h + 1) * HD] for h in heads]
    q_t = [a.T for a in q]
    do_t = [a.T for a in do]
    top = [jnp.full((1, rows), NEG, F32) for _ in heads]
    place = lax.broadcasted_iota(jnp.int32, (rows, rows), 0)
    for j, here in enumerate(spans):
        mask = place >= thr_ref[j:j + 1, :]
        if j == 0:
            mask = mask & (place <= lax.broadcasted_iota(jnp.int32, (rows, rows), 1))
        for h in heads:
            s = jnp.dot(k_all[here, :], q_t[h], preferred_element_type=F32)
            s = jnp.where(mask, s, NEG)
            s_ref[h, here, :] = s
            top[h] = jnp.maximum(top[h], jnp.max(s, axis=0, keepdims=True))
    total = [jnp.zeros((1, rows), F32) for _ in heads]
    for here in spans:
        for h in heads:
            e = jnp.exp2((s_ref[h, here, :] - top[h]) * (scale * log2e))
            s_ref[h, here, :] = e
            total[h] = total[h] + jnp.sum(e, axis=0, keepdims=True)
    inv = [1.0 / t for t in total]
    for here in spans:
        for h in heads:
            pb_ref[h, here, :] = (s_ref[h, here, :] * inv[h]).astype(BF16)
    delta = []
    for h in heads:
        out_b = jnp.dot(vt_all[...], pb_ref[h], preferred_element_type=F32).astype(BF16)
        att_ref[:, h * HD:(h + 1) * HD] = out_b.T
        delta.append(jnp.sum(do_t[h].astype(F32) * out_b.astype(F32), axis=0, keepdims=True))
    for here in spans:
        dk = jnp.zeros((rows, HD), F32)
        dv = jnp.zeros((rows, HD), F32)
        for h in heads:
            dp = jnp.dot(v_all[here, :], do_t[h], preferred_element_type=F32)
            ds = (s_ref[h, here, :] * inv[h] * (dp - delta[h])).astype(BF16)
            ds_ref[h, here, :] = ds
            dk = dk + jnp.dot(ds, q[h], preferred_element_type=F32)
            dv = dv + jnp.dot(pb_ref[h, here, :], do[h], preferred_element_type=F32)
        dkv_ref[here, :HD] += dk
        dkv_ref[here, HD:] += dv
    for h in heads:
        dq_t = jnp.dot(kt_all[...], ds_ref[h], preferred_element_type=F32)
        dq_ref[:, h * HD:(h + 1) * HD] = (dq_t * scale).astype(BF16).T

    @pl.when(step == pl.num_programs(0) - 1)
    def _():
        for here, out in zip(spans, (p0, p1, p2, p34.at[0], p34.at[1])):
            out[:, :HD] = dkv_ref[here, :HD] * scale
            out[:, HD:] = dkv_ref[here, HD:]


def attention(place, slots, q, do):
    rows, width = q.shape
    heads = width // HD
    keys = SLOTS * rows
    whole = lambda h, place: (0, 0)
    square = pl.BlockSpec((rows, 2 * HD), whole)
    pair = pl.BlockSpec((rows, PAIR * HD), lambda h, place: (0, h))
    part = jax.ShapeDtypeStruct((rows, 2 * HD), F32)
    return pl.pallas_call(
        attention_kernel,
        grid_spec=pltpu.PrefetchScalarGridSpec(
            num_scalar_prefetch=1,
            grid=(heads // PAIR,),
            in_specs=[pl.BlockSpec(slots[0].shape, whole)] * len(slots) + [pair] * 2,
            out_specs=[
                pair, pair, square, square, square,
                pl.BlockSpec((2, rows, 2 * HD), lambda h, place: (0, 0, 0)),
            ],
            scratch_shapes=[
                pltpu.VMEM((keys, HD), BF16),
                pltpu.VMEM((keys, HD), BF16),
                pltpu.VMEM((HD, keys), BF16),
                pltpu.VMEM((HD, keys), BF16),
                pltpu.VMEM((PAIR, keys, rows), F32),
                pltpu.VMEM((PAIR, keys, rows), BF16),
                pltpu.VMEM((PAIR, keys, rows), BF16),
                pltpu.VMEM((keys, 2 * HD), F32),
                pltpu.VMEM((8, rows), jnp.int32),
            ],
        ),
        out_shape=[
            jax.ShapeDtypeStruct((rows, width), BF16),
            jax.ShapeDtypeStruct((rows, width), BF16),
            part, part, part,
            jax.ShapeDtypeStruct((2, rows, 2 * HD), F32),
        ],
        compiler_params=pltpu.CompilerParams(vmem_limit_bytes=20 * MIB),
        cost_estimate=pl.CostEstimate(
            flops=12 * keys * width * rows, bytes_accessed=6 * MIB,
            transcendentals=keys * rows * heads,
        ),
    )(place, *slots, q, do)


def token(place, s, h, ring, few):
    return pl.multiple_of((lax.rem(place[3] + ring - s, ring) * 2 + h) * few, few)


def project_kernel(order, ring, last, place_ref, *refs):
    pieces, refs = refs[:len(order)], refs[len(order):]
    if last:
        wk_hbm, wv_hbm, seg_ref, early_ref, refs = *refs[:4], refs[6:]
    else:
        wk_hbm, wv_hbm, refs = *refs[:2], refs[2:]
    kv_ref, mine_hbm, theirs_hbm, h_ref, w_ref, come, come_w, go = refs
    few = pieces[0].shape[0]
    rows, width = h_ref.shape
    block = 2 * HD
    steps = come_w.shape[0] // 2
    depth = width // steps

    copies = [
        pltpu.make_async_copy(piece, h_ref.at[pl.ds(i * few, few), :], come.at[i])
        for i, piece in enumerate(pieces)
    ]
    weights = []
    for c in range(steps):
        at = pl.ds(c * depth, depth)
        weights.append([
            pltpu.make_async_copy(
                w.at[at, :], w_ref.at[at, pl.ds(i * HD, HD)], come_w.at[2 * c + i]
            )
            for i, w in enumerate((wk_hbm, wv_hbm))
        ])
    for copy in weights[0] + copies + sum(weights[1:], []):
        copy.start()
    for copy in copies:
        copy.wait()
    out = []
    base = 0 if not last else len(EARLY) * few
    for i in range(width // block):
        core, to = ((1 - place_ref[2], theirs_hbm), (place_ref[2], mine_hbm))[i % 2]
        first = pl.multiple_of((2 * (i // 2) + core) * block, block)
        out.append(pltpu.make_async_copy(
            h_ref.at[:, pl.ds(first, block)],
            to.at[pl.ds(base, rows), pl.ds(i // 2 * block, block)],
            go.at[i],
        ))
        out[-1].start()
    kv = jnp.zeros((rows, 2 * HD), F32)
    for c in range(steps):
        for copy in weights[c]:
            copy.wait()
        at = slice(c * depth, (c + 1) * depth)
        kv = kv + jnp.dot(h_ref[:, at], w_ref[at, :], preferred_element_type=F32)
    kv = kv.astype(BF16)
    if not last:
        kv_ref[...] = kv
    else:
        for i, (s, h) in enumerate(order):
            kv_ref[pl.ds(token(place_ref, s, h, ring, few), few), :] = kv[i * few:(i + 1) * few]
        for i, (s, h) in enumerate(EARLY):
            to = pl.ds(token(place_ref, s, h, ring, few), few)
            kv_ref[to, :] = early_ref[i * few:(i + 1) * few, :]
        total = seg_ref.shape[1]
        own = (seg_ref[...] + 1).astype(F32)
        kv_ref[total:, :] = jnp.broadcast_to(own, (kv_ref.shape[0] - total, total)).astype(BF16)
    for copy in out:
        copy.wait()


def project(place, order, pieces, key_weight, value_weight, ring, rest=()):
    few, width = pieces[0].shape
    rows = few * len(pieces)
    total = few * 2 * ring
    steps = 4
    far = pl.BlockSpec(memory_space=pl.ANY)
    whole = lambda i, place: (0, 0)
    kv_rows = total + 16 if rest else rows
    n = len(pieces)
    return pl.pallas_call(
        functools.partial(project_kernel, order, ring, bool(rest)),
        grid_spec=pltpu.PrefetchScalarGridSpec(
            num_scalar_prefetch=1,
            grid=(1,),
            in_specs=[far] * (n + 2)
            + ([pl.BlockSpec(a.shape, whole) for a in rest[:2]] + [far, far] if rest else []),
            out_specs=[pl.BlockSpec((kv_rows, 2 * HD), whole), far, far],
            scratch_shapes=[
                pltpu.VMEM((rows, width), BF16),
                pltpu.VMEM((width, 2 * HD), BF16),
                pltpu.SemaphoreType.DMA((n,)),
                pltpu.SemaphoreType.DMA((2 * steps,)),
                pltpu.SemaphoreType.DMA((width // (2 * HD),)),
            ],
        ),
        out_shape=[
            jax.ShapeDtypeStruct((kv_rows, 2 * HD), BF16),
            jax.ShapeDtypeStruct((total, width // 2), BF16),
            jax.ShapeDtypeStruct((total, width // 2), BF16),
        ],
        input_output_aliases={n + 5: 1, n + 6: 2} if rest else {},
        compiler_params=pltpu.CompilerParams(vmem_limit_bytes=VMEM),
        cost_estimate=pl.CostEstimate(
            flops=4 * rows * width * HD, bytes_accessed=8 * MIB, transcendentals=0
        ),
    )(place, *pieces, key_weight, value_weight, *rest)


def weight_grad_kernel(ring, place_ref, g_ref, gs_ref, *refs):
    hidden, (out_ref, grads_t, turn) = refs[:8], refs[8:]
    nx = out_ref.shape[1]
    few = g_ref.shape[0] // (2 * ring)

    @pl.when(pl.program_id(0) == 0)
    def _():
        for p, g in enumerate((g_ref, gs_ref)):
            for i, (s, h) in enumerate(EARLY + LATE):
                turn[i * few:(i + 1) * few, :] = g[pl.ds(token(place_ref, s, h, ring, few), few), :]
            grads_t[p] = turn[...].T

    for i, (mine, other) in enumerate(zip(hidden[:nx], hidden[nx:])):
        out_ref[0, lax.rem(i + nx - place_ref[0], nx)] = (
            jnp.dot(grads_t[0], mine[...], preferred_element_type=F32)
            + jnp.dot(grads_t[1], other[...], preferred_element_type=F32)
        ).astype(BF16)


def weight_grad(place, grads, other_grads, mine, other, nx, ny, ring):
    rows, cols = grads.shape
    block = mine.shape[1] // (nx * ny)
    flat = pl.BlockSpec((rows, cols), lambda r, place: (0, 0))

    def column(i):
        return pl.BlockSpec((rows, block), lambda r, place: (0, i * ny + r))

    return pl.pallas_call(
        functools.partial(weight_grad_kernel, ring),
        grid_spec=pltpu.PrefetchScalarGridSpec(
            num_scalar_prefetch=1,
            grid=(ny,),
            in_specs=[flat, flat] + [column(i) for i in range(nx)] * 2,
            out_specs=pl.BlockSpec((1, nx, cols, block), lambda r, place: (r, 0, 0, 0)),
            scratch_shapes=[pltpu.VMEM((2, cols, rows), BF16), pltpu.VMEM((rows, cols), BF16)],
        ),
        out_shape=jax.ShapeDtypeStruct((ny, nx, cols, block), BF16),
        compiler_params=pltpu.CompilerParams(vmem_limit_bytes=10 * MIB),
        cost_estimate=pl.CostEstimate(
            flops=4 * rows * cols * block * nx * ny, bytes_accessed=6 * MIB, transcendentals=0
        ),
    )(place, grads, other_grads, *[mine] * nx, *[other] * nx)


def add_kernel(parts, *outs):
    for i, out in enumerate(outs):
        total = parts[0, i].astype(F32)
        for r in range(1, parts.shape[0]):
            total = total + parts[r, i].astype(F32)
        out[...] = total.astype(BF16)


def add(parts):
    ny, nx, cols, block = parts.shape
    return pl.pallas_call(
        add_kernel,
        grid=(1,),
        in_specs=[pl.BlockSpec(parts.shape, lambda i: (0, 0, 0, 0))],
        out_specs=[pl.BlockSpec((cols, block), lambda i: (0, 0))] * nx,
        out_shape=[jax.ShapeDtypeStruct((cols, block), BF16)] * nx,
        compiler_params=pltpu.CompilerParams(vmem_limit_bytes=10 * MIB),
    )(parts)


def finish_kernel(a, b, c, d, key_ref, value_ref):
    total = (a[...].astype(F32) + b[...].astype(F32)) + (c[...].astype(F32) + d[...].astype(F32))
    key_ref[...] = total[:HD].T
    value_ref[...] = total[HD:].T


def finish(parts):
    cols, block = parts[0].shape
    half = pl.BlockSpec((block, HD), lambda i: (0, 0))
    shape = jax.ShapeDtypeStruct((block, HD), F32)
    return pl.pallas_call(
        finish_kernel,
        grid=(1,),
        in_specs=[pl.BlockSpec((cols, block), lambda i: (0, 0))] * 4,
        out_specs=[half, half],
        out_shape=[shape, shape],
        compiler_params=pltpu.CompilerParams(vmem_limit_bytes=8 * MIB),
    )(*parts)


def spread_kernel(b0, b1, b2, b3, wa_ref, wb_ref, o0, o1, o2, o3, left):
    few = o0.shape[1]
    heads = left.shape[0]

    @pl.when(pl.program_id(0) == 0)
    def _():
        for s, b in enumerate((b0, b1, b2, b3)):
            left[:, s * few:(s + 1) * few, :] = b[...]

    contract = (((1,), (1,)), ((), ()))
    for p, w in enumerate((wa_ref, wb_ref)):
        acc = lax.dot_general(w[0], left[0], contract, preferred_element_type=F32)
        for h in range(1, heads):
            acc = acc + lax.dot_general(w[h], left[h], contract, preferred_element_type=F32)
        turned = acc.T.astype(BF16)
        for s, out in enumerate((o0, o1, o2, o3)):
            out[p] = turned[s * few:(s + 1) * few]


def spread(blocks, wa, wb):
    heads, few, cols = blocks[0].shape
    depth = wa.shape[1]
    tile = depth // 4
    weight = pl.BlockSpec((heads, tile, cols), lambda i: (0, i, 0))
    return pl.pallas_call(
        spread_kernel,
        grid=(depth // tile,),
        in_specs=[pl.BlockSpec((heads, few, cols), lambda i: (0, 0, 0))] * 4 + [weight, weight],
        out_specs=[pl.BlockSpec((2, few, tile), lambda i: (0, 0, i))] * 4,
        out_shape=[jax.ShapeDtypeStruct((2, few, depth), BF16)] * 4,
        scratch_shapes=[pltpu.VMEM((heads, 4 * few, cols), BF16)],
        compiler_params=pltpu.CompilerParams(vmem_limit_bytes=VMEM),
        cost_estimate=pl.CostEstimate(
            flops=16 * few * heads * cols * depth, bytes_accessed=9 * MIB, transcendentals=0
        ),
    )(*blocks, wa, wb)


def assemble_kernel(place_ref, a, b, c, d, out_ref):
    depth = a.shape[2]
    for s, piece in enumerate((a, b, c, d)):
        part = lax.rem(place_ref[0] + s, 4) * 2
        for p in range(2):
            core = place_ref[2] if p == 0 else 1 - place_ref[2]
            out_ref[:, pl.ds(pl.multiple_of((part + core) * depth, depth), depth)] = piece[p]


def assemble(place, pieces):
    two, few, depth = pieces[0].shape
    return pl.pallas_call(
        assemble_kernel,
        grid_spec=pltpu.PrefetchScalarGridSpec(
            num_scalar_prefetch=1,
            grid=(1,),
            in_specs=[pl.BlockSpec((two, few, depth), lambda i, place: (0, 0, 0))] * 4,
            out_specs=pl.BlockSpec((few, 4 * two * depth), lambda i, place: (0, 0)),
        ),
        out_shape=jax.ShapeDtypeStruct((few, 4 * two * depth), BF16),
        compiler_params=pltpu.CompilerParams(vmem_limit_bytes=6 * MIB),
    )(place, *pieces)


def on_device(hidden, key_weight, value_weight, queries, out_grad, segment_ids):
    rows = queries.shape[1]
    x_count, width = hidden.shape[1:]
    nx = lax.axis_size("dp")
    ny = lax.axis_size("y")
    heads = lax.axis_size("tp")
    x = lax.axis_index("dp")
    core = lax.axis_index("core")
    place = jnp.stack([x, lax.axis_index("y"), core, lax.axis_index("tp")]).astype(jnp.int32)
    swap = [(0, 1), (1, 0)]

    def swapped(a):
        return lax.ppermute(a, "core", swap)

    def shifted(a, s, axis="dp"):
        n = lax.axis_size(axis)
        return lax.ppermute(a, axis, [(i, (i + s) % n) for i in range(n)])

    half = x_count // 2
    ring = {(0, h): hidden[0, h * half:(h + 1) * half] for h in range(2)}
    for s in range(1, heads // 2 + 1):
        for h in range(2):
            if s < heads // 2 or h == 0:
                ring[s, h] = shifted(ring[s - 1, h], 1, "tp")
            if s < heads // 2 or h == 1:
                ring[heads - s, h] = shifted(ring[(heads - s + 1) % heads, h], -1, "tp")
    weights = (key_weight, value_weight)
    early = project(place, EARLY, [ring[i] for i in EARLY], *weights, heads)
    kv, mine, theirs = project(
        place, LATE, [ring[i] for i in LATE], *weights, heads, (segment_ids, *early)
    )

    depth = width // (2 * nx)
    first = (x * 2 + core) * depth
    part_w = jnp.concatenate(
        [lax.dynamic_slice_in_dim(w, first, depth, axis=0) for w in (key_weight, value_weight)], axis=1
    )
    part_w, kv = lax.optimization_barrier((part_w, kv))
    all_w = lax.all_gather(part_w, "tp", axis=0)

    down1 = [(i, i + 1) for i in range(ny - 1)]
    down2 = [(i, i + 2) for i in range(ny - 2)]
    kv1 = lax.ppermute(kv, "y", down1)
    kv2 = lax.ppermute(kv, "y", down2)
    near = lax.ppermute(kv, "core", [(0, 1)])
    kv3 = swapped(kv1)
    far = lax.ppermute(kv2, "core", [(1, 0)])

    att, dq, part0, part1, part2, part34 = attention(
        place, (kv, kv1, kv2, kv3, near, far), queries[0], out_grad[0]
    )

    up1 = [(i + 1, i) for i in range(ny - 1)]
    up2 = [(i + 2, i) for i in range(ny - 2)]
    got = swapped(part34)
    send1 = (part1 + got[0]).astype(BF16)
    send2 = (part2 + jnp.where(core == 0, 0.0, got[1])).astype(BF16)
    own = part0 + jnp.where(core == 0, got[1], 0.0)
    got1 = lax.ppermute(send1, "y", up1)
    got2 = lax.ppermute(send2, "y", up2)
    grads = (own + got1.astype(F32) + got2.astype(F32)).astype(BF16)

    other = swapped(theirs)
    other_grads = swapped(grads)
    by_head = lax.all_to_all(grads.reshape(heads, x_count, 2 * HD), "tp", 0, 0, tiled=True)
    sums = weight_grad(place, grads, other_grads, mine, other, nx, ny, heads)
    by_head, sums, all_w = lax.optimization_barrier((by_head, sums, all_w))
    other_w = swapped(all_w)
    sums = lax.all_to_all(sums, "y", 0, 0, tiled=True)

    group_heads = [by_head] + [shifted(by_head, s) for s in range(1, nx)]
    pieces = spread(group_heads, all_w, other_w)
    _, sums = lax.optimization_barrier((pieces, sums))
    sums = add(sums)
    key_wgrad, value_wgrad = finish(
        [sums[0]] + [shifted(sums[s], s) for s in range(1, nx)]
    )
    hidden_grad = assemble(place, [pieces[0]] + [shifted(pieces[s], nx - s) for s in range(1, nx)])
    return (
        att[None],
        dq[None],
        hidden_grad[None],
        key_wgrad,
        value_wgrad,
    )


def solution(mesh):
    fine = Mesh(
        mesh.devices.reshape(mesh.shape["dp"], mesh.shape["ctx"] // 2, 2, mesh.shape["tp"]),
        ("dp", "y", "core", "tp"),
    )
    ctx = ("y", "core")
    in_specs = (
        P("dp", ("y", "core", "tp"), None),
        P(None, "tp"),
        P(None, "tp"),
        P("dp", ctx, "tp"),
        P("dp", ctx, "tp"),
        P("dp", ctx),
    )
    out_specs = (
        P("dp", ctx, "tp"),
        P("dp", ctx, "tp"),
        P("dp", ("y", "core", "tp"), None),
        P(("dp", "y", "core"), "tp"),
        P(("dp", "y", "core"), "tp"),
    )
    return jax.shard_map(
        on_device, mesh=fine, in_specs=in_specs, out_specs=out_specs, check_vma=False
    )
```

time: 187 us -> 173 us (0.925)
  starting transfers between devices: 14.6 us -> 64 us
  blocking collectives: 46.7 us -> 0 us
  Pallas kernels: 18.5 us -> 41 us
  waiting for transfers between devices: 56.6 us -> 42.5 us
  local copies, waits for them, and re-layouts: 18.1 us -> 5.92 us
  matrix products: 11.6 us -> 0 us
    all_gather x1, waiting for transfers between devices: 42.6 us -> 0.01 us  [on_device(): all_w = lax.all_gather(part_w, 'tp', axis=0)]
    ppermute x5 -> x28, starting transfers between devices: 1.94 us -> 41 us  [the longest x23 40.6 us: shifted(): return lax.ppermute(a, axis, [(i, (i + s) % n) for i in range(n)])]
    all_to_all x1 -> x0, blocking collectives: 35.7 us -> none  [on_device(): blocks = lax.all_to_all(blocks, ('dp', 'y'), 0, 0, tiled=True)]
    pallas_call x1 -> x8, Pallas kernels: 18.5 us -> 41 us  [the longest x1 13.7 us: attention(): pl.pallas_call(attention_kernel, grid_spec=pltpu.PrefetchScalarGridSpec(n...]
    ppermute x5 -> x28, waiting for transfers between devices: 5.72 us -> 23.5 us  [the longest x23 21 us: shifted(): return lax.ppermute(a, axis, [(i, (i + s) % n) for i in range(n)])]
    dot_general x4 -> x0, matrix products: 11.6 us -> none  [the longest x1 5.44 us: on_device(): lax.dot_general(grads, weights, (((1,), (1,)), ((), ())), preferred_eleme...]
    all_gather x1 -> x0, blocking collectives: 11 us -> none  [on_device(): all_seg = lax.all_gather(segment_ids[0], ('y', 'core'), axis=0, tiled=True)]
    all_to_all x0 -> x2, starting transfers between devices: none -> 9.57 us  [the longest x1 5.8 us: on_device(): lax.all_to_all(grads.reshape(heads, x_count, 2 * HD), 'tp', 0, 0, tiled=T...]
  transfers between devices with their start and end apart: 13 -> 37, of which waited for: 8 -> 19; matrix products, arithmetic and copies ran while one was open for 13% -> 3% of each run, Pallas kernels for 0% -> 19%
where the time goes in v2:
time: 173 us; the launch traced here: 172 us
  starting transfers between devices  64 us (37%)
  waiting for transfers between devices  42.5 us (25%)
  Pallas kernels  41 us (24%)
  between operations  14.4 us (8%)
  local copies, waits for them, and re-layouts  5.92 us (3%)
  other arithmetic  4.27 us (2%)
    ppermute x23, starting transfers between devices, shifted(): return lax.ppermute(a, axis, [(i, (i + s) % n) for i in range(n)])  40.6 us
    ppermute x23, waiting for transfers between devices, shifted(): return lax.ppermute(a, axis, [(i, (i + s) % n) for i in range(n)])  21 us
    pallas_call x1, Pallas kernels, attention(): pl.pallas_call(attention_kernel, grid_spec=pltpu.PrefetchScalarGridSpec(n...  13.7 us
    pallas_call x2, Pallas kernels, project(): pl.pallas_call(functools.partial(project_kernel, order, ring, bool(rest))...  13.7 us
    pallas_call x1, Pallas kernels, spread(): pl.pallas_call(spread_kernel, grid=(depth // tile,), in_specs=[pl.BlockSp...  6.45 us
    all_to_all x1, starting transfers between devices, on_device(): lax.all_to_all(grads.reshape(heads, x_count, 2 * HD), 'tp', 0, 0, tiled=T...  5.8 us
    ppermute x1, waiting for transfers between devices, on_device(): got1 = lax.ppermute(send1, 'y', up1)  5.49 us
    ppermute x1, starting transfers between devices, on_device(): kv2 = lax.ppermute(kv, 'y', down2)  5.1 us
  transfers between devices with their start and end apart: 37, of which 19 were waited for; matrix products, arithmetic and copies ran while one was open for 3% of the time, Pallas kernels for 19%

profile of v2, /device:TPU:2, one launch (start us, length us, event | category | flops | bytes accessed | tf_op | source)
XLA Modules:
  0.0 172.0 jit_solution(16334645785423195247)
XLA Ops:
  7.2 1.1 slice_bitcast_fusion.1
  8.3 2.0 %collective-permute-start.6 = (bf16[16,8192]{1,0:T(8,128)(2,1)S(1)}, bf16[16,8192]{1,0:T(8,128)(2,1)S(1)}, u32[]{:S(2)}, u32[]{:S(2)}) collective-permute-start(bf16[16,8192]{1,0:T(8,128)(2,1)S(1)} %get-tuple-element.63.refs_0_), channel_id=1, source_target_pairs={{0,1},{1,2},{2,3},{3,4},{4,5},{5,6},{6,7},{7,0},{8,9},{9,10},{10,1... | collective-permute-start | bytes 786440 | tf_op jit(solution)/shard_map/ppermute | solution.py:416
  10.3 4.0 %collective-permute-start.10 = (bf16[16,8192]{1,0:T(8,128)(2,1)S(1)}, bf16[16,8192]{1,0:T(8,128)(2,1)S(1)}, u32[]{:S(2)}, u32[]{:S(2)}) collective-permute-start(bf16[16,8192]{1,0:T(8,128)(2,1)S(1)} %get-tuple-element.64.refs_1_), channel_id=1, source_target_pairs={{0,7},{1,0},{2,1},{3,2},{4,3},{5,4},{6,5},{7,6},{8,15},{9,8},{10,9... | collective-permute-start | bytes 786440 | tf_op jit(solution)/shard_map/ppermute | solution.py:416
  14.3 1.9 %collective-permute-start.3 = (bf16[16,8192]{1,0:T(8,128)(2,1)S(1)}, bf16[16,8192]{1,0:T(8,128)(2,1)S(1)}, u32[]{:S(2)}, u32[]{:S(2)}) collective-permute-start(bf16[16,8192]{1,0:T(8,128)(2,1)S(1)} %get-tuple-element.63.refs_0_), channel_id=1, source_target_pairs={{0,7},{1,0},{2,1},{3,2},{4,3},{5,4},{6,5},{7,6},{8,15},{9,8},{10,9... | collective-permute-start | bytes 786440 | tf_op jit(solution)/shard_map/ppermute | solution.py:416
  16.4 5.0 %collective-permute-done.6.refs_2_ = bf16[16,8192]{1,0:T(8,128)(2,1)S(1)} collective-permute-done((bf16[16,8192]{1,0:T(8,128)(2,1)S(1)}, bf16[16,8192]{1,0:T(8,128)(2,1)S(1)}, u32[]{:S(2)}, u32[]{:S(2)}) %collective-permute-start.6) | collective-permute-done | bytes 262176 | tf_op jit(solution)/shard_map/ppermute | solution.py:416
  21.4 3.3 %collective-permute-start.11 = (bf16[16,8192]{1,0:T(8,128)(2,1)S(1)}, bf16[16,8192]{1,0:T(8,128)(2,1)S(1)}, u32[]{:S(2)}, u32[]{:S(2)}) collective-permute-start(bf16[16,8192]{1,0:T(8,128)(2,1)S(1)} %collective-permute-done.10.refs_5_), channel_id=1, source_target_pairs={{0,7},{1,0},{2,1},{3,2},{4,3},{5,4},{6,5},{7,6},{8,15},{9,8},{10,9... | collective-permute-start | bytes 786440 | tf_op jit(solution)/shard_map/ppermute | solution.py:416
  24.7 1.9 %collective-permute-done.3.refs_4_ = bf16[16,8192]{1,0:T(8,128)(2,1)S(1)} collective-permute-done((bf16[16,8192]{1,0:T(8,128)(2,1)S(1)}, bf16[16,8192]{1,0:T(8,128)(2,1)S(1)}, u32[]{:S(2)}, u32[]{:S(2)}) %collective-permute-start.3) | collective-permute-done | bytes 262176 | tf_op jit(solution)/shard_map/ppermute | solution.py:416
  26.7 3.7 %collective-permute-start.4 = (bf16[16,8192]{1,0:T(8,128)(2,1)S(1)}, bf16[16,8192]{1,0:T(8,128)(2,1)S(1)}, u32[]{:S(2)}, u32[]{:S(2)}) collective-permute-start(bf16[16,8192]{1,0:T(8,128)(2,1)S(1)} %collective-permute-done.3.refs_4_), channel_id=1, source_target_pairs={{0,7},{1,0},{2,1},{3,2},{4,3},{5,4},{6,5},{7,6},{8,15},{9,8},{10,9... | collective-permute-start | bytes 786440 | tf_op jit(solution)/shard_map/ppermute | solution.py:416
  30.4 1.4 collective-permute-done.7.refs_6_
  32.3 3.7 %collective-permute-start.12 = (bf16[16,8192]{1,0:T(8,128)(2,1)S(1)}, bf16[16,8192]{1,0:T(8,128)(2,1)}, u32[]{:S(2)}, u32[]{:S(2)}) collective-permute-start(bf16[16,8192]{1,0:T(8,128)(2,1)S(1)} %collective-permute-done.11.refs_9_), channel_id=1, source_target_pairs={{0,7},{1,0},{2,1},{3,2},{4,3},{5,4},{6,5},{7,6},{8,15},{9,8},{10,9... | collective-permute-start | bytes 786440 | tf_op jit(solution)/shard_map/ppermute | solution.py:416
  36.0 1.1 constant_dynamic-slice_fusion
  37.9 3.7 %collective-permute-start.5 = (bf16[16,8192]{1,0:T(8,128)(2,1)S(1)}, bf16[16,8192]{1,0:T(8,128)(2,1)S(1)}, u32[]{:S(2)}, u32[]{:S(2)}) collective-permute-start(bf16[16,8192]{1,0:T(8,128)(2,1)S(1)} %collective-permute-done.4.refs_8_), channel_id=1, source_target_pairs={{0,7},{1,0},{2,1},{3,2},{4,3},{5,4},{6,5},{7,6},{8,15},{9,8},{10,9... | collective-permute-start | bytes 786440 | tf_op jit(solution)/shard_map/ppermute | solution.py:416
  41.6 1.9 %collective-permute-done.8.refs_10_ = bf16[16,8192]{1,0:T(8,128)(2,1)} collective-permute-done((bf16[16,8192]{1,0:T(8,128)(2,1)S(1)}, bf16[16,8192]{1,0:T(8,128)(2,1)}, u32[]{:S(2)}, u32[]{:S(2)}) %collective-permute-start.8) | collective-permute-done | bytes 262176 | tf_op jit(solution)/shard_map/ppermute | solution.py:416
  43.5 3.8 %collective-permute-start.13 = (bf16[16,8192]{1,0:T(8,128)(2,1)}, bf16[16,8192]{1,0:T(8,128)(2,1)S(1)}, u32[]{:S(2)}, u32[]{:S(2)}) collective-permute-start(bf16[16,8192]{1,0:T(8,128)(2,1)} %collective-permute-done.12.refs_11_), channel_id=1, source_target_pairs={{0,7},{1,0},{2,1},{3,2},{4,3},{5,4},{6,5},{7,6},{8,15},{9,8},{10,9... | collective-permute-start | bytes 786440 | tf_op jit(solution)/shard_map/ppermute | solution.py:416
  48.8 6.9 %shard_map.101 = (bf16[192,256]{1,0:T(8,128)(2,1)}, bf16[256,4096]{1,0:T(8,128)(2,1)}, bf16[256,4096]{1,0:T(8,128)(2,1)}) custom-call(s32[4]{0:T(128)} %pad_add_fusion.place_ref, bf16[16,8192]{1,0:T(8,128)(2,1)} %copy-done.7, bf16[16,8192]{1,0:T(8,128)(2,1)} %copy-done.8, bf16[16,8192]{1,0:T(8,128)(2,1)} %copy-done.14, bf16[16,8192]{1,0:T(8,128)(2,1)} %copy-done.17, ...), custom_call_target="tpu_custom_call" | custom-call | flops 805306368 | bytes 8388608 | tf_op jit(solution)/shard_map/pallas_call | solution.py:225
  56.7 6.8 %shard_map.102 = (bf16[272,256]{1,0:T(8,128)(2,1)}, bf16[256,4096]{1,0:T(8,128)(2,1)}, bf16[256,4096]{1,0:T(8,128)(2,1)}) custom-call(s32[4]{0:T(128)} %pad_add_fusion.place_ref, bf16[16,8192]{1,0:T(8,128)(2,1)} %copy-done.11, bf16[16,8192]{1,0:T(8,128)(2,1)} %copy-done.10, ...), custom_call_target="tpu_custom_call", output_to_operand_aliasing={{1}: (9, {}), {2}: (10, {})} | custom-call | flops 268435456 | bytes 8388608 | tf_op jit(solution)/shard_map/pallas_call | solution.py:225
  63.6 5.1 %collective-permute-start.15 = (bf16[272,256]{1,0:T(8,128)(2,1)}, bf16[272,256]{1,0:T(8,128)(2,1)S(1)}, u32[]{:S(2)}, u32[]{:S(2)}) collective-permute-start(bf16[272,256]{1,0:T(8,128)(2,1)} %get-tuple-element.37.kv0), channel_id=1, source_target_pairs={{0,32},{16,48},{1,33},{17,49},{2,34},{18,50},{3,35},{19,51},{4,36}... | collective-permute-start | bytes 417800 | tf_op jit(solution)/shard_map/ppermute | solution.py:443
  68.7 2.6 %collective-permute-start.14 = (bf16[272,256]{1,0:T(8,128)(2,1)}, bf16[272,256]{1,0:T(8,128)(2,1)S(1)}, u32[]{:S(2)}, u32[]{:S(2)}) collective-permute-start(bf16[272,256]{1,0:T(8,128)(2,1)} %get-tuple-element.37.kv0), channel_id=1, source_target_pairs={{0,16},{16,32},{32,48},{1,17},{17,33},{33,49},{2,18},{18,34},{34,5... | collective-permute-start | bytes 417800 | tf_op jit(solution)/shard_map/ppermute | solution.py:442
  71.3 1.8 %collective-permute-start.17 = (bf16[272,256]{1,0:T(8,128)(2,1)}, bf16[272,256]{1,0:T(8,128)(2,1)S(1)}, u32[]{:S(2)}, u32[]{:S(2)}) collective-permute-start(bf16[272,256]{1,0:T(8,128)(2,1)} %get-tuple-element.37.kv0), channel_id=1, source_target_pairs={{0,8},{1,9},{2,10},{3,11},{4,12},{5,13},{6,14},{7,15},{16,24},{17,... | collective-permute-start | bytes 417800 | tf_op jit(solution)/shard_map/ppermute | solution.py:444
  73.1 1.3 collective-permute-start.18
  74.4 1.1 collective-permute-done.14.kv1
  76.9 0.9 copy-done.6
  77.8 13.7 %shard_map.103 = (bf16[256,1024]{1,0:T(8,128)(2,1)}, bf16[256,1024]{1,0:T(8,128)(2,1)}, f32[256,256]{1,0:T(8,128)S(1)}, f32[256,256]{1,0:T(8,128)S(1)}, f32[256,...) custom-call(s32[4]{0:T(128)S(1)} %copy-done.3, bf16[272,256]{1,0:T(8,128)(2,1)S(1)} %copy-done.6, ...), custom_call_target="tpu_custom_call" | custom-call | flops 4026531840 | bytes 6291456 | tf_op jit(solution)/shard_map/pallas_call | solution.py:113
  91.7 1.9 %collective-permute-done.19 = f32[2,256,256]{2,1,0:T(8,128)} collective-permute-done((f32[2,256,256]{2,1,0:T(8,128)S(1)}, f32[2,256,256]{2,1,0:T(8,128)}, u32[]{:S(2)}, u32[]{:S(2)}) %collective-permute-start.19) | collective-permute-done | bytes 524320 | tf_op jit(solution)/shard_map/ppermute | solution.py:412
  93.6 1.1 fusion.1
  94.7 1.3 collective-permute-start.20
  96.0 1.3 collective-permute-start.21
  97.3 5.5 %collective-permute-done.20 = bf16[256,256]{1,0:T(8,128)(2,1)S(1)} collective-permute-done((bf16[256,256]{1,0:T(8,128)(2,1)S(1)}, bf16[256,256]{1,0:T(8,128)(2,1)S(1)}, u32[]{:S(2)}, u32[]{:S(2)}) %collective-permute-start.20) | collective-permute-done | bytes 131104 | tf_op jit(solution)/shard_map/ppermute | solution.py:458
  102.8 3.1 %collective-permute-done.21 = bf16[256,256]{1,0:T(8,128)(2,1)S(1)} collective-permute-done((bf16[256,256]{1,0:T(8,128)(2,1)S(1)}, bf16[256,256]{1,0:T(8,128)(2,1)S(1)}, u32[]{:S(2)}, u32[]{:S(2)}) %collective-permute-start.21) | collective-permute-done | bytes 131104 | tf_op jit(solution)/shard_map/ppermute | solution.py:459
  105.9 1.7 fusion.5.g_ref
  107.6 5.8 %all-to-all-start = ((bf16[8,32,256]{2,1,0:T(8,128)(2,1)}), bf16[8,32,256]{2,1,0:T(8,128)(2,1)S(1)}, u32[]{:S(2)}, u32[]{:S(2)}) async-start(bf16[8,32,256]{2,1,0:T(8,128)(2,1)} %bitcast.13), calls=%async_computation | async-start | bytes 262144 | tf_op jit(solution)/shard_map/all_to_all | solution.py:464
  113.4 4.7 %shard_map.104 = bf16[4,4,256,256]{3,2,1,0:T(8,128)(2,1)S(1)} custom-call(s32[4]{0:T(128)S(1)} %copy-done.3, bf16[256,256]{1,0:T(8,128)(2,1)} %fusion.5.g_ref, bf16[256,256]{1,0:T(8,128)(2,1)S(1)} %collective-permute-done.22.gs_ref, bf16[256,4096]{1,0:T(8,128)(2,1)S(1)} %copy-done, bf16[256,4096]{1,0:T(8,128)(2,1)S(1)} %copy-done, ...), custom_call_target="tpu_custom_call" | custom-call | flops 1073741824 | bytes 6291456 | tf_op jit(solution)/shard_map/pallas_call | solution.py:281
  118.1 1.3 copy-done.1
  119.4 3.9 %all-to-all-done.b0 = bf16[8,32,256]{2,1,0:T(8,128)(2,1)S(1)} async-done(((bf16[8,32,256]{2,1,0:T(8,128)(2,1)}), bf16[8,32,256]{2,1,0:T(8,128)(2,1)S(1)}, u32[]{:S(2)}, u32[]{:S(2)}) %all-to-all-start) | async-done | bytes 131104 | tf_op jit(solution)/shard_map/all_to_all | solution.py:464
  123.3 3.8 %all-to-all-start.1 = ((bf16[4,4,256,256]{3,2,1,0:T(8,128)(2,1)}), bf16[4,4,256,256]{3,2,1,0:T(8,128)(2,1)S(1)}, u32[]{:S(2)}, u32[]{:S(2)}) async-start(bf16[4,4,256,256]{3,2,1,0:T(8,128)(2,1)} %copy-done.1), calls=%async_computation.1 | async-start | bytes 4194304 | tf_op jit(solution)/shard_map/all_to_all | solution.py:468
  127.6 2.4 %collective-permute-start.25 = (bf16[8,32,256]{2,1,0:T(8,128)(2,1)S(1)}, bf16[8,32,256]{2,1,0:T(8,128)(2,1)S(1)}, u32[]{:S(2)}, u32[]{:S(2)}) collective-permute-start(bf16[8,32,256]{2,1,0:T(8,128)(2,1)S(1)} %all-to-all-done.b0), channel_id=1, source_target_pairs={{0,128},{64,192},{128,0},{192,64},{1,129},{65,193},{129,1},{193,65... | collective-permute-start | bytes 393224 | tf_op jit(solution)/shard_map/ppermute | solution.py:416
  130.1 1.8 %collective-permute-start.24 = (bf16[8,32,256]{2,1,0:T(8,128)(2,1)S(1)}, bf16[8,32,256]{2,1,0:T(8,128)(2,1)S(1)}, u32[]{:S(2)}, u32[]{:S(2)}) collective-permute-start(bf16[8,32,256]{2,1,0:T(8,128)(2,1)S(1)} %all-to-all-done.b0), channel_id=1, source_target_pairs={{0,64},{64,128},{128,192},{192,0},{1,65},{65,129},{129,193},{193,1... | collective-permute-start | bytes 393224 | tf_op jit(solution)/shard_map/ppermute | solution.py:416
  131.8 1.1 collective-permute-done.26.b3
  133.0 3.7 %collective-permute-done.25.b2 = bf16[8,32,256]{2,1,0:T(8,128)(2,1)S(1)} collective-permute-done((bf16[8,32,256]{2,1,0:T(8,128)(2,1)S(1)}, bf16[8,32,256]{2,1,0:T(8,128)(2,1)S(1)}, u32[]{:S(2)}, u32[]{:S(2)}) %collective-permute-start.25) | collective-permute-done | bytes 131104 | tf_op jit(solution)/shard_map/ppermute | solution.py:416
  138.2 6.5 %shard_map.105 = (bf16[2,32,1024]{2,1,0:T(8,128)(2,1)}, bf16[2,32,1024]{2,1,0:T(8,128)(2,1)}, bf16[2,32,1024]{2,1,0:T(8,128)(2,1)}, bf16[2,32,1024]{2,1,0:T(8,128)(2,1)}) custom-call(bf16[8,32,256]{2,1,0:T(8,128)(2,1)} %copy-done.9, bf16[8,32,256]{2,1,0:T(8,128)(2,1)} %copy-done.23, bf16[8,32,256]{2,1,0:T(8,128)(2,1)} %copy-done.22, ...), custom_call_target="tpu_custom_call" | custom-call | flops 1073741824 | bytes 9437184 | tf_op jit(solution)/shard_map/pallas_call | solution.py:362
  144.7 2.8 %collective-permute-start.28 = (bf16[2,32,1024]{2,1,0:T(8,128)(2,1)}, bf16[2,32,1024]{2,1,0:T(8,128)(2,1)S(1)}, u32[]{:S(2)}, u32[]{:S(2)}) collective-permute-start(bf16[2,32,1024]{2,1,0:T(8,128)(2,1)} %get-tuple-element.50), channel_id=1, source_target_pairs={{0,192},{64,0},{128,64},{192,128},{1,193},{65,1},{129,65},{193,129... | collective-permute-start | bytes 393224 | tf_op jit(solution)/shard_map/ppermute | solution.py:416
  147.7 1.8 %collective-permute-start.30 = (bf16[2,32,1024]{2,1,0:T(8,128)(2,1)}, bf16[2,32,1024]{2,1,0:T(8,128)(2,1)S(1)}, u32[]{:S(2)}, u32[]{:S(2)}) collective-permute-start(bf16[2,32,1024]{2,1,0:T(8,128)(2,1)} %get-tuple-element.52), channel_id=1, source_target_pairs={{0,64},{64,128},{128,192},{192,0},{1,65},{65,129},{129,193},{193,1... | collective-permute-start | bytes 393224 | tf_op jit(solution)/shard_map/ppermute | solution.py:416
  149.5 4.7 %all-to-all-done.1.parts = bf16[4,4,256,256]{3,2,1,0:T(8,128)(2,1)S(1)} async-done(((bf16[4,4,256,256]{3,2,1,0:T(8,128)(2,1)}), bf16[4,4,256,256]{3,2,1,0:T(8,128)(2,1)S(1)}, u32[]{:S(2)}, u32[]{:S(2)}) %all-to-all-start.1) | async-done | bytes 2097184 | tf_op jit(solution)/shard_map/all_to_all | solution.py:468
  154.5 1.5 collective-permute-start.31
  156.0 1.2 collective-permute-start.32
  157.2 2.1 %collective-permute-start.33 = (bf16[256,256]{1,0:T(8,128)(2,1)S(1)}, bf16[256,256]{1,0:T(8,128)(2,1)S(1)}, u32[]{:S(2)}, u32[]{:S(2)}) collective-permute-start(bf16[256,256]{1,0:T(8,128)(2,1)S(1)} %get-tuple-element.58), channel_id=1, source_target_pairs={{0,192},{64,0},{128,64},{192,128},{1,193},{65,1},{129,65},{193,129... | collective-permute-start | bytes 393224 | tf_op jit(solution)/shard_map/ppermute | solution.py:416
  159.3 1.4 shard_map.106
  160.6 3.0 %collective-permute-done.32.c = bf16[256,256]{1,0:T(8,128)(2,1)S(1)} collective-permute-done((bf16[256,256]{1,0:T(8,128)(2,1)S(1)}, bf16[256,256]{1,0:T(8,128)(2,1)S(1)}, u32[]{:S(2)}, u32[]{:S(2)}) %collective-permute-start.32) | collective-permute-done | bytes 131104 | tf_op jit(solution)/shard_map/ppermute | solution.py:416
  (89 shorter events, 9.6 us)
Async XLA Ops:
  7.2 116.2 %all-gather.3.cloned.1.call-start = ((), (), s32[]{:S(2)}) async-start(), calls=%async_computation.2 | async-start | bytes 4718592 | tf_op jit(solution)/shard_map/all_gather | solution.py:438
  8.3 40.5 %copy-start.7 = (bf16[16,8192]{1,0:T(8,128)(2,1)}, bf16[16,8192]{1,0:T(8,128)(2,1)S(1)}, u32[]{:S(2)}) copy-start(bf16[16,8192]{1,0:T(8,128)(2,1)S(1)} %get-tuple-element.63.refs_0_) | copy-start | bytes 786436
  8.3 40.5 %copy-start.8 = (bf16[16,8192]{1,0:T(8,128)(2,1)}, bf16[16,8192]{1,0:T(8,128)(2,1)S(1)}, u32[]{:S(2)}) copy-start(bf16[16,8192]{1,0:T(8,128)(2,1)S(1)} %get-tuple-element.64.refs_1_) | copy-start | bytes 786436
  8.3 13.1 %collective-permute-start.6 = (bf16[16,8192]{1,0:T(8,128)(2,1)S(1)}, bf16[16,8192]{1,0:T(8,128)(2,1)S(1)}, u32[]{:S(2)}, u32[]{:S(2)}) collective-permute-start(bf16[16,8192]{1,0:T(8,128)(2,1)S(1)} %get-tuple-element.63.refs_0_), channel_id=1, source_target_pairs={{0,1},{1,2},{2,3},{3,4},{4,5},{5,6},{6,7},{7,0},{8,9},{9,10},{10,1... | collective-permute-start | bytes 786440 | tf_op jit(solution)/shard_map/ppermute | solution.py:416
  10.3 11.1 %collective-permute-start.10 = (bf16[16,8192]{1,0:T(8,128)(2,1)S(1)}, bf16[16,8192]{1,0:T(8,128)(2,1)S(1)}, u32[]{:S(2)}, u32[]{:S(2)}) collective-permute-start(bf16[16,8192]{1,0:T(8,128)(2,1)S(1)} %get-tuple-element.64.refs_1_), channel_id=1, source_target_pairs={{0,7},{1,0},{2,1},{3,2},{4,3},{5,4},{6,5},{7,6},{8,15},{9,8},{10,9... | collective-permute-start | bytes 786440 | tf_op jit(solution)/shard_map/ppermute | solution.py:416
  14.3 12.3 %collective-permute-start.3 = (bf16[16,8192]{1,0:T(8,128)(2,1)S(1)}, bf16[16,8192]{1,0:T(8,128)(2,1)S(1)}, u32[]{:S(2)}, u32[]{:S(2)}) collective-permute-start(bf16[16,8192]{1,0:T(8,128)(2,1)S(1)} %get-tuple-element.63.refs_0_), channel_id=1, source_target_pairs={{0,7},{1,0},{2,1},{3,2},{4,3},{5,4},{6,5},{7,6},{8,15},{9,8},{10,9... | collective-permute-start | bytes 786440 | tf_op jit(solution)/shard_map/ppermute | solution.py:416
  16.3 14.1 %collective-permute-start = (bf16[16,8192]{1,0:T(8,128)(2,1)S(1)}, bf16[16,8192]{1,0:T(8,128)(2,1)S(1)}, u32[]{:S(2)}, u32[]{:S(2)}) collective-permute-start(bf16[16,8192]{1,0:T(8,128)(2,1)S(1)} %get-tuple-element.64.refs_1_), channel_id=1, source_target_pairs={{0,1},{1,2},{2,3},{3,4},{4,5},{5,6},{6,7},{7,0},{8,9},{9,10},{10,1... | collective-permute-start | bytes 786440 | tf_op jit(solution)/shard_map/ppermute | solution.py:416
  21.4 27.4 %copy-start.14 = (bf16[16,8192]{1,0:T(8,128)(2,1)}, bf16[16,8192]{1,0:T(8,128)(2,1)S(1)}, u32[]{:S(2)}) copy-start(bf16[16,8192]{1,0:T(8,128)(2,1)S(1)} %collective-permute-done.6.refs_2_) | copy-start | bytes 786436
  21.4 10.4 %collective-permute-start.7 = (bf16[16,8192]{1,0:T(8,128)(2,1)S(1)}, bf16[16,8192]{1,0:T(8,128)(2,1)S(1)}, u32[]{:S(2)}, u32[]{:S(2)}) collective-permute-start(bf16[16,8192]{1,0:T(8,128)(2,1)S(1)} %collective-permute-done.6.refs_2_), channel_id=1, source_target_pairs={{0,1},{1,2},{2,3},{3,4},{4,5},{5,6},{6,7},{7,0},{8,9},{9,10},{10,1... | collective-permute-start | bytes 786440 | tf_op jit(solution)/shard_map/ppermute | solution.py:416
  21.4 27.4 %copy-start.15 = (bf16[16,8192]{1,0:T(8,128)(2,1)}, bf16[16,8192]{1,0:T(8,128)(2,1)S(1)}, u32[]{:S(2)}) copy-start(bf16[16,8192]{1,0:T(8,128)(2,1)S(1)} %collective-permute-done.10.refs_5_) | copy-start | bytes 786436
  21.4 10.9 %collective-permute-start.11 = (bf16[16,8192]{1,0:T(8,128)(2,1)S(1)}, bf16[16,8192]{1,0:T(8,128)(2,1)S(1)}, u32[]{:S(2)}, u32[]{:S(2)}) collective-permute-start(bf16[16,8192]{1,0:T(8,128)(2,1)S(1)} %collective-permute-done.10.refs_5_), channel_id=1, source_target_pairs={{0,7},{1,0},{2,1},{3,2},{4,3},{5,4},{6,5},{7,6},{8,15},{9,8},{10,9... | collective-permute-start | bytes 786440 | tf_op jit(solution)/shard_map/ppermute | solution.py:416
  26.7 22.1 %copy-start.16 = (bf16[16,8192]{1,0:T(8,128)(2,1)}, bf16[16,8192]{1,0:T(8,128)(2,1)S(1)}, u32[]{:S(2)}) copy-start(bf16[16,8192]{1,0:T(8,128)(2,1)S(1)} %collective-permute-done.3.refs_4_) | copy-start | bytes 786436
  26.7 11.2 %collective-permute-start.4 = (bf16[16,8192]{1,0:T(8,128)(2,1)S(1)}, bf16[16,8192]{1,0:T(8,128)(2,1)S(1)}, u32[]{:S(2)}, u32[]{:S(2)}) collective-permute-start(bf16[16,8192]{1,0:T(8,128)(2,1)S(1)} %collective-permute-done.3.refs_4_), channel_id=1, source_target_pairs={{0,7},{1,0},{2,1},{3,2},{4,3},{5,4},{6,5},{7,6},{8,15},{9,8},{10,9... | collective-permute-start | bytes 786440 | tf_op jit(solution)/shard_map/ppermute | solution.py:416
  30.4 18.4 %copy-start.17 = (bf16[16,8192]{1,0:T(8,128)(2,1)}, bf16[16,8192]{1,0:T(8,128)(2,1)S(1)}, u32[]{:S(2)}) copy-start(bf16[16,8192]{1,0:T(8,128)(2,1)S(1)} %collective-permute-done.refs_3_) | copy-start | bytes 786436
  30.4 11.2 %collective-permute-start.1 = (bf16[16,8192]{1,0:T(8,128)(2,1)S(1)}, bf16[16,8192]{1,0:T(8,128)(2,1)}, u32[]{:S(2)}, u32[]{:S(2)}) collective-permute-start(bf16[16,8192]{1,0:T(8,128)(2,1)S(1)} %collective-permute-done.refs_3_), channel_id=1, source_target_pairs={{0,1},{1,2},{2,3},{3,4},{4,5},{5,6},{6,7},{7,0},{8,9},{9,10},{10,1... | collective-permute-start | bytes 786440 | tf_op jit(solution)/shard_map/ppermute | solution.py:416
  31.8 17.0 %copy-start.18 = (bf16[16,8192]{1,0:T(8,128)(2,1)}, bf16[16,8192]{1,0:T(8,128)(2,1)S(1)}, u32[]{:S(2)}) copy-start(bf16[16,8192]{1,0:T(8,128)(2,1)S(1)} %collective-permute-done.7.refs_6_) | copy-start | bytes 786436
  31.8 11.7 %collective-permute-start.8 = (bf16[16,8192]{1,0:T(8,128)(2,1)S(1)}, bf16[16,8192]{1,0:T(8,128)(2,1)}, u32[]{:S(2)}, u32[]{:S(2)}) collective-permute-start(bf16[16,8192]{1,0:T(8,128)(2,1)S(1)} %collective-permute-done.7.refs_6_), channel_id=1, source_target_pairs={{0,1},{1,2},{2,3},{3,4},{4,5},{5,6},{6,7},{7,0},{8,9},{9,10},{10,1... | collective-permute-start | bytes 786440 | tf_op jit(solution)/shard_map/ppermute | solution.py:416
  32.3 11.2 %collective-permute-start.12 = (bf16[16,8192]{1,0:T(8,128)(2,1)S(1)}, bf16[16,8192]{1,0:T(8,128)(2,1)}, u32[]{:S(2)}, u32[]{:S(2)}) collective-permute-start(bf16[16,8192]{1,0:T(8,128)(2,1)S(1)} %collective-permute-done.11.refs_9_), channel_id=1, source_target_pairs={{0,7},{1,0},{2,1},{3,2},{4,3},{5,4},{6,5},{7,6},{8,15},{9,8},{10,9... | collective-permute-start | bytes 786440 | tf_op jit(solution)/shard_map/ppermute | solution.py:416
  37.9 17.8 %collective-permute-start.5 = (bf16[16,8192]{1,0:T(8,128)(2,1)S(1)}, bf16[16,8192]{1,0:T(8,128)(2,1)S(1)}, u32[]{:S(2)}, u32[]{:S(2)}) collective-permute-start(bf16[16,8192]{1,0:T(8,128)(2,1)S(1)} %collective-permute-done.4.refs_8_), channel_id=1, source_target_pairs={{0,7},{1,0},{2,1},{3,2},{4,3},{5,4},{6,5},{7,6},{8,15},{9,8},{10,9... | collective-permute-start | bytes 786440 | tf_op jit(solution)/shard_map/ppermute | solution.py:416
  41.6 14.1 %collective-permute-start.2 = (bf16[16,8192]{1,0:T(8,128)(2,1)}, bf16[16,8192]{1,0:T(8,128)(2,1)S(1)}, u32[]{:S(2)}, u32[]{:S(2)}) collective-permute-start(bf16[16,8192]{1,0:T(8,128)(2,1)} %collective-permute-done.1.refs_7_), channel_id=1, source_target_pairs={{0,1},{1,2},{2,3},{3,4},{4,5},{5,6},{6,7},{7,0},{8,9},{9,10},{10,1... | collective-permute-start | bytes 786440 | tf_op jit(solution)/shard_map/ppermute | solution.py:416
  43.5 12.3 %collective-permute-start.9 = (bf16[16,8192]{1,0:T(8,128)(2,1)}, bf16[16,8192]{1,0:T(8,128)(2,1)S(1)}, u32[]{:S(2)}, u32[]{:S(2)}) collective-permute-start(bf16[16,8192]{1,0:T(8,128)(2,1)} %collective-permute-done.8.refs_10_), channel_id=1, source_target_pairs={{0,1},{1,2},{2,3},{3,4},{4,5},{5,6},{6,7},{7,0},{8,9},{9,10},{10,1... | collective-permute-start | bytes 786440 | tf_op jit(solution)/shard_map/ppermute | solution.py:416
  43.5 12.3 %collective-permute-start.13 = (bf16[16,8192]{1,0:T(8,128)(2,1)}, bf16[16,8192]{1,0:T(8,128)(2,1)S(1)}, u32[]{:S(2)}, u32[]{:S(2)}) collective-permute-start(bf16[16,8192]{1,0:T(8,128)(2,1)} %collective-permute-done.12.refs_11_), channel_id=1, source_target_pairs={{0,7},{1,0},{2,1},{3,2},{4,3},{5,4},{6,5},{7,6},{8,15},{9,8},{10,9... | collective-permute-start | bytes 786440 | tf_op jit(solution)/shard_map/ppermute | solution.py:416
  56.7 20.2 %copy-start.3 = (s32[4]{0:T(128)S(1)}, s32[4]{0:T(128)}, u32[]{:S(2)}) copy-start(s32[4]{0:T(128)} %pad_add_fusion.place_ref) | copy-start | bytes 52
  56.7 20.2 %copy-start.4 = (bf16[1,256,1024]{2,1,0:T(8,128)(2,1)S(1)}, bf16[1,256,1024]{2,1,0:T(8,128)(2,1)}, u32[]{:S(2)}) copy-start(bf16[1,256,1024]{2,1,0:T(8,128)(2,1)} %param.9) | copy-start | bytes 1572868
  56.7 20.2 %copy-start.5 = (bf16[1,256,1024]{2,1,0:T(8,128)(2,1)S(1)}, bf16[1,256,1024]{2,1,0:T(8,128)(2,1)}, u32[]{:S(2)}) copy-start(bf16[1,256,1024]{2,1,0:T(8,128)(2,1)} %param.10) | copy-start | bytes 1572868
  63.5 49.9 %collective-permute-start.23 = (bf16[256,4096]{1,0:T(8,128)(2,1)}, bf16[256,4096]{1,0:T(8,128)(2,1)}, u32[]{:S(2)}, u32[]{:S(2)}) collective-permute-start(bf16[256,4096]{1,0:T(8,128)(2,1)} %get-tuple-element.45), channel_id=1, source_target_pairs={{0,8},{8,0},{1,9},{9,1},{2,10},{10,2},{3,11},{11,3},{4,12},{12,4},... | collective-permute-start | bytes 6291464 | tf_op jit(solution)/shard_map/ppermute | solution.py:412
  63.6 9.6 %collective-permute-start.15 = (bf16[272,256]{1,0:T(8,128)(2,1)}, bf16[272,256]{1,0:T(8,128)(2,1)S(1)}, u32[]{:S(2)}, u32[]{:S(2)}) collective-permute-start(bf16[272,256]{1,0:T(8,128)(2,1)} %get-tuple-element.37.kv0), channel_id=1, source_target_pairs={{0,32},{16,48},{1,33},{17,49},{2,34},{18,50},{3,35},{19,51},{4,36}... | collective-permute-start | bytes 417800 | tf_op jit(solution)/shard_map/ppermute | solution.py:443
  68.7 6.9 %collective-permute-start.14 = (bf16[272,256]{1,0:T(8,128)(2,1)}, bf16[272,256]{1,0:T(8,128)(2,1)S(1)}, u32[]{:S(2)}, u32[]{:S(2)}) collective-permute-start(bf16[272,256]{1,0:T(8,128)(2,1)} %get-tuple-element.37.kv0), channel_id=1, source_target_pairs={{0,16},{16,32},{32,48},{1,17},{17,33},{33,49},{2,18},{18,34},{34,5... | collective-permute-start | bytes 417800 | tf_op jit(solution)/shard_map/ppermute | solution.py:442
  71.3 4.4 %collective-permute-start.17 = (bf16[272,256]{1,0:T(8,128)(2,1)}, bf16[272,256]{1,0:T(8,128)(2,1)S(1)}, u32[]{:S(2)}, u32[]{:S(2)}) collective-permute-start(bf16[272,256]{1,0:T(8,128)(2,1)} %get-tuple-element.37.kv0), channel_id=1, source_target_pairs={{0,8},{1,9},{2,10},{3,11},{4,12},{5,13},{6,14},{7,15},{16,24},{17,... | collective-permute-start | bytes 417800 | tf_op jit(solution)/shard_map/ppermute | solution.py:444
  73.1 3.3 %collective-permute-start.18 = (bf16[272,256]{1,0:T(8,128)(2,1)S(1)}, bf16[272,256]{1,0:T(8,128)(2,1)S(1)}, u32[]{:S(2)}, u32[]{:S(2)}) collective-permute-start(bf16[272,256]{1,0:T(8,128)(2,1)S(1)} %collective-permute-done.15.kv2), channel_id=1, source_target_pairs={{8,0},{9,1},{10,2},{11,3},{12,4},{13,5},{14,6},{15,7},{24,16},{25,... | collective-permute-start | bytes 417800 | tf_op jit(solution)/shard_map/ppermute | solution.py:446
  75.5 1.4 collective-permute-start.16
  91.5 21.9 %copy-start = (bf16[256,4096]{1,0:T(8,128)(2,1)S(1)}, bf16[256,4096]{1,0:T(8,128)(2,1)}, u32[]{:S(2)}) copy-start(bf16[256,4096]{1,0:T(8,128)(2,1)} %get-tuple-element.44.refs_0_.refs_1_.refs_2_.refs_3_) | copy-start | bytes 6291460
  91.5 2.0 %collective-permute-start.19 = (f32[2,256,256]{2,1,0:T(8,128)S(1)}, f32[2,256,256]{2,1,0:T(8,128)}, u32[]{:S(2)}, u32[]{:S(2)}) collective-permute-start(f32[2,256,256]{2,1,0:T(8,128)S(1)} %get-tuple-element.41), channel_id=1, source_target_pairs={{0,8},{8,0},{1,9},{9,1},{2,10},{10,2},{3,11},{11,3},{4,12},{12,4},... | collective-permute-start | bytes 1572872 | tf_op jit(solution)/shard_map/ppermute | solution.py:412
  94.7 8.1 %collective-permute-start.20 = (bf16[256,256]{1,0:T(8,128)(2,1)S(1)}, bf16[256,256]{1,0:T(8,128)(2,1)S(1)}, u32[]{:S(2)}, u32[]{:S(2)}) collective-permute-start(bf16[256,256]{1,0:T(8,128)(2,1)S(1)} %get-tuple-element.61), channel_id=1, source_target_pairs={{16,0},{32,16},{48,32},{17,1},{33,17},{49,33},{18,2},{34,18},{50,3... | collective-permute-start | bytes 393224 | tf_op jit(solution)/shard_map/ppermute | solution.py:458
  96.0 9.9 %collective-permute-start.21 = (bf16[256,256]{1,0:T(8,128)(2,1)S(1)}, bf16[256,256]{1,0:T(8,128)(2,1)S(1)}, u32[]{:S(2)}, u32[]{:S(2)}) collective-permute-start(bf16[256,256]{1,0:T(8,128)(2,1)S(1)} %get-tuple-element.62), channel_id=1, source_target_pairs={{32,0},{48,16},{33,1},{49,17},{34,2},{50,18},{35,3},{51,19},{36,4}... | collective-permute-start | bytes 393224 | tf_op jit(solution)/shard_map/ppermute | solution.py:459
  107.6 5.8 %collective-permute-start.22 = (bf16[256,256]{1,0:T(8,128)(2,1)}, bf16[256,256]{1,0:T(8,128)(2,1)S(1)}, u32[]{:S(2)}, u32[]{:S(2)}) collective-permute-start(bf16[256,256]{1,0:T(8,128)(2,1)} %fusion.5.g_ref), channel_id=1, source_target_pairs={{0,8},{8,0},{1,9},{9,1},{2,10},{10,2},{3,11},{11,3},{4,12},{12,4},... | collective-permute-start | bytes 393224 | tf_op jit(solution)/shard_map/ppermute | solution.py:412
  107.6 15.7 %all-to-all-start = ((bf16[8,32,256]{2,1,0:T(8,128)(2,1)}), bf16[8,32,256]{2,1,0:T(8,128)(2,1)S(1)}, u32[]{:S(2)}, u32[]{:S(2)}) async-start(bf16[8,32,256]{2,1,0:T(8,128)(2,1)} %bitcast.13), calls=%async_computation | async-start | bytes 262144 | tf_op jit(solution)/shard_map/all_to_all | solution.py:464
  123.3 14.2 %collective-permute-start.27 = (bf16[8,1024,256]{2,1,0:T(8,128)(2,1)}, bf16[8,1024,256]{2,1,0:T(8,128)(2,1)}, u32[]{:S(2)}, u32[]{:S(2)}) collective-permute-start(bf16[8,1024,256]{2,1,0:T(8,128)(2,1)} %bitcast.35), channel_id=1, source_target_pairs={{0,8},{8,0},{1,9},{9,1},{2,10},{10,2},{3,11},{11,3},{4,12},{12,4},... | collective-permute-start | bytes 12582920 | tf_op jit(solution)/shard_map/ppermute | solution.py:412
  123.3 30.9 %all-to-all-start.1 = ((bf16[4,4,256,256]{3,2,1,0:T(8,128)(2,1)}), bf16[4,4,256,256]{3,2,1,0:T(8,128)(2,1)S(1)}, u32[]{:S(2)}, u32[]{:S(2)}) async-start(bf16[4,4,256,256]{3,2,1,0:T(8,128)(2,1)} %copy-done.1), calls=%async_computation.1 | async-start | bytes 4194304 | tf_op jit(solution)/shard_map/all_to_all | solution.py:468
  127.1 5.8 %collective-permute-start.26 = (bf16[8,32,256]{2,1,0:T(8,128)(2,1)S(1)}, bf16[8,32,256]{2,1,0:T(8,128)(2,1)S(1)}, u32[]{:S(2)}, u32[]{:S(2)}) collective-permute-start(bf16[8,32,256]{2,1,0:T(8,128)(2,1)S(1)} %all-to-all-done.b0), channel_id=1, source_target_pairs={{0,192},{64,0},{128,64},{192,128},{1,193},{65,1},{129,65},{193,129... | collective-permute-start | bytes 393224 | tf_op jit(solution)/shard_map/ppermute | solution.py:416
  127.6 9.0 %collective-permute-start.25 = (bf16[8,32,256]{2,1,0:T(8,128)(2,1)S(1)}, bf16[8,32,256]{2,1,0:T(8,128)(2,1)S(1)}, u32[]{:S(2)}, u32[]{:S(2)}) collective-permute-start(bf16[8,32,256]{2,1,0:T(8,128)(2,1)S(1)} %all-to-all-done.b0), channel_id=1, source_target_pairs={{0,128},{64,192},{128,0},{192,64},{1,129},{65,193},{129,1},{193,65... | collective-permute-start | bytes 393224 | tf_op jit(solution)/shard_map/ppermute | solution.py:416
  130.1 7.5 %collective-permute-start.24 = (bf16[8,32,256]{2,1,0:T(8,128)(2,1)S(1)}, bf16[8,32,256]{2,1,0:T(8,128)(2,1)S(1)}, u32[]{:S(2)}, u32[]{:S(2)}) collective-permute-start(bf16[8,32,256]{2,1,0:T(8,128)(2,1)S(1)} %all-to-all-done.b0), channel_id=1, source_target_pairs={{0,64},{64,128},{128,192},{192,0},{1,65},{65,129},{129,193},{193,1... | collective-permute-start | bytes 393224 | tf_op jit(solution)/shard_map/ppermute | solution.py:416
  144.7 12.5 %collective-permute-start.28 = (bf16[2,32,1024]{2,1,0:T(8,128)(2,1)}, bf16[2,32,1024]{2,1,0:T(8,128)(2,1)S(1)}, u32[]{:S(2)}, u32[]{:S(2)}) collective-permute-start(bf16[2,32,1024]{2,1,0:T(8,128)(2,1)} %get-tuple-element.50), channel_id=1, source_target_pairs={{0,192},{64,0},{128,64},{192,128},{1,193},{65,1},{129,65},{193,129... | collective-permute-start | bytes 393224 | tf_op jit(solution)/shard_map/ppermute | solution.py:416
  147.4 11.8 %collective-permute-start.29 = (bf16[2,32,1024]{2,1,0:T(8,128)(2,1)}, bf16[2,32,1024]{2,1,0:T(8,128)(2,1)S(1)}, u32[]{:S(2)}, u32[]{:S(2)}) collective-permute-start(bf16[2,32,1024]{2,1,0:T(8,128)(2,1)} %get-tuple-element.51), channel_id=1, source_target_pairs={{0,128},{64,192},{128,0},{192,64},{1,129},{65,193},{129,1},{193,65... | collective-permute-start | bytes 393224 | tf_op jit(solution)/shard_map/ppermute | solution.py:416
  147.7 11.6 %collective-permute-start.30 = (bf16[2,32,1024]{2,1,0:T(8,128)(2,1)}, bf16[2,32,1024]{2,1,0:T(8,128)(2,1)S(1)}, u32[]{:S(2)}, u32[]{:S(2)}) collective-permute-start(bf16[2,32,1024]{2,1,0:T(8,128)(2,1)} %get-tuple-element.52), channel_id=1, source_target_pairs={{0,64},{64,128},{128,192},{192,0},{1,65},{65,129},{129,193},{193,1... | collective-permute-start | bytes 393224 | tf_op jit(solution)/shard_map/ppermute | solution.py:416
  154.5 6.2 %collective-permute-start.31 = (bf16[256,256]{1,0:T(8,128)(2,1)S(1)}, bf16[256,256]{1,0:T(8,128)(2,1)S(1)}, u32[]{:S(2)}, u32[]{:S(2)}) collective-permute-start(bf16[256,256]{1,0:T(8,128)(2,1)S(1)} %get-tuple-element.56), channel_id=1, source_target_pairs={{0,64},{64,128},{128,192},{192,0},{1,65},{65,129},{129,193},{193,1... | collective-permute-start | bytes 393224 | tf_op jit(solution)/shard_map/ppermute | solution.py:416
  156.0 7.6 %collective-permute-start.32 = (bf16[256,256]{1,0:T(8,128)(2,1)S(1)}, bf16[256,256]{1,0:T(8,128)(2,1)S(1)}, u32[]{:S(2)}, u32[]{:S(2)}) collective-permute-start(bf16[256,256]{1,0:T(8,128)(2,1)S(1)} %get-tuple-element.57), channel_id=1, source_target_pairs={{0,128},{64,192},{128,0},{192,64},{1,129},{65,193},{129,1},{193,65... | collective-permute-start | bytes 393224 | tf_op jit(solution)/shard_map/ppermute | solution.py:416
  157.2 7.2 %collective-permute-start.33 = (bf16[256,256]{1,0:T(8,128)(2,1)S(1)}, bf16[256,256]{1,0:T(8,128)(2,1)S(1)}, u32[]{:S(2)}, u32[]{:S(2)}) collective-permute-start(bf16[256,256]{1,0:T(8,128)(2,1)S(1)} %get-tuple-element.58), channel_id=1, source_target_pairs={{0,192},{64,0},{128,64},{192,128},{1,193},{65,1},{129,65},{193,129... | collective-permute-start | bytes 393224 | tf_op jit(solution)/shard_map/ppermute | solution.py:416
  (13 other events, 60.3 us)
Sparse Core Ops, SparseCore 0:
  63.6 55.5 all-gather.2

commit v3 on v2

--- a/solution.py
+++ b/solution.py
@@ -10,9 +10,11 @@
 
 HD = 128
 SLOTS = 5
-PAIR = 2
+PAIR = 4
 EARLY = [(s, h) for s in (0, 1, 7, 2, 6) for h in (0, 1)] + [(3, 0), (5, 1)]
 LATE = [(3, 1), (5, 0), (4, 0), (4, 1)]
+FIRST = [(4, 0), (3, 1), (4, 1), (5, 0), (3, 0), (2, 1), (5, 1), (6, 0)]
+REST = [(s, h) for s in range(8) for h in (0, 1) if (s, h) not in FIRST]
 NEG = -1e30
 MIB = 1024 * 1024
 VMEM = 56 * MIB
@@ -22,7 +24,7 @@
 
 def attention_kernel(place_ref, kv0, kv1, kv2, kv3, near, far, q_ref, do_ref,
                      att_ref, dq_ref, p0, p1, p2, p34,
-                     k_all, v_all, kt_all, vt_all, s_ref, pb_ref, ds_ref, dkv_ref, thr_ref):
+                     k_all, v_all, kt_all, vt_all, s_ref, pb_ref, ds_ref, dp_ref, dkv_ref, thr_ref):
     rows = q_ref.shape[0]
     scale = 1.0 / math.sqrt(HD)
     log2e = math.log2(math.e)
@@ -71,6 +73,7 @@
             e = jnp.exp2((s_ref[h, here, :] - top[h]) * (scale * log2e))
             s_ref[h, here, :] = e
             total[h] = total[h] + jnp.sum(e, axis=0, keepdims=True)
+            dp_ref[h, here, :] = jnp.dot(v_all[here, :], do_t[h], preferred_element_type=F32)
     inv = [1.0 / t for t in total]
     for here in spans:
         for h in heads:
@@ -84,8 +87,7 @@
         dk = jnp.zeros((rows, HD), F32)
         dv = jnp.zeros((rows, HD), F32)
         for h in heads:
-            dp = jnp.dot(v_all[here, :], do_t[h], preferred_element_type=F32)
-            ds = (s_ref[h, here, :] * inv[h] * (dp - delta[h])).astype(BF16)
+            ds = (s_ref[h, here, :] * inv[h] * (dp_ref[h, here, :] - delta[h])).astype(BF16)
             ds_ref[h, here, :] = ds
             dk = dk + jnp.dot(ds, q[h], preferred_element_type=F32)
             dv = dv + jnp.dot(pb_ref[h, here, :], do[h], preferred_element_type=F32)
@@ -128,6 +130,7 @@
                 pltpu.VMEM((PAIR, keys, rows), F32),
                 pltpu.VMEM((PAIR, keys, rows), BF16),
                 pltpu.VMEM((PAIR, keys, rows), BF16),
+                pltpu.VMEM((PAIR, keys, rows), F32),
                 pltpu.VMEM((keys, 2 * HD), F32),
                 pltpu.VMEM((8, rows), jnp.int32),
             ],
@@ -138,7 +141,7 @@
             part, part, part,
             jax.ShapeDtypeStruct((2, rows, 2 * HD), F32),
         ],
-        compiler_params=pltpu.CompilerParams(vmem_limit_bytes=20 * MIB),
+        compiler_params=pltpu.CompilerParams(vmem_limit_bytes=30 * MIB),
         cost_estimate=pl.CostEstimate(
             flops=12 * keys * width * rows, bytes_accessed=6 * MIB,
             transcendentals=keys * rows * heads,
@@ -253,7 +256,6 @@
 
 def weight_grad_kernel(ring, place_ref, g_ref, gs_ref, *refs):
     hidden, (out_ref, grads_t, turn) = refs[:8], refs[8:]
-    nx = out_ref.shape[1]
     few = g_ref.shape[0] // (2 * ring)
 
     @pl.when(pl.program_id(0) == 0)
@@ -263,8 +265,8 @@
                 turn[i * few:(i + 1) * few, :] = g[pl.ds(token(place_ref, s, h, ring, few), few), :]
             grads_t[p] = turn[...].T
 
-    for i, (mine, other) in enumerate(zip(hidden[:nx], hidden[nx:])):
-        out_ref[0, lax.rem(i + nx - place_ref[0], nx)] = (
+    for i, (mine, other) in enumerate(zip(hidden[:4], hidden[4:])):
+        out_ref[i] = (
             jnp.dot(grads_t[0], mine[...], preferred_element_type=F32)
             + jnp.dot(grads_t[1], other[...], preferred_element_type=F32)
         ).astype(BF16)
@@ -276,125 +278,87 @@
     flat = pl.BlockSpec((rows, cols), lambda r, place: (0, 0))
 
     def column(i):
-        return pl.BlockSpec((rows, block), lambda r, place: (0, i * ny + r))
+        return pl.BlockSpec((rows, block), lambda r, place: (0, r * ny + i))
 
     return pl.pallas_call(
         functools.partial(weight_grad_kernel, ring),
         grid_spec=pltpu.PrefetchScalarGridSpec(
             num_scalar_prefetch=1,
-            grid=(ny,),
-            in_specs=[flat, flat] + [column(i) for i in range(nx)] * 2,
-            out_specs=pl.BlockSpec((1, nx, cols, block), lambda r, place: (r, 0, 0, 0)),
+            grid=(nx,),
+            in_specs=[flat, flat] + [column(i) for i in range(ny)] * 2,
+            out_specs=pl.BlockSpec((ny, cols, block), lambda r, place: (r, 0, 0)),
             scratch_shapes=[pltpu.VMEM((2, cols, rows), BF16), pltpu.VMEM((rows, cols), BF16)],
         ),
-        out_shape=jax.ShapeDtypeStruct((ny, nx, cols, block), BF16),
+        out_shape=jax.ShapeDtypeStruct((nx * ny, cols, block), BF16),
         compiler_params=pltpu.CompilerParams(vmem_limit_bytes=10 * MIB),
         cost_estimate=pl.CostEstimate(
             flops=4 * rows * cols * block * nx * ny, bytes_accessed=6 * MIB, transcendentals=0
         ),
-    )(place, grads, other_grads, *[mine] * nx, *[other] * nx)
-
-
-def add_kernel(parts, *outs):
-    for i, out in enumerate(outs):
-        total = parts[0, i].astype(F32)
-        for r in range(1, parts.shape[0]):
-            total = total + parts[r, i].astype(F32)
-        out[...] = total.astype(BF16)
-
-
-def add(parts):
-    ny, nx, cols, block = parts.shape
-    return pl.pallas_call(
-        add_kernel,
-        grid=(1,),
-        in_specs=[pl.BlockSpec(parts.shape, lambda i: (0, 0, 0, 0))],
-        out_specs=[pl.BlockSpec((cols, block), lambda i: (0, 0))] * nx,
-        out_shape=[jax.ShapeDtypeStruct((cols, block), BF16)] * nx,
-        compiler_params=pltpu.CompilerParams(vmem_limit_bytes=10 * MIB),
-    )(parts)
-
-
-def finish_kernel(a, b, c, d, key_ref, value_ref):
-    total = (a[...].astype(F32) + b[...].astype(F32)) + (c[...].astype(F32) + d[...].astype(F32))
+    )(place, grads, other_grads, *[mine] * ny, *[other] * ny)
+
+
+def finish_kernel(parts, key_ref, value_ref):
+    total = parts[0].astype(F32)
+    for i in range(1, parts.shape[0]):
+        total = total + parts[i].astype(F32)
     key_ref[...] = total[:HD].T
     value_ref[...] = total[HD:].T
 
 
 def finish(parts):
-    cols, block = parts[0].shape
+    _, cols, block = parts.shape
     half = pl.BlockSpec((block, HD), lambda i: (0, 0))
     shape = jax.ShapeDtypeStruct((block, HD), F32)
     return pl.pallas_call(
         finish_kernel,
         grid=(1,),
-        in_specs=[pl.BlockSpec((cols, block), lambda i: (0, 0))] * 4,
+        in_specs=[pl.BlockSpec(parts.shape, lambda i: (0, 0, 0))],
         out_specs=[half, half],
         out_shape=[shape, shape],
         compiler_params=pltpu.CompilerParams(vmem_limit_bytes=8 * MIB),
-    )(*parts)
-
-
-def spread_kernel(b0, b1, b2, b3, wa_ref, wb_ref, o0, o1, o2, o3, left):
-    few = o0.shape[1]
-    heads = left.shape[0]
+    )(parts)
+
+
+def spread_kernel(order, ring, place_ref, g_ref, wk_ref, wv_ref, *refs):
+    outs, rows = refs[:-1], refs[-1]
+    few = outs[0].shape[0]
 
     @pl.when(pl.program_id(0) == 0)
     def _():
-        for s, b in enumerate((b0, b1, b2, b3)):
-            left[:, s * few:(s + 1) * few, :] = b[...]
+        for i, (s, h) in enumerate(order):
+            rows[i * few:(i + 1) * few, :] = g_ref[
+                pl.ds(token(place_ref, ring - s, h, ring, few), few), :
+            ]
 
     contract = (((1,), (1,)), ((), ()))
-    for p, w in enumerate((wa_ref, wb_ref)):
-        acc = lax.dot_general(w[0], left[0], contract, preferred_element_type=F32)
-        for h in range(1, heads):
-            acc = acc + lax.dot_general(w[h], left[h], contract, preferred_element_type=F32)
-        turned = acc.T.astype(BF16)
-        for s, out in enumerate((o0, o1, o2, o3)):
-            out[p] = turned[s * few:(s + 1) * few]
-
-
-def spread(blocks, wa, wb):
-    heads, few, cols = blocks[0].shape
-    depth = wa.shape[1]
-    tile = depth // 4
-    weight = pl.BlockSpec((heads, tile, cols), lambda i: (0, i, 0))
+    part = lax.dot_general(
+        rows[:, :HD], wk_ref[...], contract, preferred_element_type=F32
+    ) + lax.dot_general(rows[:, HD:], wv_ref[...], contract, preferred_element_type=F32)
+    for i, out in enumerate(outs):
+        out[...] = part[i * few:(i + 1) * few].astype(BF16)
+
+
+def spread(place, order, grads, key_weight, value_weight, ring):
+    rows, cols = grads.shape
+    few = rows // (2 * ring)
+    width = key_weight.shape[0]
+    tile = width // 8
+    weight = pl.BlockSpec((tile, HD), lambda i, place: (i, 0))
     return pl.pallas_call(
-        spread_kernel,
-        grid=(depth // tile,),
-        in_specs=[pl.BlockSpec((heads, few, cols), lambda i: (0, 0, 0))] * 4 + [weight, weight],
-        out_specs=[pl.BlockSpec((2, few, tile), lambda i: (0, 0, i))] * 4,
-        out_shape=[jax.ShapeDtypeStruct((2, few, depth), BF16)] * 4,
-        scratch_shapes=[pltpu.VMEM((heads, 4 * few, cols), BF16)],
-        compiler_params=pltpu.CompilerParams(vmem_limit_bytes=VMEM),
-        cost_estimate=pl.CostEstimate(
-            flops=16 * few * heads * cols * depth, bytes_accessed=9 * MIB, transcendentals=0
-        ),
-    )(*blocks, wa, wb)
-
-
-def assemble_kernel(place_ref, a, b, c, d, out_ref):
-    depth = a.shape[2]
-    for s, piece in enumerate((a, b, c, d)):
-        part = lax.rem(place_ref[0] + s, 4) * 2
-        for p in range(2):
-            core = place_ref[2] if p == 0 else 1 - place_ref[2]
-            out_ref[:, pl.ds(pl.multiple_of((part + core) * depth, depth), depth)] = piece[p]
-
-
-def assemble(place, pieces):
-    two, few, depth = pieces[0].shape
-    return pl.pallas_call(
-        assemble_kernel,
+        functools.partial(spread_kernel, order, ring),
         grid_spec=pltpu.PrefetchScalarGridSpec(
             num_scalar_prefetch=1,
-            grid=(1,),
-            in_specs=[pl.BlockSpec((two, few, depth), lambda i, place: (0, 0, 0))] * 4,
-            out_specs=pl.BlockSpec((few, 4 * two * depth), lambda i, place: (0, 0)),
-        ),
-        out_shape=jax.ShapeDtypeStruct((few, 4 * two * depth), BF16),
-        compiler_params=pltpu.CompilerParams(vmem_limit_bytes=6 * MIB),
-    )(place, *pieces)
+            grid=(width // tile,),
+            in_specs=[pl.BlockSpec((rows, cols), lambda i, place: (0, 0)), weight, weight],
+            out_specs=[pl.BlockSpec((few, tile), lambda i, place: (0, i))] * len(order),
+            scratch_shapes=[pltpu.VMEM((few * len(order), cols), BF16)],
+        ),
+        out_shape=[jax.ShapeDtypeStruct((few, width), BF16)] * len(order),
+        compiler_params=pltpu.CompilerParams(vmem_limit_bytes=8 * MIB),
+        cost_estimate=pl.CostEstimate(
+            flops=2 * few * len(order) * cols * width, bytes_accessed=6 * MIB, transcendentals=0
+        ),
+    )(place, grads, key_weight, value_weight)
 
 
 def on_device(hidden, key_weight, value_weight, queries, out_grad, segment_ids):
@@ -429,14 +393,6 @@
         place, LATE, [ring[i] for i in LATE], *weights, heads, (segment_ids, *early)
     )
 
-    depth = width // (2 * nx)
-    first = (x * 2 + core) * depth
-    part_w = jnp.concatenate(
-        [lax.dynamic_slice_in_dim(w, first, depth, axis=0) for w in (key_weight, value_weight)], axis=1
-    )
-    part_w, kv = lax.optimization_barrier((part_w, kv))
-    all_w = lax.all_gather(part_w, "tp", axis=0)
-
     down1 = [(i, i + 1) for i in range(ny - 1)]
     down2 = [(i, i + 2) for i in range(ny - 2)]
     kv1 = lax.ppermute(kv, "y", down1)
@@ -459,22 +415,34 @@
     got2 = lax.ppermute(send2, "y", up2)
     grads = (own + got1.astype(F32) + got2.astype(F32)).astype(BF16)
 
+    other_grads = swapped(grads)
+    part = dict(zip(FIRST, spread(place, FIRST, grads, *weights, heads)))
     other = swapped(theirs)
-    other_grads = swapped(grads)
-    by_head = lax.all_to_all(grads.reshape(heads, x_count, 2 * HD), "tp", 0, 0, tiled=True)
+    grads, _ = lax.optimization_barrier((grads, part))
     sums = weight_grad(place, grads, other_grads, mine, other, nx, ny, heads)
-    by_head, sums, all_w = lax.optimization_barrier((by_head, sums, all_w))
-    other_w = swapped(all_w)
-    sums = lax.all_to_all(sums, "y", 0, 0, tiled=True)
-
-    group_heads = [by_head] + [shifted(by_head, s) for s in range(1, nx)]
-    pieces = spread(group_heads, all_w, other_w)
-    _, sums = lax.optimization_barrier((pieces, sums))
-    sums = add(sums)
-    key_wgrad, value_wgrad = finish(
-        [sums[0]] + [shifted(sums[s], s) for s in range(1, nx)]
-    )
-    hidden_grad = assemble(place, [pieces[0]] + [shifted(pieces[s], nx - s) for s in range(1, nx)])
+    grads, sums = lax.optimization_barrier((grads, sums))
+    key_wgrad, value_wgrad = finish(lax.all_to_all(sums, ("dp", "y"), 0, 0, tiled=True))
+
+    part.update(zip(REST, spread(place, REST, grads, *weights, heads)))
+
+    def travel(half, steps, by):
+        moving = shifted(part[steps[0], half], by, "tp")
+        for i, s in enumerate(steps[1:]):
+            if i == 0:
+                moving, _ = lax.optimization_barrier((moving, sums))
+            moving = (moving.astype(F32) + part[s, half].astype(F32)).astype(BF16)
+            moving = shifted(moving, by, "tp")
+        return moving
+
+    came = [
+        travel(0, (4, 3, 2, 1), 1), travel(0, (5, 6, 7), -1),
+        travel(1, (3, 2, 1), 1), travel(1, (4, 5, 6, 7), -1),
+    ]
+    came, key_wgrad, value_wgrad = lax.optimization_barrier((came, key_wgrad, value_wgrad))
+    hidden_grad = jnp.concatenate([
+        part[0, h].astype(F32) + came[2 * h].astype(F32) + came[2 * h + 1].astype(F32)
+        for h in range(2)
+    ]).astype(BF16)
     return (
         att[None],
         dq[None],

time: 173 us -> 163 us (0.942)
  between operations: 14.4 us -> 1.08 us
  waiting for transfers between devices: 42.5 us -> 35.5 us
  starting transfers between devices: 64 us -> 68.7 us
  other arithmetic: 4.27 us -> 8.36 us
    all_to_all x2 -> x1, waiting for transfers between devices: 8.59 us -> 0.01 us  [on_device(): lax.all_to_all(sums, ('dp', 'y'), 0, 0, tiled=True)]
    ppermute x23 -> x28, starting transfers between devices: 40.6 us -> 48.2 us  [shifted(): return lax.ppermute(a, axis, [(i, (i + s) % n) for i in range(n)])]
    convert_element_type x0 -> x10, other arithmetic: none -> 4.58 us  [travel(): moving = (moving.astype(F32) + part[s, half].astype(F32)).astype(BF16)]
    all_to_all x2 -> x1, starting transfers between devices: 9.57 us -> 6.66 us  [on_device(): lax.all_to_all(sums, ('dp', 'y'), 0, 0, tiled=True)]
    pallas_call x4 -> x3, Pallas kernels: 8.89 us -> 10.8 us  [the longest x2 8.21 us: spread(): pl.pallas_call(functools.partial(spread_kernel, order, ring), grid_spec=p...]
    ppermute x5 -> x4, waiting for transfers between devices: 2.41 us -> 3.96 us  [swapped(): return lax.ppermute(a, 'core', swap)]
    unnamed x48 -> x44, local copies, waits for them, and re-layouts: 3.79 us -> 4.78 us
    ppermute x23 -> x28, waiting for transfers between devices: 21 us -> 21.1 us  [shifted(): return lax.ppermute(a, axis, [(i, (i + s) % n) for i in range(n)])]
  transfers between devices with their start and end apart: 37 -> 39, of which waited for: 19 -> 18; matrix products, arithmetic and copies ran while one was open for 3% -> 5% of each run, Pallas kernels for 19% -> 22%
where the time goes in v3:
time: 163 us; the launch traced here: 162 us
  starting transfers between devices  68.7 us (42%)
  Pallas kernels  42.1 us (26%)
  waiting for transfers between devices  35.5 us (22%)
  other arithmetic  8.36 us (5%)
  local copies, waits for them, and re-layouts  5.85 us (4%)
    ppermute x28, starting transfers between devices, shifted(): return lax.ppermute(a, axis, [(i, (i + s) % n) for i in range(n)])  48.2 us
    ppermute x28, waiting for transfers between devices, shifted(): return lax.ppermute(a, axis, [(i, (i + s) % n) for i in range(n)])  21.1 us
    pallas_call x2, Pallas kernels, project(): pl.pallas_call(functools.partial(project_kernel, order, ring, bool(rest))...  13.5 us
    pallas_call x1, Pallas kernels, attention(): pl.pallas_call(attention_kernel, grid_spec=pltpu.PrefetchScalarGridSpec(n...  13.2 us
    pallas_call x2, Pallas kernels, spread(): pl.pallas_call(functools.partial(spread_kernel, order, ring), grid_spec=p...  8.21 us
    all_to_all x1, starting transfers between devices, on_device(): lax.all_to_all(sums, ('dp', 'y'), 0, 0, tiled=True)  6.66 us
    ppermute x1, waiting for transfers between devices, on_device(): got1 = lax.ppermute(send1, 'y', up1)  5.48 us
    ppermute x1, starting transfers between devices, on_device(): kv2 = lax.ppermute(kv, 'y', down2)  5.11 us
  transfers between devices with their start and end apart: 39, of which 18 were waited for; matrix products, arithmetic and copies ran while one was open for 5% of the time, Pallas kernels for 22%

profile of v3, /device:TPU:2, one launch (start us, length us, event | category | flops | bytes accessed | tf_op | source)
XLA Modules:
  0.0 161.6 jit_solution(8148515852567222723)
XLA Ops:
  0.6 1.1 slice_bitcast_fusion.1
  1.7 2.0 %collective-permute-start.6 = (bf16[16,8192]{1,0:T(8,128)(2,1)S(1)}, bf16[16,8192]{1,0:T(8,128)(2,1)S(1)}, u32[]{:S(2)}, u32[]{:S(2)}) collective-permute-start(bf16[16,8192]{1,0:T(8,128)(2,1)S(1)} %get-tuple-element.93.refs_0_), channel_id=1, source_target_pairs={{0,1},{1,2},{2,3},{3,4},{4,5},{5,6},{6,7},{7,0},{8,9},{9,10},{10,1... | collective-permute-start | bytes 786440 | tf_op jit(solution)/shard_map/ppermute | solution.py:380
  3.7 4.0 %collective-permute-start.10 = (bf16[16,8192]{1,0:T(8,128)(2,1)S(1)}, bf16[16,8192]{1,0:T(8,128)(2,1)S(1)}, u32[]{:S(2)}, u32[]{:S(2)}) collective-permute-start(bf16[16,8192]{1,0:T(8,128)(2,1)S(1)} %get-tuple-element.94.refs_1_), channel_id=1, source_target_pairs={{0,7},{1,0},{2,1},{3,2},{4,3},{5,4},{6,5},{7,6},{8,15},{9,8},{10,9... | collective-permute-start | bytes 786440 | tf_op jit(solution)/shard_map/ppermute | solution.py:380
  7.7 1.9 %collective-permute-start.3 = (bf16[16,8192]{1,0:T(8,128)(2,1)S(1)}, bf16[16,8192]{1,0:T(8,128)(2,1)S(1)}, u32[]{:S(2)}, u32[]{:S(2)}) collective-permute-start(bf16[16,8192]{1,0:T(8,128)(2,1)S(1)} %get-tuple-element.93.refs_0_), channel_id=1, source_target_pairs={{0,7},{1,0},{2,1},{3,2},{4,3},{5,4},{6,5},{7,6},{8,15},{9,8},{10,9... | collective-permute-start | bytes 786440 | tf_op jit(solution)/shard_map/ppermute | solution.py:380
  9.8 5.0 %collective-permute-done.6.refs_2_ = bf16[16,8192]{1,0:T(8,128)(2,1)S(1)} collective-permute-done((bf16[16,8192]{1,0:T(8,128)(2,1)S(1)}, bf16[16,8192]{1,0:T(8,128)(2,1)S(1)}, u32[]{:S(2)}, u32[]{:S(2)}) %collective-permute-start.6) | collective-permute-done | bytes 262176 | tf_op jit(solution)/shard_map/ppermute | solution.py:380
  14.8 3.3 %collective-permute-start.11 = (bf16[16,8192]{1,0:T(8,128)(2,1)S(1)}, bf16[16,8192]{1,0:T(8,128)(2,1)S(1)}, u32[]{:S(2)}, u32[]{:S(2)}) collective-permute-start(bf16[16,8192]{1,0:T(8,128)(2,1)S(1)} %collective-permute-done.10.refs_5_), channel_id=1, source_target_pairs={{0,7},{1,0},{2,1},{3,2},{4,3},{5,4},{6,5},{7,6},{8,15},{9,8},{10,9... | collective-permute-start | bytes 786440 | tf_op jit(solution)/shard_map/ppermute | solution.py:380
  18.2 1.9 %collective-permute-done.3.refs_4_ = bf16[16,8192]{1,0:T(8,128)(2,1)S(1)} collective-permute-done((bf16[16,8192]{1,0:T(8,128)(2,1)S(1)}, bf16[16,8192]{1,0:T(8,128)(2,1)S(1)}, u32[]{:S(2)}, u32[]{:S(2)}) %collective-permute-start.3) | collective-permute-done | bytes 262176 | tf_op jit(solution)/shard_map/ppermute | solution.py:380
  20.1 3.7 %collective-permute-start.4 = (bf16[16,8192]{1,0:T(8,128)(2,1)S(1)}, bf16[16,8192]{1,0:T(8,128)(2,1)S(1)}, u32[]{:S(2)}, u32[]{:S(2)}) collective-permute-start(bf16[16,8192]{1,0:T(8,128)(2,1)S(1)} %collective-permute-done.3.refs_4_), channel_id=1, source_target_pairs={{0,7},{1,0},{2,1},{3,2},{4,3},{5,4},{6,5},{7,6},{8,15},{9,8},{10,9... | collective-permute-start | bytes 786440 | tf_op jit(solution)/shard_map/ppermute | solution.py:380
  23.8 1.4 collective-permute-done.7.refs_6_
  25.7 3.7 %collective-permute-start.12 = (bf16[16,8192]{1,0:T(8,128)(2,1)S(1)}, bf16[16,8192]{1,0:T(8,128)(2,1)}, u32[]{:S(2)}, u32[]{:S(2)}) collective-permute-start(bf16[16,8192]{1,0:T(8,128)(2,1)S(1)} %collective-permute-done.11.refs_9_), channel_id=1, source_target_pairs={{0,7},{1,0},{2,1},{3,2},{4,3},{5,4},{6,5},{7,6},{8,15},{9,8},{10,9... | collective-permute-start | bytes 786440 | tf_op jit(solution)/shard_map/ppermute | solution.py:380
  29.4 1.9 %collective-permute-done.4.refs_8_ = bf16[16,8192]{1,0:T(8,128)(2,1)S(1)} collective-permute-done((bf16[16,8192]{1,0:T(8,128)(2,1)S(1)}, bf16[16,8192]{1,0:T(8,128)(2,1)S(1)}, u32[]{:S(2)}, u32[]{:S(2)}) %collective-permute-start.4) | collective-permute-done | bytes 262176 | tf_op jit(solution)/shard_map/ppermute | solution.py:380
  31.3 3.7 %collective-permute-start.5 = (bf16[16,8192]{1,0:T(8,128)(2,1)S(1)}, bf16[16,8192]{1,0:T(8,128)(2,1)S(1)}, u32[]{:S(2)}, u32[]{:S(2)}) collective-permute-start(bf16[16,8192]{1,0:T(8,128)(2,1)S(1)} %collective-permute-done.4.refs_8_), channel_id=1, source_target_pairs={{0,7},{1,0},{2,1},{3,2},{4,3},{5,4},{6,5},{7,6},{8,15},{9,8},{10,9... | collective-permute-start | bytes 786440 | tf_op jit(solution)/shard_map/ppermute | solution.py:380
  35.0 1.9 %collective-permute-done.8.refs_10_ = bf16[16,8192]{1,0:T(8,128)(2,1)} collective-permute-done((bf16[16,8192]{1,0:T(8,128)(2,1)S(1)}, bf16[16,8192]{1,0:T(8,128)(2,1)}, u32[]{:S(2)}, u32[]{:S(2)}) %collective-permute-start.8) | collective-permute-done | bytes 262176 | tf_op jit(solution)/shard_map/ppermute | solution.py:380
  36.9 3.8 %collective-permute-start.13 = (bf16[16,8192]{1,0:T(8,128)(2,1)}, bf16[16,8192]{1,0:T(8,128)(2,1)S(1)}, u32[]{:S(2)}, u32[]{:S(2)}) collective-permute-start(bf16[16,8192]{1,0:T(8,128)(2,1)} %collective-permute-done.12.refs_11_), channel_id=1, source_target_pairs={{0,7},{1,0},{2,1},{3,2},{4,3},{5,4},{6,5},{7,6},{8,15},{9,8},{10,9... | collective-permute-start | bytes 786440 | tf_op jit(solution)/shard_map/ppermute | solution.py:380
  41.4 6.8 %shard_map.101 = (bf16[192,256]{1,0:T(8,128)(2,1)}, bf16[256,4096]{1,0:T(8,128)(2,1)}, bf16[256,4096]{1,0:T(8,128)(2,1)}) custom-call(s32[4]{0:T(128)} %pad_add_fusion.place_ref, bf16[16,8192]{1,0:T(8,128)(2,1)} %copy-done.9, bf16[16,8192]{1,0:T(8,128)(2,1)} %copy-done.10, bf16[16,8192]{1,0:T(8,128)(2,1)} %copy-done.15, bf16[16,8192]{1,0:T(8,128)(2,1)} %copy-done.18, ...), custom_call_target="tpu_custom_call" | custom-call | flops 805306368 | bytes 8388608 | tf_op jit(solution)/shard_map/pallas_call | solution.py:228
  49.3 6.7 %shard_map.102 = (bf16[272,256]{1,0:T(8,128)(2,1)}, bf16[256,4096]{1,0:T(8,128)(2,1)}, bf16[256,4096]{1,0:T(8,128)(2,1)}) custom-call(s32[4]{0:T(128)} %pad_add_fusion.place_ref, bf16[16,8192]{1,0:T(8,128)(2,1)} %copy-done.12, bf16[16,8192]{1,0:T(8,128)(2,1)} %copy-done.11, ...), custom_call_target="tpu_custom_call", output_to_operand_aliasing={{1}: (9, {}), {2}: (10, {})} | custom-call | flops 268435456 | bytes 8388608 | tf_op jit(solution)/shard_map/pallas_call | solution.py:228
  56.1 5.1 %collective-permute-start.15 = (bf16[272,256]{1,0:T(8,128)(2,1)}, bf16[272,256]{1,0:T(8,128)(2,1)S(1)}, u32[]{:S(2)}, u32[]{:S(2)}) collective-permute-start(bf16[272,256]{1,0:T(8,128)(2,1)} %get-tuple-element.51.kv0), channel_id=1, source_target_pairs={{0,32},{16,48},{1,33},{17,49},{2,34},{18,50},{3,35},{19,51},{4,36}... | collective-permute-start | bytes 417800 | tf_op jit(solution)/shard_map/ppermute | solution.py:399
  61.2 2.6 %collective-permute-start.14 = (bf16[272,256]{1,0:T(8,128)(2,1)}, bf16[272,256]{1,0:T(8,128)(2,1)S(1)}, u32[]{:S(2)}, u32[]{:S(2)}) collective-permute-start(bf16[272,256]{1,0:T(8,128)(2,1)} %get-tuple-element.51.kv0), channel_id=1, source_target_pairs={{0,16},{16,32},{32,48},{1,17},{17,33},{33,49},{2,18},{18,34},{34,5... | collective-permute-start | bytes 417800 | tf_op jit(solution)/shard_map/ppermute | solution.py:398
  63.8 1.8 %collective-permute-start.17 = (bf16[272,256]{1,0:T(8,128)(2,1)}, bf16[272,256]{1,0:T(8,128)(2,1)S(1)}, u32[]{:S(2)}, u32[]{:S(2)}) collective-permute-start(bf16[272,256]{1,0:T(8,128)(2,1)} %get-tuple-element.51.kv0), channel_id=1, source_target_pairs={{0,8},{1,9},{2,10},{3,11},{4,12},{5,13},{6,14},{7,15},{16,24},{17,... | collective-permute-start | bytes 417800 | tf_op jit(solution)/shard_map/ppermute | solution.py:400
  65.6 1.3 collective-permute-start.18
  66.9 1.1 collective-permute-done.14.kv1
  70.3 13.2 %shard_map.103 = (bf16[256,1024]{1,0:T(8,128)(2,1)}, bf16[256,1024]{1,0:T(8,128)(2,1)}, f32[256,256]{1,0:T(8,128)S(1)}, f32[256,256]{1,0:T(8,128)S(1)}, f32[256,256]{1,0:T(8,128)S(1)}, /*index=5*/f32[2,256,256]{2,1,0:T(8,128)}) custom-call(s32[4]{0:T(128)S(1)} %copy-done.5, bf16[272,256]{1,0:T(8,128)(2,1)S(1)} %copy-done.8, ...), custom_call_target="tpu_custom_call" | custom-call | flops 4026531840 | bytes 6291456 | tf_op jit(solution)/shard_map/pallas_call | solution.py:115
  83.7 2.1 %collective-permute-done.19 = f32[2,256,256]{2,1,0:T(8,128)} collective-permute-done((f32[2,256,256]{2,1,0:T(8,128)}, f32[2,256,256]{2,1,0:T(8,128)}, u32[]{:S(2)}, u32[]{:S(2)}) %collective-permute-start.19) | collective-permute-done | bytes 524320 | tf_op jit(solution)/shard_map/ppermute | solution.py:376
  85.8 1.1 fusion.3
  86.9 1.3 collective-permute-start.20
  88.2 1.3 collective-permute-start.21
  89.5 5.5 %collective-permute-done.20 = bf16[256,256]{1,0:T(8,128)(2,1)S(1)} collective-permute-done((bf16[256,256]{1,0:T(8,128)(2,1)S(1)}, bf16[256,256]{1,0:T(8,128)(2,1)S(1)}, u32[]{:S(2)}, u32[]{:S(2)}) %collective-permute-start.20) | collective-permute-done | bytes 131104 | tf_op jit(solution)/shard_map/ppermute | solution.py:414
  95.0 3.1 %collective-permute-done.21 = bf16[256,256]{1,0:T(8,128)(2,1)S(1)} collective-permute-done((bf16[256,256]{1,0:T(8,128)(2,1)S(1)}, bf16[256,256]{1,0:T(8,128)(2,1)S(1)}, u32[]{:S(2)}, u32[]{:S(2)}) %collective-permute-start.21) | collective-permute-done | bytes 131104 | tf_op jit(solution)/shard_map/ppermute | solution.py:415
  99.1 1.6 copy-done.2
  100.7 4.7 %shard_map.104 = (bf16[16,8192]{1,0:T(8,128)(2,1)S(1)}, bf16[16,8192]{1,0:T(8,128)(2,1)}, bf16[16,8192]{1,0:T(8,128)(2,1)}, bf16[16,8192]{1,0:T(8,128)(2,1)}, bf...) custom-call(s32[4]{0:T(128)S(1)} %copy-done.5, ...), custom_call_target="tpu_custom_call" | custom-call | flops 536870912 | bytes 6291456 | tf_op jit(solution)/shard_map/pallas_call | solution.py:347
  105.4 2.1 %collective-permute-start.34 = (bf16[16,8192]{1,0:T(8,128)(2,1)}, bf16[16,8192]{1,0:T(8,128)(2,1)}, u32[]{:S(2)}, u32[]{:S(2)}) collective-permute-start(bf16[16,8192]{1,0:T(8,128)(2,1)} %get-tuple-element.62), channel_id=1, source_target_pairs={{0,7},{1,0},{2,1},{3,2},{4,3},{5,4},{6,5},{7,6},{8,15},{9,8},{10,9... | collective-permute-start | bytes 786440 | tf_op jit(solution)/shard_map/ppermute | solution.py:380
  107.6 1.3 collective-permute-done.22.gs_ref
  108.9 1.9 %collective-permute-start.28 = (bf16[16,8192]{1,0:T(8,128)(2,1)}, bf16[16,8192]{1,0:T(8,128)(2,1)}, u32[]{:S(2)}, u32[]{:S(2)}) collective-permute-start(bf16[16,8192]{1,0:T(8,128)(2,1)} %get-tuple-element.63), channel_id=1, source_target_pairs={{0,7},{1,0},{2,1},{3,2},{4,3},{5,4},{6,5},{7,6},{8,15},{9,8},{10,9... | collective-permute-start | bytes 786440 | tf_op jit(solution)/shard_map/ppermute | solution.py:380
  110.8 4.6 %shard_map.105 = bf16[16,256,256]{2,1,0:T(8,128)(2,1)S(1)} custom-call(s32[4]{0:T(128)S(1)} %copy-done.5, bf16[256,256]{1,0:T(8,128)(2,1)S(1)} %fusion.7.g_ref, bf16[256,256]{1,0:T(8,128)(2,1)S(1)} %collective-permute-done.22.gs_ref, bf16[256,4096]{1,0:T(8,128)(2,1)S(1)} %copy-done, bf16[256,4096]{1,0:T(8,128)(2,1)S(1)} %copy-done, ...), custom_call_target="tpu_custom_call" | custom-call | flops 1073741824 | bytes 6291456 | tf_op jit(solution)/shard_map/pallas_call | solution.py:283
  115.5 1.3 copy-done.4
  116.8 6.7 %all-to-all-start = ((bf16[16,256,256]{2,1,0:T(8,128)(2,1)}), bf16[16,256,256]{2,1,0:T(8,128)(2,1)}, u32[]{:S(2)}, u32[]{:S(2)}) async-start(bf16[16,256,256]{2,1,0:T(8,128)(2,1)} %copy-done.4), calls=%async_computation | async-start | bytes 4194304 | tf_op jit(solution)/shard_map/all_to_all | solution.py:424
  123.5 1.2 add_convert_fusion.4
  127.9 3.2 %collective-permute-start.29 = (bf16[16,8192]{1,0:T(8,128)(2,1)S(1)}, bf16[16,8192]{1,0:T(8,128)(2,1)S(1)}, u32[]{:S(2)}, u32[]{:S(2)}) collective-permute-start(bf16[16,8192]{1,0:T(8,128)(2,1)S(1)} %add_convert_fusion.8), channel_id=1, source_target_pairs={{0,7},{1,0},{2,1},{3,2},{4,3},{5,4},{6,5},{7,6},{8,15},{9,8},{10,9... | collective-permute-start | bytes 786440 | tf_op jit(solution)/shard_map/ppermute | solution.py:380
  131.1 3.2 %collective-permute-start.35 = (bf16[16,8192]{1,0:T(8,128)(2,1)S(1)}, bf16[16,8192]{1,0:T(8,128)(2,1)S(1)}, u32[]{:S(2)}, u32[]{:S(2)}) collective-permute-start(bf16[16,8192]{1,0:T(8,128)(2,1)S(1)} %add_convert_fusion.4), channel_id=1, source_target_pairs={{0,7},{1,0},{2,1},{3,2},{4,3},{5,4},{6,5},{7,6},{8,15},{9,8},{10,9... | collective-permute-start | bytes 786440 | tf_op jit(solution)/shard_map/ppermute | solution.py:380
  134.3 3.5 %shard_map.106 = (bf16[16,8192]{1,0:T(8,128)(2,1)S(1)}, bf16[16,8192]{1,0:T(8,128)(2,1)S(1)}, bf16[16,8192]{1,0:T(8,128)(2,1)S(1)}, bf16[16,8192]{1,0:T(8,128)(2...) custom-call(s32[4]{0:T(128)S(1)} %copy-done.5, ...), custom_call_target="tpu_custom_call" | custom-call | flops 536870912 | bytes 6291456 | tf_op jit(solution)/shard_map/pallas_call | solution.py:347
  138.1 3.6 %collective-permute-start.30 = (bf16[16,8192]{1,0:T(8,128)(2,1)S(1)}, bf16[16,8192]{1,0:T(8,128)(2,1)S(1)}, u32[]{:S(2)}, u32[]{:S(2)}) collective-permute-start(bf16[16,8192]{1,0:T(8,128)(2,1)S(1)} %add_convert_fusion.7), channel_id=1, source_target_pairs={{0,7},{1,0},{2,1},{3,2},{4,3},{5,4},{6,5},{7,6},{8,15},{9,8},{10,9... | collective-permute-start | bytes 786440 | tf_op jit(solution)/shard_map/ppermute | solution.py:380
  142.4 1.1 collective-permute-done.35
  143.5 3.8 %collective-permute-start.36 = (bf16[16,8192]{1,0:T(8,128)(2,1)S(1)}, bf16[16,8192]{1,0:T(8,128)(2,1)S(1)}, u32[]{:S(2)}, u32[]{:S(2)}) collective-permute-start(bf16[16,8192]{1,0:T(8,128)(2,1)S(1)} %add_convert_fusion.3), channel_id=1, source_target_pairs={{0,7},{1,0},{2,1},{3,2},{4,3},{5,4},{6,5},{7,6},{8,15},{9,8},{10,9... | collective-permute-start | bytes 786440 | tf_op jit(solution)/shard_map/ppermute | solution.py:380
  147.3 1.2 collective-permute-done.26
  148.6 4.3 %collective-permute-done.36 = bf16[16,8192]{1,0:T(8,128)(2,1)S(1)} collective-permute-done((bf16[16,8192]{1,0:T(8,128)(2,1)S(1)}, bf16[16,8192]{1,0:T(8,128)(2,1)S(1)}, u32[]{:S(2)}, u32[]{:S(2)}) %collective-permute-start.36) | collective-permute-done | bytes 262176 | tf_op jit(solution)/shard_map/ppermute | solution.py:380
  153.0 3.6 %collective-permute-start.37 = (bf16[16,8192]{1,0:T(8,128)(2,1)S(1)}, bf16[16,8192]{1,0:T(8,128)(2,1)S(1)}, u32[]{:S(2)}, u32[]{:S(2)}) collective-permute-start(bf16[16,8192]{1,0:T(8,128)(2,1)S(1)} %add_convert_fusion.2), channel_id=1, source_target_pairs={{0,7},{1,0},{2,1},{3,2},{4,3},{5,4},{6,5},{7,6},{8,15},{9,8},{10,9... | collective-permute-start | bytes 786440 | tf_op jit(solution)/shard_map/ppermute | solution.py:380
  156.6 2.6 %shard_map.107 = (f32[256,128]{1,0:T(8,128)}, f32[256,128]{1,0:T(8,128)}) custom-call(bf16[16,256,256]{2,1,0:T(8,128)(2,1)} %all-to-all-done.parts), custom_call_target="tpu_custom_call" | custom-call | tf_op jit(solution)/shard_map/pallas_call | solution.py:312
  159.2 1.3 collective-permute-done.37
  (97 shorter events, 11.3 us)
Async XLA Ops:
  1.7 39.7 %copy-start.9 = (bf16[16,8192]{1,0:T(8,128)(2,1)}, bf16[16,8192]{1,0:T(8,128)(2,1)S(1)}, u32[]{:S(2)}) copy-start(bf16[16,8192]{1,0:T(8,128)(2,1)S(1)} %get-tuple-element.93.refs_0_) | copy-start | bytes 786436
  1.7 39.7 %copy-start.10 = (bf16[16,8192]{1,0:T(8,128)(2,1)}, bf16[16,8192]{1,0:T(8,128)(2,1)S(1)}, u32[]{:S(2)}) copy-start(bf16[16,8192]{1,0:T(8,128)(2,1)S(1)} %get-tuple-element.94.refs_1_) | copy-start | bytes 786436
  1.7 13.1 %collective-permute-start.6 = (bf16[16,8192]{1,0:T(8,128)(2,1)S(1)}, bf16[16,8192]{1,0:T(8,128)(2,1)S(1)}, u32[]{:S(2)}, u32[]{:S(2)}) collective-permute-start(bf16[16,8192]{1,0:T(8,128)(2,1)S(1)} %get-tuple-element.93.refs_0_), channel_id=1, source_target_pairs={{0,1},{1,2},{2,3},{3,4},{4,5},{5,6},{6,7},{7,0},{8,9},{9,10},{10,1... | collective-permute-start | bytes 786440 | tf_op jit(solution)/shard_map/ppermute | solution.py:380
  3.7 11.1 %collective-permute-start.10 = (bf16[16,8192]{1,0:T(8,128)(2,1)S(1)}, bf16[16,8192]{1,0:T(8,128)(2,1)S(1)}, u32[]{:S(2)}, u32[]{:S(2)}) collective-permute-start(bf16[16,8192]{1,0:T(8,128)(2,1)S(1)} %get-tuple-element.94.refs_1_), channel_id=1, source_target_pairs={{0,7},{1,0},{2,1},{3,2},{4,3},{5,4},{6,5},{7,6},{8,15},{9,8},{10,9... | collective-permute-start | bytes 786440 | tf_op jit(solution)/shard_map/ppermute | solution.py:380
  7.7 12.3 %collective-permute-start.3 = (bf16[16,8192]{1,0:T(8,128)(2,1)S(1)}, bf16[16,8192]{1,0:T(8,128)(2,1)S(1)}, u32[]{:S(2)}, u32[]{:S(2)}) collective-permute-start(bf16[16,8192]{1,0:T(8,128)(2,1)S(1)} %get-tuple-element.93.refs_0_), channel_id=1, source_target_pairs={{0,7},{1,0},{2,1},{3,2},{4,3},{5,4},{6,5},{7,6},{8,15},{9,8},{10,9... | collective-permute-start | bytes 786440 | tf_op jit(solution)/shard_map/ppermute | solution.py:380
  9.7 14.1 %collective-permute-start = (bf16[16,8192]{1,0:T(8,128)(2,1)S(1)}, bf16[16,8192]{1,0:T(8,128)(2,1)S(1)}, u32[]{:S(2)}, u32[]{:S(2)}) collective-permute-start(bf16[16,8192]{1,0:T(8,128)(2,1)S(1)} %get-tuple-element.94.refs_1_), channel_id=1, source_target_pairs={{0,1},{1,2},{2,3},{3,4},{4,5},{5,6},{6,7},{7,0},{8,9},{9,10},{10,1... | collective-permute-start | bytes 786440 | tf_op jit(solution)/shard_map/ppermute | solution.py:380
  14.8 26.6 %copy-start.15 = (bf16[16,8192]{1,0:T(8,128)(2,1)}, bf16[16,8192]{1,0:T(8,128)(2,1)S(1)}, u32[]{:S(2)}) copy-start(bf16[16,8192]{1,0:T(8,128)(2,1)S(1)} %collective-permute-done.6.refs_2_) | copy-start | bytes 786436
  14.8 10.4 %collective-permute-start.7 = (bf16[16,8192]{1,0:T(8,128)(2,1)S(1)}, bf16[16,8192]{1,0:T(8,128)(2,1)S(1)}, u32[]{:S(2)}, u32[]{:S(2)}) collective-permute-start(bf16[16,8192]{1,0:T(8,128)(2,1)S(1)} %collective-permute-done.6.refs_2_), channel_id=1, source_target_pairs={{0,1},{1,2},{2,3},{3,4},{4,5},{5,6},{6,7},{7,0},{8,9},{9,10},{10,1... | collective-permute-start | bytes 786440 | tf_op jit(solution)/shard_map/ppermute | solution.py:380
  14.8 26.6 %copy-start.16 = (bf16[16,8192]{1,0:T(8,128)(2,1)}, bf16[16,8192]{1,0:T(8,128)(2,1)S(1)}, u32[]{:S(2)}) copy-start(bf16[16,8192]{1,0:T(8,128)(2,1)S(1)} %collective-permute-done.10.refs_5_) | copy-start | bytes 786436
  14.8 10.9 %collective-permute-start.11 = (bf16[16,8192]{1,0:T(8,128)(2,1)S(1)}, bf16[16,8192]{1,0:T(8,128)(2,1)S(1)}, u32[]{:S(2)}, u32[]{:S(2)}) collective-permute-start(bf16[16,8192]{1,0:T(8,128)(2,1)S(1)} %collective-permute-done.10.refs_5_), channel_id=1, source_target_pairs={{0,7},{1,0},{2,1},{3,2},{4,3},{5,4},{6,5},{7,6},{8,15},{9,8},{10,9... | collective-permute-start | bytes 786440 | tf_op jit(solution)/shard_map/ppermute | solution.py:380
  20.1 21.3 %copy-start.17 = (bf16[16,8192]{1,0:T(8,128)(2,1)}, bf16[16,8192]{1,0:T(8,128)(2,1)S(1)}, u32[]{:S(2)}) copy-start(bf16[16,8192]{1,0:T(8,128)(2,1)S(1)} %collective-permute-done.3.refs_4_) | copy-start | bytes 786436
  20.1 11.2 %collective-permute-start.4 = (bf16[16,8192]{1,0:T(8,128)(2,1)S(1)}, bf16[16,8192]{1,0:T(8,128)(2,1)S(1)}, u32[]{:S(2)}, u32[]{:S(2)}) collective-permute-start(bf16[16,8192]{1,0:T(8,128)(2,1)S(1)} %collective-permute-done.3.refs_4_), channel_id=1, source_target_pairs={{0,7},{1,0},{2,1},{3,2},{4,3},{5,4},{6,5},{7,6},{8,15},{9,8},{10,9... | collective-permute-start | bytes 786440 | tf_op jit(solution)/shard_map/ppermute | solution.py:380
  23.8 17.6 %copy-start.18 = (bf16[16,8192]{1,0:T(8,128)(2,1)}, bf16[16,8192]{1,0:T(8,128)(2,1)S(1)}, u32[]{:S(2)}) copy-start(bf16[16,8192]{1,0:T(8,128)(2,1)S(1)} %collective-permute-done.refs_3_) | copy-start | bytes 786436
  23.8 11.2 %collective-permute-start.1 = (bf16[16,8192]{1,0:T(8,128)(2,1)S(1)}, bf16[16,8192]{1,0:T(8,128)(2,1)}, u32[]{:S(2)}, u32[]{:S(2)}) collective-permute-start(bf16[16,8192]{1,0:T(8,128)(2,1)S(1)} %collective-permute-done.refs_3_), channel_id=1, source_target_pairs={{0,1},{1,2},{2,3},{3,4},{4,5},{5,6},{6,7},{7,0},{8,9},{9,10},{10,1... | collective-permute-start | bytes 786440 | tf_op jit(solution)/shard_map/ppermute | solution.py:380
  25.2 11.7 %collective-permute-start.8 = (bf16[16,8192]{1,0:T(8,128)(2,1)S(1)}, bf16[16,8192]{1,0:T(8,128)(2,1)}, u32[]{:S(2)}, u32[]{:S(2)}) collective-permute-start(bf16[16,8192]{1,0:T(8,128)(2,1)S(1)} %collective-permute-done.7.refs_6_), channel_id=1, source_target_pairs={{0,1},{1,2},{2,3},{3,4},{4,5},{5,6},{6,7},{7,0},{8,9},{9,10},{10,1... | collective-permute-start | bytes 786440 | tf_op jit(solution)/shard_map/ppermute | solution.py:380
  25.7 11.2 %collective-permute-start.12 = (bf16[16,8192]{1,0:T(8,128)(2,1)S(1)}, bf16[16,8192]{1,0:T(8,128)(2,1)}, u32[]{:S(2)}, u32[]{:S(2)}) collective-permute-start(bf16[16,8192]{1,0:T(8,128)(2,1)S(1)} %collective-permute-done.11.refs_9_), channel_id=1, source_target_pairs={{0,7},{1,0},{2,1},{3,2},{4,3},{5,4},{6,5},{7,6},{8,15},{9,8},{10,9... | collective-permute-start | bytes 786440 | tf_op jit(solution)/shard_map/ppermute | solution.py:380
  31.3 17.0 %collective-permute-start.5 = (bf16[16,8192]{1,0:T(8,128)(2,1)S(1)}, bf16[16,8192]{1,0:T(8,128)(2,1)S(1)}, u32[]{:S(2)}, u32[]{:S(2)}) collective-permute-start(bf16[16,8192]{1,0:T(8,128)(2,1)S(1)} %collective-permute-done.4.refs_8_), channel_id=1, source_target_pairs={{0,7},{1,0},{2,1},{3,2},{4,3},{5,4},{6,5},{7,6},{8,15},{9,8},{10,9... | collective-permute-start | bytes 786440 | tf_op jit(solution)/shard_map/ppermute | solution.py:380
  35.0 13.3 %collective-permute-start.2 = (bf16[16,8192]{1,0:T(8,128)(2,1)}, bf16[16,8192]{1,0:T(8,128)(2,1)S(1)}, u32[]{:S(2)}, u32[]{:S(2)}) collective-permute-start(bf16[16,8192]{1,0:T(8,128)(2,1)} %collective-permute-done.1.refs_7_), channel_id=1, source_target_pairs={{0,1},{1,2},{2,3},{3,4},{4,5},{5,6},{6,7},{7,0},{8,9},{9,10},{10,1... | collective-permute-start | bytes 786440 | tf_op jit(solution)/shard_map/ppermute | solution.py:380
  36.9 11.4 %collective-permute-start.9 = (bf16[16,8192]{1,0:T(8,128)(2,1)}, bf16[16,8192]{1,0:T(8,128)(2,1)S(1)}, u32[]{:S(2)}, u32[]{:S(2)}) collective-permute-start(bf16[16,8192]{1,0:T(8,128)(2,1)} %collective-permute-done.8.refs_10_), channel_id=1, source_target_pairs={{0,1},{1,2},{2,3},{3,4},{4,5},{5,6},{6,7},{7,0},{8,9},{9,10},{10,1... | collective-permute-start | bytes 786440 | tf_op jit(solution)/shard_map/ppermute | solution.py:380
  36.9 11.4 %collective-permute-start.13 = (bf16[16,8192]{1,0:T(8,128)(2,1)}, bf16[16,8192]{1,0:T(8,128)(2,1)S(1)}, u32[]{:S(2)}, u32[]{:S(2)}) collective-permute-start(bf16[16,8192]{1,0:T(8,128)(2,1)} %collective-permute-done.12.refs_11_), channel_id=1, source_target_pairs={{0,7},{1,0},{2,1},{3,2},{4,3},{5,4},{6,5},{7,6},{8,15},{9,8},{10,9... | collective-permute-start | bytes 786440 | tf_op jit(solution)/shard_map/ppermute | solution.py:380
  49.3 20.1 %copy-start.5 = (s32[4]{0:T(128)S(1)}, s32[4]{0:T(128)}, u32[]{:S(2)}) copy-start(s32[4]{0:T(128)} %pad_add_fusion.place_ref) | copy-start | bytes 52
  49.3 20.1 %copy-start.6 = (bf16[1,256,1024]{2,1,0:T(8,128)(2,1)S(1)}, bf16[1,256,1024]{2,1,0:T(8,128)(2,1)}, u32[]{:S(2)}) copy-start(bf16[1,256,1024]{2,1,0:T(8,128)(2,1)} %param.9) | copy-start | bytes 1572868
  49.3 20.1 %copy-start.7 = (bf16[1,256,1024]{2,1,0:T(8,128)(2,1)S(1)}, bf16[1,256,1024]{2,1,0:T(8,128)(2,1)}, u32[]{:S(2)}) copy-start(bf16[1,256,1024]{2,1,0:T(8,128)(2,1)} %param.10) | copy-start | bytes 1572868
  56.0 54.9 %collective-permute-start.23 = (bf16[256,4096]{1,0:T(8,128)(2,1)}, bf16[256,4096]{1,0:T(8,128)(2,1)}, u32[]{:S(2)}, u32[]{:S(2)}) collective-permute-start(bf16[256,4096]{1,0:T(8,128)(2,1)} %get-tuple-element.68), channel_id=1, source_target_pairs={{0,8},{8,0},{1,9},{9,1},{2,10},{10,2},{3,11},{11,3},{4,12},{12,4},... | collective-permute-start | bytes 6291464 | tf_op jit(solution)/shard_map/ppermute | solution.py:376
  56.1 9.6 %collective-permute-start.15 = (bf16[272,256]{1,0:T(8,128)(2,1)}, bf16[272,256]{1,0:T(8,128)(2,1)S(1)}, u32[]{:S(2)}, u32[]{:S(2)}) collective-permute-start(bf16[272,256]{1,0:T(8,128)(2,1)} %get-tuple-element.51.kv0), channel_id=1, source_target_pairs={{0,32},{16,48},{1,33},{17,49},{2,34},{18,50},{3,35},{19,51},{4,36}... | collective-permute-start | bytes 417800 | tf_op jit(solution)/shard_map/ppermute | solution.py:399
  61.2 6.9 %collective-permute-start.14 = (bf16[272,256]{1,0:T(8,128)(2,1)}, bf16[272,256]{1,0:T(8,128)(2,1)S(1)}, u32[]{:S(2)}, u32[]{:S(2)}) collective-permute-start(bf16[272,256]{1,0:T(8,128)(2,1)} %get-tuple-element.51.kv0), channel_id=1, source_target_pairs={{0,16},{16,32},{32,48},{1,17},{17,33},{33,49},{2,18},{18,34},{34,5... | collective-permute-start | bytes 417800 | tf_op jit(solution)/shard_map/ppermute | solution.py:398
  63.8 4.4 %collective-permute-start.17 = (bf16[272,256]{1,0:T(8,128)(2,1)}, bf16[272,256]{1,0:T(8,128)(2,1)S(1)}, u32[]{:S(2)}, u32[]{:S(2)}) collective-permute-start(bf16[272,256]{1,0:T(8,128)(2,1)} %get-tuple-element.51.kv0), channel_id=1, source_target_pairs={{0,8},{1,9},{2,10},{3,11},{4,12},{5,13},{6,14},{7,15},{16,24},{17,... | collective-permute-start | bytes 417800 | tf_op jit(solution)/shard_map/ppermute | solution.py:400
  65.6 3.3 %collective-permute-start.18 = (bf16[272,256]{1,0:T(8,128)(2,1)S(1)}, bf16[272,256]{1,0:T(8,128)(2,1)S(1)}, u32[]{:S(2)}, u32[]{:S(2)}) collective-permute-start(bf16[272,256]{1,0:T(8,128)(2,1)S(1)} %collective-permute-done.15.kv2), channel_id=1, source_target_pairs={{8,0},{9,1},{10,2},{11,3},{12,4},{13,5},{14,6},{15,7},{24,16},{25,... | collective-permute-start | bytes 417800 | tf_op jit(solution)/shard_map/ppermute | solution.py:402
  68.0 1.4 collective-permute-start.16
  83.5 2.3 %collective-permute-start.19 = (f32[2,256,256]{2,1,0:T(8,128)}, f32[2,256,256]{2,1,0:T(8,128)}, u32[]{:S(2)}, u32[]{:S(2)}) collective-permute-start(f32[2,256,256]{2,1,0:T(8,128)} %get-tuple-element.55), channel_id=1, source_target_pairs={{0,8},{8,0},{1,9},{9,1},{2,10},{10,2},{3,11},{11,3},{4,12},{12,4},... | collective-permute-start | bytes 1572872 | tf_op jit(solution)/shard_map/ppermute | solution.py:376
  86.9 8.1 %collective-permute-start.20 = (bf16[256,256]{1,0:T(8,128)(2,1)S(1)}, bf16[256,256]{1,0:T(8,128)(2,1)S(1)}, u32[]{:S(2)}, u32[]{:S(2)}) collective-permute-start(bf16[256,256]{1,0:T(8,128)(2,1)S(1)} %get-tuple-element.91), channel_id=1, source_target_pairs={{16,0},{32,16},{48,32},{17,1},{33,17},{49,33},{18,2},{34,18},{50,3... | collective-permute-start | bytes 393224 | tf_op jit(solution)/shard_map/ppermute | solution.py:414
  88.2 9.9 %collective-permute-start.21 = (bf16[256,256]{1,0:T(8,128)(2,1)S(1)}, bf16[256,256]{1,0:T(8,128)(2,1)S(1)}, u32[]{:S(2)}, u32[]{:S(2)}) collective-permute-start(bf16[256,256]{1,0:T(8,128)(2,1)S(1)} %get-tuple-element.92), channel_id=1, source_target_pairs={{32,0},{48,16},{33,1},{49,17},{34,2},{50,18},{35,3},{51,19},{36,4}... | collective-permute-start | bytes 393224 | tf_op jit(solution)/shard_map/ppermute | solution.py:415
  105.4 18.0 %collective-permute-start.34 = (bf16[16,8192]{1,0:T(8,128)(2,1)}, bf16[16,8192]{1,0:T(8,128)(2,1)}, u32[]{:S(2)}, u32[]{:S(2)}) collective-permute-start(bf16[16,8192]{1,0:T(8,128)(2,1)} %get-tuple-element.62), channel_id=1, source_target_pairs={{0,7},{1,0},{2,1},{3,2},{4,3},{5,4},{6,5},{7,6},{8,15},{9,8},{10,9... | collective-permute-start | bytes 786440 | tf_op jit(solution)/shard_map/ppermute | solution.py:380
  107.6 1.3 collective-permute-start.22
  107.6 17.1 %collective-permute-start.31 = (bf16[16,8192]{1,0:T(8,128)(2,1)}, bf16[16,8192]{1,0:T(8,128)(2,1)}, u32[]{:S(2)}, u32[]{:S(2)}) collective-permute-start(bf16[16,8192]{1,0:T(8,128)(2,1)} %get-tuple-element.60), channel_id=1, source_target_pairs={{0,1},{1,2},{2,3},{3,4},{4,5},{5,6},{6,7},{7,0},{8,9},{9,10},{10,1... | collective-permute-start | bytes 786440 | tf_op jit(solution)/shard_map/ppermute | solution.py:380
  107.6 18.1 %collective-permute-start.24 = (bf16[16,8192]{1,0:T(8,128)(2,1)S(1)}, bf16[16,8192]{1,0:T(8,128)(2,1)}, u32[]{:S(2)}, u32[]{:S(2)}) collective-permute-start(bf16[16,8192]{1,0:T(8,128)(2,1)S(1)} %get-tuple-element.61), channel_id=1, source_target_pairs={{0,1},{1,2},{2,3},{3,4},{4,5},{5,6},{6,7},{7,0},{8,9},{9,10},{10,1... | collective-permute-start | bytes 786440 | tf_op jit(solution)/shard_map/ppermute | solution.py:380
  108.9 16.7 %collective-permute-start.28 = (bf16[16,8192]{1,0:T(8,128)(2,1)}, bf16[16,8192]{1,0:T(8,128)(2,1)}, u32[]{:S(2)}, u32[]{:S(2)}) collective-permute-start(bf16[16,8192]{1,0:T(8,128)(2,1)} %get-tuple-element.63), channel_id=1, source_target_pairs={{0,7},{1,0},{2,1},{3,2},{4,3},{5,4},{6,5},{7,6},{8,15},{9,8},{10,9... | collective-permute-start | bytes 786440 | tf_op jit(solution)/shard_map/ppermute | solution.py:380
  116.8 39.8 %all-to-all-start = ((bf16[16,256,256]{2,1,0:T(8,128)(2,1)}), bf16[16,256,256]{2,1,0:T(8,128)(2,1)}, u32[]{:S(2)}, u32[]{:S(2)}) async-start(bf16[16,256,256]{2,1,0:T(8,128)(2,1)} %copy-done.4), calls=%async_computation | async-start | bytes 4194304 | tf_op jit(solution)/shard_map/all_to_all | solution.py:424
  126.7 11.2 %collective-permute-start.25 = (bf16[16,8192]{1,0:T(8,128)(2,1)S(1)}, bf16[16,8192]{1,0:T(8,128)(2,1)S(1)}, u32[]{:S(2)}, u32[]{:S(2)}) collective-permute-start(bf16[16,8192]{1,0:T(8,128)(2,1)S(1)} %add_convert_fusion.11), channel_id=1, source_target_pairs={{0,1},{1,2},{2,3},{3,4},{4,5},{5,6},{6,7},{7,0},{8,9},{9,10},{10,1... | collective-permute-start | bytes 786440 | tf_op jit(solution)/shard_map/ppermute | solution.py:380
  127.9 10.2 %collective-permute-start.29 = (bf16[16,8192]{1,0:T(8,128)(2,1)S(1)}, bf16[16,8192]{1,0:T(8,128)(2,1)S(1)}, u32[]{:S(2)}, u32[]{:S(2)}) collective-permute-start(bf16[16,8192]{1,0:T(8,128)(2,1)S(1)} %add_convert_fusion.8), channel_id=1, source_target_pairs={{0,7},{1,0},{2,1},{3,2},{4,3},{5,4},{6,5},{7,6},{8,15},{9,8},{10,9... | collective-permute-start | bytes 786440 | tf_op jit(solution)/shard_map/ppermute | solution.py:380
  131.1 11.1 %collective-permute-start.32 = (bf16[16,8192]{1,0:T(8,128)(2,1)S(1)}, bf16[16,8192]{1,0:T(8,128)(2,1)S(1)}, u32[]{:S(2)}, u32[]{:S(2)}) collective-permute-start(bf16[16,8192]{1,0:T(8,128)(2,1)S(1)} %add_convert_fusion.6), channel_id=1, source_target_pairs={{0,1},{1,2},{2,3},{3,4},{4,5},{5,6},{6,7},{7,0},{8,9},{9,10},{10,1... | collective-permute-start | bytes 786440 | tf_op jit(solution)/shard_map/ppermute | solution.py:380
  131.1 12.4 %collective-permute-start.35 = (bf16[16,8192]{1,0:T(8,128)(2,1)S(1)}, bf16[16,8192]{1,0:T(8,128)(2,1)S(1)}, u32[]{:S(2)}, u32[]{:S(2)}) collective-permute-start(bf16[16,8192]{1,0:T(8,128)(2,1)S(1)} %add_convert_fusion.4), channel_id=1, source_target_pairs={{0,7},{1,0},{2,1},{3,2},{4,3},{5,4},{6,5},{7,6},{8,15},{9,8},{10,9... | collective-permute-start | bytes 786440 | tf_op jit(solution)/shard_map/ppermute | solution.py:380
  137.9 10.5 %collective-permute-start.26 = (bf16[16,8192]{1,0:T(8,128)(2,1)S(1)}, bf16[16,8192]{1,0:T(8,128)(2,1)S(1)}, u32[]{:S(2)}, u32[]{:S(2)}) collective-permute-start(bf16[16,8192]{1,0:T(8,128)(2,1)S(1)} %add_convert_fusion.10), channel_id=1, source_target_pairs={{0,1},{1,2},{2,3},{3,4},{4,5},{5,6},{6,7},{7,0},{8,9},{9,10},{10,1... | collective-permute-start | bytes 786440 | tf_op jit(solution)/shard_map/ppermute | solution.py:380
  138.1 21.1 %collective-permute-start.30 = (bf16[16,8192]{1,0:T(8,128)(2,1)S(1)}, bf16[16,8192]{1,0:T(8,128)(2,1)S(1)}, u32[]{:S(2)}, u32[]{:S(2)}) collective-permute-start(bf16[16,8192]{1,0:T(8,128)(2,1)S(1)} %add_convert_fusion.7), channel_id=1, source_target_pairs={{0,7},{1,0},{2,1},{3,2},{4,3},{5,4},{6,5},{7,6},{8,15},{9,8},{10,9... | collective-permute-start | bytes 786440 | tf_op jit(solution)/shard_map/ppermute | solution.py:380
  142.3 16.9 %collective-permute-start.33 = (bf16[16,8192]{1,0:T(8,128)(2,1)S(1)}, bf16[16,8192]{1,0:T(8,128)(2,1)S(1)}, u32[]{:S(2)}, u32[]{:S(2)}) collective-permute-start(bf16[16,8192]{1,0:T(8,128)(2,1)S(1)} %add_convert_fusion.5), channel_id=1, source_target_pairs={{0,1},{1,2},{2,3},{3,4},{4,5},{5,6},{6,7},{7,0},{8,9},{9,10},{10,1... | collective-permute-start | bytes 786440 | tf_op jit(solution)/shard_map/ppermute | solution.py:380
  143.5 9.4 %collective-permute-start.36 = (bf16[16,8192]{1,0:T(8,128)(2,1)S(1)}, bf16[16,8192]{1,0:T(8,128)(2,1)S(1)}, u32[]{:S(2)}, u32[]{:S(2)}) collective-permute-start(bf16[16,8192]{1,0:T(8,128)(2,1)S(1)} %add_convert_fusion.3), channel_id=1, source_target_pairs={{0,7},{1,0},{2,1},{3,2},{4,3},{5,4},{6,5},{7,6},{8,15},{9,8},{10,9... | collective-permute-start | bytes 786440 | tf_op jit(solution)/shard_map/ppermute | solution.py:380
  148.6 10.7 %collective-permute-start.27 = (bf16[16,8192]{1,0:T(8,128)(2,1)S(1)}, bf16[16,8192]{1,0:T(8,128)(2,1)S(1)}, u32[]{:S(2)}, u32[]{:S(2)}) collective-permute-start(bf16[16,8192]{1,0:T(8,128)(2,1)S(1)} %add_convert_fusion.9), channel_id=1, source_target_pairs={{0,1},{1,2},{2,3},{3,4},{4,5},{5,6},{6,7},{7,0},{8,9},{9,10},{10,1... | collective-permute-start | bytes 786440 | tf_op jit(solution)/shard_map/ppermute | solution.py:380
  153.0 7.5 %collective-permute-start.37 = (bf16[16,8192]{1,0:T(8,128)(2,1)S(1)}, bf16[16,8192]{1,0:T(8,128)(2,1)S(1)}, u32[]{:S(2)}, u32[]{:S(2)}) collective-permute-start(bf16[16,8192]{1,0:T(8,128)(2,1)S(1)} %add_convert_fusion.2), channel_id=1, source_target_pairs={{0,7},{1,0},{2,1},{3,2},{4,3},{5,4},{6,5},{7,6},{8,15},{9,8},{10,9... | collective-permute-start | bytes 786440 | tf_op jit(solution)/shard_map/ppermute | solution.py:380
  (13 other events, 85.7 us)

commit v4 on v3

--- a/solution.py
+++ b/solution.py
@@ -156,7 +156,8 @@
 def project_kernel(order, ring, last, place_ref, *refs):
     pieces, refs = refs[:len(order)], refs[len(order):]
     if last:
-        wk_hbm, wv_hbm, seg_ref, early_ref, refs = *refs[:4], refs[6:]
+        wk_hbm, wv_hbm, seg_hbm, early_hbm, refs = *refs[:4], refs[6:]
+        *refs, seg_ref, early_ref, come_rest = refs
     else:
         wk_hbm, wv_hbm, refs = *refs[:2], refs[2:]
     kv_ref, mine_hbm, theirs_hbm, h_ref, w_ref, come, come_w, go = refs
@@ -179,7 +180,13 @@
             )
             for i, w in enumerate((wk_hbm, wv_hbm))
         ])
-    for copy in weights[0] + copies + sum(weights[1:], []):
+    rest = []
+    if last:
+        rest = [
+            pltpu.make_async_copy(seg_hbm, seg_ref, come_rest.at[0]),
+            pltpu.make_async_copy(early_hbm, early_ref, come_rest.at[1]),
+        ]
+    for copy in weights[0] + copies + sum(weights[1:], []) + rest:
         copy.start()
     for copy in copies:
         copy.wait()
@@ -201,6 +208,8 @@
         at = slice(c * depth, (c + 1) * depth)
         kv = kv + jnp.dot(h_ref[:, at], w_ref[at, :], preferred_element_type=F32)
     kv = kv.astype(BF16)
+    for copy in rest:
+        copy.wait()
     if not last:
         kv_ref[...] = kv
     else:
@@ -231,7 +240,7 @@
             num_scalar_prefetch=1,
             grid=(1,),
             in_specs=[far] * (n + 2)
-            + ([pl.BlockSpec(a.shape, whole) for a in rest[:2]] + [far, far] if rest else []),
+            + [far] * len(rest),
             out_specs=[pl.BlockSpec((kv_rows, 2 * HD), whole), far, far],
             scratch_shapes=[
                 pltpu.VMEM((rows, width), BF16),
@@ -239,7 +248,9 @@
                 pltpu.SemaphoreType.DMA((n,)),
                 pltpu.SemaphoreType.DMA((2 * steps,)),
                 pltpu.SemaphoreType.DMA((width // (2 * HD),)),
-            ],
+            ]
+            + ([pltpu.VMEM(a.shape, a.dtype) for a in rest[:2]] if rest else [])
+            + ([pltpu.SemaphoreType.DMA((2,))] if rest else []),
         ),
         out_shape=[
             jax.ShapeDtypeStruct((kv_rows, 2 * HD), BF16),
@@ -421,26 +432,29 @@
     grads, _ = lax.optimization_barrier((grads, part))
     sums = weight_grad(place, grads, other_grads, mine, other, nx, ny, heads)
     grads, sums = lax.optimization_barrier((grads, sums))
+    part.update(zip(REST, spread(place, REST, grads, *weights, heads)))
+
+    def joined(moving, s, half):
+        return (moving.astype(F32) + part[s, half].astype(F32)).astype(BF16)
+
+    routes = [
+        (0, (4, 3, 2, 1), 1), (1, (4, 5, 6, 7), -1), (1, (3, 2, 1), 1), (0, (5, 6, 7), -1)
+    ]
+    came = [shifted(part[steps[0], half], by, "tp") for half, steps, by in routes]
+    sums, *came[:2] = lax.optimization_barrier((sums, *came[:2]))
+    came[:2] = [joined(moving, steps[1], half) for moving, (half, steps, _) in zip(came, routes[:2])]
+    sums, *came[:2] = lax.optimization_barrier((sums, *came[:2]))
+    _, *came[2:] = lax.optimization_barrier((came[0], *came[2:]))
+    came[2:] = [joined(moving, steps[1], half) for moving, (half, steps, _) in zip(came[2:], routes[2:])]
     key_wgrad, value_wgrad = finish(lax.all_to_all(sums, ("dp", "y"), 0, 0, tiled=True))
-
-    part.update(zip(REST, spread(place, REST, grads, *weights, heads)))
-
-    def travel(half, steps, by):
-        moving = shifted(part[steps[0], half], by, "tp")
-        for i, s in enumerate(steps[1:]):
-            if i == 0:
-                moving, _ = lax.optimization_barrier((moving, sums))
-            moving = (moving.astype(F32) + part[s, half].astype(F32)).astype(BF16)
-            moving = shifted(moving, by, "tp")
-        return moving
-
-    came = [
-        travel(0, (4, 3, 2, 1), 1), travel(0, (5, 6, 7), -1),
-        travel(1, (3, 2, 1), 1), travel(1, (4, 5, 6, 7), -1),
-    ]
+    for i, (half, steps, by) in enumerate(routes):
+        moving = shifted(came[i], by, "tp")
+        for s in steps[2:]:
+            moving = shifted(joined(moving, s, half), by, "tp")
+        came[i] = moving
     came, key_wgrad, value_wgrad = lax.optimization_barrier((came, key_wgrad, value_wgrad))
     hidden_grad = jnp.concatenate([
-        part[0, h].astype(F32) + came[2 * h].astype(F32) + came[2 * h + 1].astype(F32)
+        part[0, h].astype(F32) + came[h].astype(F32) + came[3 - h].astype(F32)
         for h in range(2)
     ]).astype(BF16)
     return (

time: 163 us -> 158 us (0.969)
  other arithmetic: 8.36 us -> 5.35 us
  Pallas kernels: 42.1 us -> 39.8 us
    convert_element_type x10 -> x9, other arithmetic: 4.58 us -> 1.56 us  [joined(): return (moving.astype(F32) + part[s, half].astype(F32)).astype(BF16)]
  transfers between devices with their start and end apart: 39 -> 39, of which waited for: 18 -> 19; matrix products, arithmetic and copies ran while one was open for 5% -> 3% of each run, Pallas kernels for 22% -> 22%
where the time goes in v4:
time: 158 us; the launch traced here: 156 us
  starting transfers between devices  70.1 us (44%)
  Pallas kernels  39.8 us (25%)
  waiting for transfers between devices  33.9 us (21%)
  local copies, waits for them, and re-layouts  6.11 us (4%)
  other arithmetic  5.35 us (3%)
    ppermute x28, starting transfers between devices, shifted(): return lax.ppermute(a, axis, [(i, (i + s) % n) for i in range(n)])  49.4 us
    ppermute x28, waiting for transfers between devices, shifted(): return lax.ppermute(a, axis, [(i, (i + s) % n) for i in range(n)])  19.7 us
    pallas_call x1, Pallas kernels, attention(): pl.pallas_call(attention_kernel, grid_spec=pltpu.PrefetchScalarGridSpec(n...  13 us
    pallas_call x2, Pallas kernels, project(): pl.pallas_call(functools.partial(project_kernel, order, ring, bool(rest))...  12.6 us
    pallas_call x2, Pallas kernels, spread(): pl.pallas_call(functools.partial(spread_kernel, order, ring), grid_spec=p...  6.98 us
    all_to_all x1, starting transfers between devices, on_device(): lax.all_to_all(sums, ('dp', 'y'), 0, 0, tiled=True)  6.96 us
    ppermute x1, waiting for transfers between devices, on_device(): got1 = lax.ppermute(send1, 'y', up1)  5.47 us
    ppermute x1, starting transfers between devices, on_device(): kv2 = lax.ppermute(kv, 'y', down2)  5.11 us
  transfers between devices with their start and end apart: 39, of which 19 were waited for; matrix products, arithmetic and copies ran while one was open for 3% of the time, Pallas kernels for 22%

profile of v4, /device:TPU:2, one launch (start us, length us, event | category | flops | bytes accessed | tf_op | source)
XLA Modules:
  0.0 156.4 jit_solution(4395616683264777829)
XLA Ops:
  0.6 1.1 slice_bitcast_fusion.1
  1.7 2.0 %collective-permute-start.6 = (bf16[16,8192]{1,0:T(8,128)(2,1)S(1)}, bf16[16,8192]{1,0:T(8,128)(2,1)S(1)}, u32[]{:S(2)}, u32[]{:S(2)}) collective-permute-start(bf16[16,8192]{1,0:T(8,128)(2,1)S(1)} %get-tuple-element.101.refs_0_), channel_id=1, source_target_pairs={{0,1},{1,2},{2,3},{3,4},{4,5},{5,6},{6,7},{7,0},{8,9},{9,10},{10,1... | collective-permute-start | bytes 786440 | tf_op jit(solution)/shard_map/ppermute | solution.py:391
  3.7 4.0 %collective-permute-start.10 = (bf16[16,8192]{1,0:T(8,128)(2,1)S(1)}, bf16[16,8192]{1,0:T(8,128)(2,1)S(1)}, u32[]{:S(2)}, u32[]{:S(2)}) collective-permute-start(bf16[16,8192]{1,0:T(8,128)(2,1)S(1)} %get-tuple-element.102.refs_1_), channel_id=1, source_target_pairs={{0,7},{1,0},{2,1},{3,2},{4,3},{5,4},{6,5},{7,6},{8,15},{9,8},{10,9... | collective-permute-start | bytes 786440 | tf_op jit(solution)/shard_map/ppermute | solution.py:391
  7.7 1.9 %collective-permute-start.3 = (bf16[16,8192]{1,0:T(8,128)(2,1)S(1)}, bf16[16,8192]{1,0:T(8,128)(2,1)S(1)}, u32[]{:S(2)}, u32[]{:S(2)}) collective-permute-start(bf16[16,8192]{1,0:T(8,128)(2,1)S(1)} %get-tuple-element.101.refs_0_), channel_id=1, source_target_pairs={{0,7},{1,0},{2,1},{3,2},{4,3},{5,4},{6,5},{7,6},{8,15},{9,8},{10,9... | collective-permute-start | bytes 786440 | tf_op jit(solution)/shard_map/ppermute | solution.py:391
  9.8 5.0 %collective-permute-done.6.refs_2_ = bf16[16,8192]{1,0:T(8,128)(2,1)S(1)} collective-permute-done((bf16[16,8192]{1,0:T(8,128)(2,1)S(1)}, bf16[16,8192]{1,0:T(8,128)(2,1)S(1)}, u32[]{:S(2)}, u32[]{:S(2)}) %collective-permute-start.6) | collective-permute-done | bytes 262176 | tf_op jit(solution)/shard_map/ppermute | solution.py:391
  14.8 3.3 %collective-permute-start.11 = (bf16[16,8192]{1,0:T(8,128)(2,1)S(1)}, bf16[16,8192]{1,0:T(8,128)(2,1)S(1)}, u32[]{:S(2)}, u32[]{:S(2)}) collective-permute-start(bf16[16,8192]{1,0:T(8,128)(2,1)S(1)} %collective-permute-done.10.refs_5_), channel_id=1, source_target_pairs={{0,7},{1,0},{2,1},{3,2},{4,3},{5,4},{6,5},{7,6},{8,15},{9,8},{10,9... | collective-permute-start | bytes 786440 | tf_op jit(solution)/shard_map/ppermute | solution.py:391
  18.2 1.9 %collective-permute-done.3.refs_4_ = bf16[16,8192]{1,0:T(8,128)(2,1)S(1)} collective-permute-done((bf16[16,8192]{1,0:T(8,128)(2,1)S(1)}, bf16[16,8192]{1,0:T(8,128)(2,1)S(1)}, u32[]{:S(2)}, u32[]{:S(2)}) %collective-permute-start.3) | collective-permute-done | bytes 262176 | tf_op jit(solution)/shard_map/ppermute | solution.py:391
  20.1 3.7 %collective-permute-start.4 = (bf16[16,8192]{1,0:T(8,128)(2,1)S(1)}, bf16[16,8192]{1,0:T(8,128)(2,1)S(1)}, u32[]{:S(2)}, u32[]{:S(2)}) collective-permute-start(bf16[16,8192]{1,0:T(8,128)(2,1)S(1)} %collective-permute-done.3.refs_4_), channel_id=1, source_target_pairs={{0,7},{1,0},{2,1},{3,2},{4,3},{5,4},{6,5},{7,6},{8,15},{9,8},{10,9... | collective-permute-start | bytes 786440 | tf_op jit(solution)/shard_map/ppermute | solution.py:391
  23.8 1.4 collective-permute-done.7.refs_6_
  25.7 3.7 %collective-permute-start.12 = (bf16[16,8192]{1,0:T(8,128)(2,1)S(1)}, bf16[16,8192]{1,0:T(8,128)(2,1)}, u32[]{:S(2)}, u32[]{:S(2)}) collective-permute-start(bf16[16,8192]{1,0:T(8,128)(2,1)S(1)} %collective-permute-done.11.refs_9_), channel_id=1, source_target_pairs={{0,7},{1,0},{2,1},{3,2},{4,3},{5,4},{6,5},{7,6},{8,15},{9,8},{10,9... | collective-permute-start | bytes 786440 | tf_op jit(solution)/shard_map/ppermute | solution.py:391
  29.4 1.9 %collective-permute-done.4.refs_8_ = bf16[16,8192]{1,0:T(8,128)(2,1)S(1)} collective-permute-done((bf16[16,8192]{1,0:T(8,128)(2,1)S(1)}, bf16[16,8192]{1,0:T(8,128)(2,1)S(1)}, u32[]{:S(2)}, u32[]{:S(2)}) %collective-permute-start.4) | collective-permute-done | bytes 262176 | tf_op jit(solution)/shard_map/ppermute | solution.py:391
  31.3 3.7 %collective-permute-start.5 = (bf16[16,8192]{1,0:T(8,128)(2,1)S(1)}, bf16[16,8192]{1,0:T(8,128)(2,1)S(1)}, u32[]{:S(2)}, u32[]{:S(2)}) collective-permute-start(bf16[16,8192]{1,0:T(8,128)(2,1)S(1)} %collective-permute-done.4.refs_8_), channel_id=1, source_target_pairs={{0,7},{1,0},{2,1},{3,2},{4,3},{5,4},{6,5},{7,6},{8,15},{9,8},{10,9... | collective-permute-start | bytes 786440 | tf_op jit(solution)/shard_map/ppermute | solution.py:391
  35.0 1.9 %collective-permute-done.8.refs_10_ = bf16[16,8192]{1,0:T(8,128)(2,1)} collective-permute-done((bf16[16,8192]{1,0:T(8,128)(2,1)S(1)}, bf16[16,8192]{1,0:T(8,128)(2,1)}, u32[]{:S(2)}, u32[]{:S(2)}) %collective-permute-start.8) | collective-permute-done | bytes 262176 | tf_op jit(solution)/shard_map/ppermute | solution.py:391
  36.9 3.8 %collective-permute-start.13 = (bf16[16,8192]{1,0:T(8,128)(2,1)}, bf16[16,8192]{1,0:T(8,128)(2,1)S(1)}, u32[]{:S(2)}, u32[]{:S(2)}) collective-permute-start(bf16[16,8192]{1,0:T(8,128)(2,1)} %collective-permute-done.12.refs_11_), channel_id=1, source_target_pairs={{0,7},{1,0},{2,1},{3,2},{4,3},{5,4},{6,5},{7,6},{8,15},{9,8},{10,9... | collective-permute-start | bytes 786440 | tf_op jit(solution)/shard_map/ppermute | solution.py:391
  41.4 6.8 %shard_map.101 = (bf16[192,256]{1,0:T(8,128)(2,1)}, bf16[256,4096]{1,0:T(8,128)(2,1)}, bf16[256,4096]{1,0:T(8,128)(2,1)}) custom-call(s32[4]{0:T(128)} %pad_add_fusion.place_ref, bf16[16,8192]{1,0:T(8,128)(2,1)} %copy-done.9, bf16[16,8192]{1,0:T(8,128)(2,1)} %copy-done.10, bf16[16,8192]{1,0:T(8,128)(2,1)} %copy-done.15, bf16[16,8192]{1,0:T(8,128)(2,1)} %copy-done.18, ...), custom_call_target="tpu_custom_call" | custom-call | flops 805306368 | bytes 8388608 | tf_op jit(solution)/shard_map/pallas_call | solution.py:237
  49.3 5.8 %shard_map.102 = (bf16[272,256]{1,0:T(8,128)(2,1)}, bf16[256,4096]{1,0:T(8,128)(2,1)}, bf16[256,4096]{1,0:T(8,128)(2,1)}) custom-call(s32[4]{0:T(128)} %pad_add_fusion.place_ref, bf16[16,8192]{1,0:T(8,128)(2,1)} %copy-done.12, bf16[16,8192]{1,0:T(8,128)(2,1)} %copy-done.11, ...), custom_call_target="tpu_custom_call", output_to_operand_aliasing={{1}: (9, {}), {2}: (10, {})} | custom-call | flops 268435456 | bytes 8388608 | tf_op jit(solution)/shard_map/pallas_call | solution.py:237
  55.2 5.1 %collective-permute-start.15 = (bf16[272,256]{1,0:T(8,128)(2,1)}, bf16[272,256]{1,0:T(8,128)(2,1)S(1)}, u32[]{:S(2)}, u32[]{:S(2)}) collective-permute-start(bf16[272,256]{1,0:T(8,128)(2,1)} %get-tuple-element.55.kv0), channel_id=1, source_target_pairs={{0,32},{16,48},{1,33},{17,49},{2,34},{18,50},{3,35},{19,51},{4,36}... | collective-permute-start | bytes 417800 | tf_op jit(solution)/shard_map/ppermute | solution.py:410
  60.3 2.6 %collective-permute-start.14 = (bf16[272,256]{1,0:T(8,128)(2,1)}, bf16[272,256]{1,0:T(8,128)(2,1)S(1)}, u32[]{:S(2)}, u32[]{:S(2)}) collective-permute-start(bf16[272,256]{1,0:T(8,128)(2,1)} %get-tuple-element.55.kv0), channel_id=1, source_target_pairs={{0,16},{16,32},{32,48},{1,17},{17,33},{33,49},{2,18},{18,34},{34,5... | collective-permute-start | bytes 417800 | tf_op jit(solution)/shard_map/ppermute | solution.py:409
  62.9 1.8 %collective-permute-start.17 = (bf16[272,256]{1,0:T(8,128)(2,1)}, bf16[272,256]{1,0:T(8,128)(2,1)S(1)}, u32[]{:S(2)}, u32[]{:S(2)}) collective-permute-start(bf16[272,256]{1,0:T(8,128)(2,1)} %get-tuple-element.55.kv0), channel_id=1, source_target_pairs={{0,8},{1,9},{2,10},{3,11},{4,12},{5,13},{6,14},{7,15},{16,24},{17,... | collective-permute-start | bytes 417800 | tf_op jit(solution)/shard_map/ppermute | solution.py:411
  64.8 1.3 collective-permute-start.18
  66.1 1.1 collective-permute-done.14.kv1
  69.4 13.0 %shard_map.103 = (bf16[256,1024]{1,0:T(8,128)(2,1)}, bf16[256,1024]{1,0:T(8,128)(2,1)}, f32[256,256]{1,0:T(8,128)S(1)}, f32[256,256]{1,0:T(8,128)S(1)}, f32[256,...) custom-call(s32[4]{0:T(128)S(1)} %copy-done.5, bf16[272,256]{1,0:T(8,128)(2,1)S(1)} %copy-done.8, ...), custom_call_target="tpu_custom_call" | custom-call | flops 4026531840 | bytes 6291456 | tf_op jit(solution)/shard_map/pallas_call | solution.py:115
  82.6 1.9 %collective-permute-done.19 = f32[2,256,256]{2,1,0:T(8,128)} collective-permute-done((f32[2,256,256]{2,1,0:T(8,128)S(1)}, f32[2,256,256]{2,1,0:T(8,128)}, u32[]{:S(2)}, u32[]{:S(2)}) %collective-permute-start.19) | collective-permute-done | bytes 524320 | tf_op jit(solution)/shard_map/ppermute | solution.py:387
  84.5 1.1 fusion.3
  85.6 1.3 collective-permute-start.20
  86.9 1.3 collective-permute-start.21
  88.2 5.5 %collective-permute-done.20 = bf16[256,256]{1,0:T(8,128)(2,1)S(1)} collective-permute-done((bf16[256,256]{1,0:T(8,128)(2,1)S(1)}, bf16[256,256]{1,0:T(8,128)(2,1)S(1)}, u32[]{:S(2)}, u32[]{:S(2)}) %collective-permute-start.20) | collective-permute-done | bytes 131104 | tf_op jit(solution)/shard_map/ppermute | solution.py:425
  93.7 3.1 %collective-permute-done.21 = bf16[256,256]{1,0:T(8,128)(2,1)S(1)} collective-permute-done((bf16[256,256]{1,0:T(8,128)(2,1)S(1)}, bf16[256,256]{1,0:T(8,128)(2,1)S(1)}, u32[]{:S(2)}, u32[]{:S(2)}) %collective-permute-start.21) | collective-permute-done | bytes 131104 | tf_op jit(solution)/shard_map/ppermute | solution.py:426
  96.8 1.0 fusion.7.g_ref
  97.8 1.6 %copy-done.2 = bf16[8192,128]{1,0:T(8,128)(2,1)S(1)} copy-done((bf16[8192,128]{1,0:T(8,128)(2,1)S(1)}, bf16[8192,128]{1,0:T(8,128)(2,1)}, u32[]{:S(2)}) %copy-start.2) | copy-done | bytes 2097176
  99.4 3.5 %shard_map.104 = (bf16[16,8192]{1,0:T(8,128)(2,1)S(1)}, bf16[16,8192]{1,0:T(8,128)(2,1)S(1)}, bf16[16,8192]{1,0:T(8,128)(2,1)S(1)}, bf16[16,8192]{1,0:T(8,128)(2...) custom-call(s32[4]{0:T(128)S(1)} %copy-done.5, ...), custom_call_target="tpu_custom_call" | custom-call | flops 536870912 | bytes 6291456 | tf_op jit(solution)/shard_map/pallas_call | solution.py:358
  103.0 3.2 %collective-permute-start.25 = (bf16[16,8192]{1,0:T(8,128)(2,1)S(1)}, bf16[16,8192]{1,0:T(8,128)(2,1)S(1)}, u32[]{:S(2)}, u32[]{:S(2)}) collective-permute-start(bf16[16,8192]{1,0:T(8,128)(2,1)S(1)} %get-tuple-element.66), channel_id=1, source_target_pairs={{0,7},{1,0},{2,1},{3,2},{4,3},{5,4},{6,5},{7,6},{8,15},{9,8},{10,9... | collective-permute-start | bytes 786440 | tf_op jit(solution)/shard_map/ppermute | solution.py:391
  106.2 1.3 collective-permute-done.22.gs_ref
  107.5 1.9 %collective-permute-start.33 = (bf16[16,8192]{1,0:T(8,128)(2,1)S(1)}, bf16[16,8192]{1,0:T(8,128)(2,1)S(1)}, u32[]{:S(2)}, u32[]{:S(2)}) collective-permute-start(bf16[16,8192]{1,0:T(8,128)(2,1)S(1)} %get-tuple-element.67), channel_id=1, source_target_pairs={{0,7},{1,0},{2,1},{3,2},{4,3},{5,4},{6,5},{7,6},{8,15},{9,8},{10,9... | collective-permute-start | bytes 786440 | tf_op jit(solution)/shard_map/ppermute | solution.py:391
  109.4 4.6 %shard_map.105 = bf16[16,256,256]{2,1,0:T(8,128)(2,1)S(1)} custom-call(s32[4]{0:T(128)S(1)} %copy-done.5, bf16[256,256]{1,0:T(8,128)(2,1)S(1)} %fusion.7.g_ref, bf16[256,256]{1,0:T(8,128)(2,1)S(1)} %collective-permute-done.22.gs_ref, bf16[256,4096]{1,0:T(8,128)(2,1)S(1)} %copy-done, bf16[256,4096]{1,0:T(8,128)(2,1)S(1)} %copy-done, ...), custom_call_target="tpu_custom_call" | custom-call | flops 1073741824 | bytes 6291456 | tf_op jit(solution)/shard_map/pallas_call | solution.py:294
  114.1 1.1 add_convert_fusion.10
  115.9 1.4 collective-permute-done.32
  117.5 7.0 %all-to-all-start = ((bf16[16,256,256]{2,1,0:T(8,128)(2,1)}), bf16[16,256,256]{2,1,0:T(8,128)(2,1)}, u32[]{:S(2)}, u32[]{:S(2)}) async-start(bf16[16,256,256]{2,1,0:T(8,128)(2,1)} %copy-done.4), calls=%async_computation | async-start | bytes 4194304 | tf_op jit(solution)/shard_map/all_to_all | solution.py:449
  124.4 3.0 %collective-permute-start.36 = (bf16[16,8192]{1,0:T(8,128)(2,1)S(1)}, bf16[16,8192]{1,0:T(8,128)(2,1)S(1)}, u32[]{:S(2)}, u32[]{:S(2)}) collective-permute-start(bf16[16,8192]{1,0:T(8,128)(2,1)S(1)} %add_convert_fusion.3), channel_id=1, source_target_pairs={{0,7},{1,0},{2,1},{3,2},{4,3},{5,4},{6,5},{7,6},{8,15},{9,8},{10,9... | collective-permute-start | bytes 786440 | tf_op jit(solution)/shard_map/ppermute | solution.py:391
  127.4 3.2 %collective-permute-start.29 = (bf16[16,8192]{1,0:T(8,128)(2,1)}, bf16[16,8192]{1,0:T(8,128)(2,1)S(1)}, u32[]{:S(2)}, u32[]{:S(2)}) collective-permute-start(bf16[16,8192]{1,0:T(8,128)(2,1)} %get-tuple-element.82), channel_id=1, source_target_pairs={{0,7},{1,0},{2,1},{3,2},{4,3},{5,4},{6,5},{7,6},{8,15},{9,8},{10,9... | collective-permute-start | bytes 786440 | tf_op jit(solution)/shard_map/ppermute | solution.py:391
  130.6 1.6 %copy-done.3 = bf16[8192,128]{1,0:T(8,128)(2,1)S(1)} copy-done((bf16[8192,128]{1,0:T(8,128)(2,1)S(1)}, bf16[8192,128]{1,0:T(8,128)(2,1)}, u32[]{:S(2)}) %copy-start.3) | copy-done | bytes 2097176
  132.2 3.5 %shard_map.106 = (bf16[16,8192]{1,0:T(8,128)(2,1)S(1)}, bf16[16,8192]{1,0:T(8,128)(2,1)S(1)}, bf16[16,8192]{1,0:T(8,128)(2,1)S(1)}, bf16[16,8192]{1,0:T(8,128)(2...) custom-call(s32[4]{0:T(128)S(1)} %copy-done.5, ...), custom_call_target="tpu_custom_call" | custom-call | flops 536870912 | bytes 6291456 | tf_op jit(solution)/shard_map/pallas_call | solution.py:358
  135.9 1.1 collective-permute-done.29
  137.0 3.7 %collective-permute-start.30 = (bf16[16,8192]{1,0:T(8,128)(2,1)S(1)}, bf16[16,8192]{1,0:T(8,128)(2,1)S(1)}, u32[]{:S(2)}, u32[]{:S(2)}) collective-permute-start(bf16[16,8192]{1,0:T(8,128)(2,1)S(1)} %add_convert_fusion.7), channel_id=1, source_target_pairs={{0,7},{1,0},{2,1},{3,2},{4,3},{5,4},{6,5},{7,6},{8,15},{9,8},{10,9... | collective-permute-start | bytes 786440 | tf_op jit(solution)/shard_map/ppermute | solution.py:391
  141.0 3.3 %collective-permute-start.37 = (bf16[16,8192]{1,0:T(8,128)(2,1)S(1)}, bf16[16,8192]{1,0:T(8,128)(2,1)S(1)}, u32[]{:S(2)}, u32[]{:S(2)}) collective-permute-start(bf16[16,8192]{1,0:T(8,128)(2,1)S(1)} %add_convert_fusion.2), channel_id=1, source_target_pairs={{0,7},{1,0},{2,1},{3,2},{4,3},{5,4},{6,5},{7,6},{8,15},{9,8},{10,9... | collective-permute-start | bytes 786440 | tf_op jit(solution)/shard_map/ppermute | solution.py:391
  145.1 2.2 %collective-permute-done.30 = bf16[16,8192]{1,0:T(8,128)(2,1)S(1)} collective-permute-done((bf16[16,8192]{1,0:T(8,128)(2,1)S(1)}, bf16[16,8192]{1,0:T(8,128)(2,1)S(1)}, u32[]{:S(2)}, u32[]{:S(2)}) %collective-permute-start.30) | collective-permute-done | bytes 262176 | tf_op jit(solution)/shard_map/ppermute | solution.py:391
  147.4 3.8 %collective-permute-start.31 = (bf16[16,8192]{1,0:T(8,128)(2,1)S(1)}, bf16[16,8192]{1,0:T(8,128)(2,1)S(1)}, u32[]{:S(2)}, u32[]{:S(2)}) collective-permute-start(bf16[16,8192]{1,0:T(8,128)(2,1)S(1)} %add_convert_fusion.6), channel_id=1, source_target_pairs={{0,7},{1,0},{2,1},{3,2},{4,3},{5,4},{6,5},{7,6},{8,15},{9,8},{10,9... | collective-permute-start | bytes 786440 | tf_op jit(solution)/shard_map/ppermute | solution.py:391
  151.2 2.6 %shard_map.107 = (f32[256,128]{1,0:T(8,128)}, f32[256,128]{1,0:T(8,128)}) custom-call(bf16[16,256,256]{2,1,0:T(8,128)(2,1)} %all-to-all-done.parts), custom_call_target="tpu_custom_call" | custom-call | tf_op jit(solution)/shard_map/pallas_call | solution.py:323
  (97 shorter events, 9.7 us)
Async XLA Ops:
  1.7 39.7 %copy-start.9 = (bf16[16,8192]{1,0:T(8,128)(2,1)}, bf16[16,8192]{1,0:T(8,128)(2,1)S(1)}, u32[]{:S(2)}) copy-start(bf16[16,8192]{1,0:T(8,128)(2,1)S(1)} %get-tuple-element.101.refs_0_) | copy-start | bytes 786436
  1.7 39.7 %copy-start.10 = (bf16[16,8192]{1,0:T(8,128)(2,1)}, bf16[16,8192]{1,0:T(8,128)(2,1)S(1)}, u32[]{:S(2)}) copy-start(bf16[16,8192]{1,0:T(8,128)(2,1)S(1)} %get-tuple-element.102.refs_1_) | copy-start | bytes 786436
  1.7 13.1 %collective-permute-start.6 = (bf16[16,8192]{1,0:T(8,128)(2,1)S(1)}, bf16[16,8192]{1,0:T(8,128)(2,1)S(1)}, u32[]{:S(2)}, u32[]{:S(2)}) collective-permute-start(bf16[16,8192]{1,0:T(8,128)(2,1)S(1)} %get-tuple-element.101.refs_0_), channel_id=1, source_target_pairs={{0,1},{1,2},{2,3},{3,4},{4,5},{5,6},{6,7},{7,0},{8,9},{9,10},{10,1... | collective-permute-start | bytes 786440 | tf_op jit(solution)/shard_map/ppermute | solution.py:391
  3.7 11.1 %collective-permute-start.10 = (bf16[16,8192]{1,0:T(8,128)(2,1)S(1)}, bf16[16,8192]{1,0:T(8,128)(2,1)S(1)}, u32[]{:S(2)}, u32[]{:S(2)}) collective-permute-start(bf16[16,8192]{1,0:T(8,128)(2,1)S(1)} %get-tuple-element.102.refs_1_), channel_id=1, source_target_pairs={{0,7},{1,0},{2,1},{3,2},{4,3},{5,4},{6,5},{7,6},{8,15},{9,8},{10,9... | collective-permute-start | bytes 786440 | tf_op jit(solution)/shard_map/ppermute | solution.py:391
  7.7 12.3 %collective-permute-start.3 = (bf16[16,8192]{1,0:T(8,128)(2,1)S(1)}, bf16[16,8192]{1,0:T(8,128)(2,1)S(1)}, u32[]{:S(2)}, u32[]{:S(2)}) collective-permute-start(bf16[16,8192]{1,0:T(8,128)(2,1)S(1)} %get-tuple-element.101.refs_0_), channel_id=1, source_target_pairs={{0,7},{1,0},{2,1},{3,2},{4,3},{5,4},{6,5},{7,6},{8,15},{9,8},{10,9... | collective-permute-start | bytes 786440 | tf_op jit(solution)/shard_map/ppermute | solution.py:391
  9.7 14.1 %collective-permute-start = (bf16[16,8192]{1,0:T(8,128)(2,1)S(1)}, bf16[16,8192]{1,0:T(8,128)(2,1)S(1)}, u32[]{:S(2)}, u32[]{:S(2)}) collective-permute-start(bf16[16,8192]{1,0:T(8,128)(2,1)S(1)} %get-tuple-element.102.refs_1_), channel_id=1, source_target_pairs={{0,1},{1,2},{2,3},{3,4},{4,5},{5,6},{6,7},{7,0},{8,9},{9,10},{10,1... | collective-permute-start | bytes 786440 | tf_op jit(solution)/shard_map/ppermute | solution.py:391
  14.8 26.6 %copy-start.15 = (bf16[16,8192]{1,0:T(8,128)(2,1)}, bf16[16,8192]{1,0:T(8,128)(2,1)S(1)}, u32[]{:S(2)}) copy-start(bf16[16,8192]{1,0:T(8,128)(2,1)S(1)} %collective-permute-done.6.refs_2_) | copy-start | bytes 786436
  14.8 10.4 %collective-permute-start.7 = (bf16[16,8192]{1,0:T(8,128)(2,1)S(1)}, bf16[16,8192]{1,0:T(8,128)(2,1)S(1)}, u32[]{:S(2)}, u32[]{:S(2)}) collective-permute-start(bf16[16,8192]{1,0:T(8,128)(2,1)S(1)} %collective-permute-done.6.refs_2_), channel_id=1, source_target_pairs={{0,1},{1,2},{2,3},{3,4},{4,5},{5,6},{6,7},{7,0},{8,9},{9,10},{10,1... | collective-permute-start | bytes 786440 | tf_op jit(solution)/shard_map/ppermute | solution.py:391
  14.8 26.6 %copy-start.16 = (bf16[16,8192]{1,0:T(8,128)(2,1)}, bf16[16,8192]{1,0:T(8,128)(2,1)S(1)}, u32[]{:S(2)}) copy-start(bf16[16,8192]{1,0:T(8,128)(2,1)S(1)} %collective-permute-done.10.refs_5_) | copy-start | bytes 786436
  14.8 10.9 %collective-permute-start.11 = (bf16[16,8192]{1,0:T(8,128)(2,1)S(1)}, bf16[16,8192]{1,0:T(8,128)(2,1)S(1)}, u32[]{:S(2)}, u32[]{:S(2)}) collective-permute-start(bf16[16,8192]{1,0:T(8,128)(2,1)S(1)} %collective-permute-done.10.refs_5_), channel_id=1, source_target_pairs={{0,7},{1,0},{2,1},{3,2},{4,3},{5,4},{6,5},{7,6},{8,15},{9,8},{10,9... | collective-permute-start | bytes 786440 | tf_op jit(solution)/shard_map/ppermute | solution.py:391
  20.1 21.3 %copy-start.17 = (bf16[16,8192]{1,0:T(8,128)(2,1)}, bf16[16,8192]{1,0:T(8,128)(2,1)S(1)}, u32[]{:S(2)}) copy-start(bf16[16,8192]{1,0:T(8,128)(2,1)S(1)} %collective-permute-done.3.refs_4_) | copy-start | bytes 786436
  20.1 11.2 %collective-permute-start.4 = (bf16[16,8192]{1,0:T(8,128)(2,1)S(1)}, bf16[16,8192]{1,0:T(8,128)(2,1)S(1)}, u32[]{:S(2)}, u32[]{:S(2)}) collective-permute-start(bf16[16,8192]{1,0:T(8,128)(2,1)S(1)} %collective-permute-done.3.refs_4_), channel_id=1, source_target_pairs={{0,7},{1,0},{2,1},{3,2},{4,3},{5,4},{6,5},{7,6},{8,15},{9,8},{10,9... | collective-permute-start | bytes 786440 | tf_op jit(solution)/shard_map/ppermute | solution.py:391
  23.8 17.6 %copy-start.18 = (bf16[16,8192]{1,0:T(8,128)(2,1)}, bf16[16,8192]{1,0:T(8,128)(2,1)S(1)}, u32[]{:S(2)}) copy-start(bf16[16,8192]{1,0:T(8,128)(2,1)S(1)} %collective-permute-done.refs_3_) | copy-start | bytes 786436
  23.8 11.2 %collective-permute-start.1 = (bf16[16,8192]{1,0:T(8,128)(2,1)S(1)}, bf16[16,8192]{1,0:T(8,128)(2,1)}, u32[]{:S(2)}, u32[]{:S(2)}) collective-permute-start(bf16[16,8192]{1,0:T(8,128)(2,1)S(1)} %collective-permute-done.refs_3_), channel_id=1, source_target_pairs={{0,1},{1,2},{2,3},{3,4},{4,5},{5,6},{6,7},{7,0},{8,9},{9,10},{10,1... | collective-permute-start | bytes 786440 | tf_op jit(solution)/shard_map/ppermute | solution.py:391
  25.2 11.7 %collective-permute-start.8 = (bf16[16,8192]{1,0:T(8,128)(2,1)S(1)}, bf16[16,8192]{1,0:T(8,128)(2,1)}, u32[]{:S(2)}, u32[]{:S(2)}) collective-permute-start(bf16[16,8192]{1,0:T(8,128)(2,1)S(1)} %collective-permute-done.7.refs_6_), channel_id=1, source_target_pairs={{0,1},{1,2},{2,3},{3,4},{4,5},{5,6},{6,7},{7,0},{8,9},{9,10},{10,1... | collective-permute-start | bytes 786440 | tf_op jit(solution)/shard_map/ppermute | solution.py:391
  25.7 11.2 %collective-permute-start.12 = (bf16[16,8192]{1,0:T(8,128)(2,1)S(1)}, bf16[16,8192]{1,0:T(8,128)(2,1)}, u32[]{:S(2)}, u32[]{:S(2)}) collective-permute-start(bf16[16,8192]{1,0:T(8,128)(2,1)S(1)} %collective-permute-done.11.refs_9_), channel_id=1, source_target_pairs={{0,7},{1,0},{2,1},{3,2},{4,3},{5,4},{6,5},{7,6},{8,15},{9,8},{10,9... | collective-permute-start | bytes 786440 | tf_op jit(solution)/shard_map/ppermute | solution.py:391
  31.3 17.0 %collective-permute-start.5 = (bf16[16,8192]{1,0:T(8,128)(2,1)S(1)}, bf16[16,8192]{1,0:T(8,128)(2,1)S(1)}, u32[]{:S(2)}, u32[]{:S(2)}) collective-permute-start(bf16[16,8192]{1,0:T(8,128)(2,1)S(1)} %collective-permute-done.4.refs_8_), channel_id=1, source_target_pairs={{0,7},{1,0},{2,1},{3,2},{4,3},{5,4},{6,5},{7,6},{8,15},{9,8},{10,9... | collective-permute-start | bytes 786440 | tf_op jit(solution)/shard_map/ppermute | solution.py:391
  35.0 13.3 %collective-permute-start.2 = (bf16[16,8192]{1,0:T(8,128)(2,1)}, bf16[16,8192]{1,0:T(8,128)(2,1)S(1)}, u32[]{:S(2)}, u32[]{:S(2)}) collective-permute-start(bf16[16,8192]{1,0:T(8,128)(2,1)} %collective-permute-done.1.refs_7_), channel_id=1, source_target_pairs={{0,1},{1,2},{2,3},{3,4},{4,5},{5,6},{6,7},{7,0},{8,9},{9,10},{10,1... | collective-permute-start | bytes 786440 | tf_op jit(solution)/shard_map/ppermute | solution.py:391
  36.9 11.4 %collective-permute-start.9 = (bf16[16,8192]{1,0:T(8,128)(2,1)}, bf16[16,8192]{1,0:T(8,128)(2,1)S(1)}, u32[]{:S(2)}, u32[]{:S(2)}) collective-permute-start(bf16[16,8192]{1,0:T(8,128)(2,1)} %collective-permute-done.8.refs_10_), channel_id=1, source_target_pairs={{0,1},{1,2},{2,3},{3,4},{4,5},{5,6},{6,7},{7,0},{8,9},{9,10},{10,1... | collective-permute-start | bytes 786440 | tf_op jit(solution)/shard_map/ppermute | solution.py:391
  36.9 11.4 %collective-permute-start.13 = (bf16[16,8192]{1,0:T(8,128)(2,1)}, bf16[16,8192]{1,0:T(8,128)(2,1)S(1)}, u32[]{:S(2)}, u32[]{:S(2)}) collective-permute-start(bf16[16,8192]{1,0:T(8,128)(2,1)} %collective-permute-done.12.refs_11_), channel_id=1, source_target_pairs={{0,7},{1,0},{2,1},{3,2},{4,3},{5,4},{6,5},{7,6},{8,15},{9,8},{10,9... | collective-permute-start | bytes 786440 | tf_op jit(solution)/shard_map/ppermute | solution.py:391
  49.3 19.2 %copy-start.5 = (s32[4]{0:T(128)S(1)}, s32[4]{0:T(128)}, u32[]{:S(2)}) copy-start(s32[4]{0:T(128)} %pad_add_fusion.place_ref) | copy-start | bytes 52
  49.3 19.2 %copy-start.6 = (bf16[1,256,1024]{2,1,0:T(8,128)(2,1)S(1)}, bf16[1,256,1024]{2,1,0:T(8,128)(2,1)}, u32[]{:S(2)}) copy-start(bf16[1,256,1024]{2,1,0:T(8,128)(2,1)} %param.9) | copy-start | bytes 1572868
  49.3 19.2 %copy-start.7 = (bf16[1,256,1024]{2,1,0:T(8,128)(2,1)S(1)}, bf16[1,256,1024]{2,1,0:T(8,128)(2,1)}, u32[]{:S(2)}) copy-start(bf16[1,256,1024]{2,1,0:T(8,128)(2,1)} %param.10) | copy-start | bytes 1572868
  55.1 54.3 %collective-permute-start.23 = (bf16[256,4096]{1,0:T(8,128)(2,1)}, bf16[256,4096]{1,0:T(8,128)(2,1)}, u32[]{:S(2)}, u32[]{:S(2)}) collective-permute-start(bf16[256,4096]{1,0:T(8,128)(2,1)} %get-tuple-element.72), channel_id=1, source_target_pairs={{0,8},{8,0},{1,9},{9,1},{2,10},{10,2},{3,11},{11,3},{4,12},{12,4},... | collective-permute-start | bytes 6291464 | tf_op jit(solution)/shard_map/ppermute | solution.py:387
  55.2 9.6 %collective-permute-start.15 = (bf16[272,256]{1,0:T(8,128)(2,1)}, bf16[272,256]{1,0:T(8,128)(2,1)S(1)}, u32[]{:S(2)}, u32[]{:S(2)}) collective-permute-start(bf16[272,256]{1,0:T(8,128)(2,1)} %get-tuple-element.55.kv0), channel_id=1, source_target_pairs={{0,32},{16,48},{1,33},{17,49},{2,34},{18,50},{3,35},{19,51},{4,36}... | collective-permute-start | bytes 417800 | tf_op jit(solution)/shard_map/ppermute | solution.py:410
  60.3 6.9 %collective-permute-start.14 = (bf16[272,256]{1,0:T(8,128)(2,1)}, bf16[272,256]{1,0:T(8,128)(2,1)S(1)}, u32[]{:S(2)}, u32[]{:S(2)}) collective-permute-start(bf16[272,256]{1,0:T(8,128)(2,1)} %get-tuple-element.55.kv0), channel_id=1, source_target_pairs={{0,16},{16,32},{32,48},{1,17},{17,33},{33,49},{2,18},{18,34},{34,5... | collective-permute-start | bytes 417800 | tf_op jit(solution)/shard_map/ppermute | solution.py:409
  62.9 4.4 %collective-permute-start.17 = (bf16[272,256]{1,0:T(8,128)(2,1)}, bf16[272,256]{1,0:T(8,128)(2,1)S(1)}, u32[]{:S(2)}, u32[]{:S(2)}) collective-permute-start(bf16[272,256]{1,0:T(8,128)(2,1)} %get-tuple-element.55.kv0), channel_id=1, source_target_pairs={{0,8},{1,9},{2,10},{3,11},{4,12},{5,13},{6,14},{7,15},{16,24},{17,... | collective-permute-start | bytes 417800 | tf_op jit(solution)/shard_map/ppermute | solution.py:411
  64.8 3.3 %collective-permute-start.18 = (bf16[272,256]{1,0:T(8,128)(2,1)S(1)}, bf16[272,256]{1,0:T(8,128)(2,1)S(1)}, u32[]{:S(2)}, u32[]{:S(2)}) collective-permute-start(bf16[272,256]{1,0:T(8,128)(2,1)S(1)} %collective-permute-done.15.kv2), channel_id=1, source_target_pairs={{8,0},{9,1},{10,2},{11,3},{12,4},{13,5},{14,6},{15,7},{24,16},{25,... | collective-permute-start | bytes 417800 | tf_op jit(solution)/shard_map/ppermute | solution.py:413
  67.2 1.4 collective-permute-start.16
  82.5 2.0 %collective-permute-start.19 = (f32[2,256,256]{2,1,0:T(8,128)S(1)}, f32[2,256,256]{2,1,0:T(8,128)}, u32[]{:S(2)}, u32[]{:S(2)}) collective-permute-start(f32[2,256,256]{2,1,0:T(8,128)S(1)} %get-tuple-element.59), channel_id=1, source_target_pairs={{0,8},{8,0},{1,9},{9,1},{2,10},{10,2},{3,11},{11,3},{4,12},{12,4},... | collective-permute-start | bytes 1572872 | tf_op jit(solution)/shard_map/ppermute | solution.py:387
  85.6 8.1 %collective-permute-start.20 = (bf16[256,256]{1,0:T(8,128)(2,1)S(1)}, bf16[256,256]{1,0:T(8,128)(2,1)S(1)}, u32[]{:S(2)}, u32[]{:S(2)}) collective-permute-start(bf16[256,256]{1,0:T(8,128)(2,1)S(1)} %get-tuple-element.99), channel_id=1, source_target_pairs={{16,0},{32,16},{48,32},{17,1},{33,17},{49,33},{18,2},{34,18},{50,3... | collective-permute-start | bytes 393224 | tf_op jit(solution)/shard_map/ppermute | solution.py:425
  86.9 9.8 %collective-permute-start.21 = (bf16[256,256]{1,0:T(8,128)(2,1)S(1)}, bf16[256,256]{1,0:T(8,128)(2,1)S(1)}, u32[]{:S(2)}, u32[]{:S(2)}) collective-permute-start(bf16[256,256]{1,0:T(8,128)(2,1)S(1)} %get-tuple-element.100), channel_id=1, source_target_pairs={{32,0},{48,16},{33,1},{49,17},{34,2},{50,18},{35,3},{51,19},{36,4}... | collective-permute-start | bytes 393224 | tf_op jit(solution)/shard_map/ppermute | solution.py:426
  102.9 11.2 %collective-permute-start.24 = (bf16[16,8192]{1,0:T(8,128)(2,1)S(1)}, bf16[16,8192]{1,0:T(8,128)(2,1)S(1)}, u32[]{:S(2)}, u32[]{:S(2)}) collective-permute-start(bf16[16,8192]{1,0:T(8,128)(2,1)S(1)} %get-tuple-element.65), channel_id=1, source_target_pairs={{0,1},{1,2},{2,3},{3,4},{4,5},{5,6},{6,7},{7,0},{8,9},{9,10},{10,1... | collective-permute-start | bytes 786440 | tf_op jit(solution)/shard_map/ppermute | solution.py:391
  103.0 11.1 %collective-permute-start.25 = (bf16[16,8192]{1,0:T(8,128)(2,1)S(1)}, bf16[16,8192]{1,0:T(8,128)(2,1)S(1)}, u32[]{:S(2)}, u32[]{:S(2)}) collective-permute-start(bf16[16,8192]{1,0:T(8,128)(2,1)S(1)} %get-tuple-element.66), channel_id=1, source_target_pairs={{0,7},{1,0},{2,1},{3,2},{4,3},{5,4},{6,5},{7,6},{8,15},{9,8},{10,9... | collective-permute-start | bytes 786440 | tf_op jit(solution)/shard_map/ppermute | solution.py:391
  106.2 1.3 collective-permute-start.22
  106.2 11.1 %collective-permute-start.32 = (bf16[16,8192]{1,0:T(8,128)(2,1)S(1)}, bf16[16,8192]{1,0:T(8,128)(2,1)S(1)}, u32[]{:S(2)}, u32[]{:S(2)}) collective-permute-start(bf16[16,8192]{1,0:T(8,128)(2,1)S(1)} %get-tuple-element.64), channel_id=1, source_target_pairs={{0,1},{1,2},{2,3},{3,4},{4,5},{5,6},{6,7},{7,0},{8,9},{9,10},{10,1... | collective-permute-start | bytes 786440 | tf_op jit(solution)/shard_map/ppermute | solution.py:391
  107.5 9.8 %collective-permute-start.33 = (bf16[16,8192]{1,0:T(8,128)(2,1)S(1)}, bf16[16,8192]{1,0:T(8,128)(2,1)S(1)}, u32[]{:S(2)}, u32[]{:S(2)}) collective-permute-start(bf16[16,8192]{1,0:T(8,128)(2,1)S(1)} %get-tuple-element.67), channel_id=1, source_target_pairs={{0,7},{1,0},{2,1},{3,2},{4,3},{5,4},{6,5},{7,6},{8,15},{9,8},{10,9... | collective-permute-start | bytes 786440 | tf_op jit(solution)/shard_map/ppermute | solution.py:391
  115.1 20.6 %collective-permute-start.26 = (bf16[16,8192]{1,0:T(8,128)(2,1)}, bf16[16,8192]{1,0:T(8,128)(2,1)S(1)}, u32[]{:S(2)}, u32[]{:S(2)}) collective-permute-start(bf16[16,8192]{1,0:T(8,128)(2,1)} %get-tuple-element.79), channel_id=1, source_target_pairs={{0,1},{1,2},{2,3},{3,4},{4,5},{5,6},{6,7},{7,0},{8,9},{9,10},{10,1... | collective-permute-start | bytes 786440 | tf_op jit(solution)/shard_map/ppermute | solution.py:391
  117.5 33.7 %all-to-all-start = ((bf16[16,256,256]{2,1,0:T(8,128)(2,1)}), bf16[16,256,256]{2,1,0:T(8,128)(2,1)}, u32[]{:S(2)}, u32[]{:S(2)}) async-start(bf16[16,256,256]{2,1,0:T(8,128)(2,1)} %copy-done.4), calls=%async_computation | async-start | bytes 4194304 | tf_op jit(solution)/shard_map/all_to_all | solution.py:449
  124.4 16.5 %collective-permute-start.36 = (bf16[16,8192]{1,0:T(8,128)(2,1)S(1)}, bf16[16,8192]{1,0:T(8,128)(2,1)S(1)}, u32[]{:S(2)}, u32[]{:S(2)}) collective-permute-start(bf16[16,8192]{1,0:T(8,128)(2,1)S(1)} %add_convert_fusion.3), channel_id=1, source_target_pairs={{0,7},{1,0},{2,1},{3,2},{4,3},{5,4},{6,5},{7,6},{8,15},{9,8},{10,9... | collective-permute-start | bytes 786440 | tf_op jit(solution)/shard_map/ppermute | solution.py:391
  127.4 13.3 %collective-permute-start.34 = (bf16[16,8192]{1,0:T(8,128)(2,1)S(1)}, bf16[16,8192]{1,0:T(8,128)(2,1)S(1)}, u32[]{:S(2)}, u32[]{:S(2)}) collective-permute-start(bf16[16,8192]{1,0:T(8,128)(2,1)S(1)} %add_convert_fusion.5), channel_id=1, source_target_pairs={{0,1},{1,2},{2,3},{3,4},{4,5},{5,6},{6,7},{7,0},{8,9},{9,10},{10,1... | collective-permute-start | bytes 786440 | tf_op jit(solution)/shard_map/ppermute | solution.py:391
  127.4 9.6 %collective-permute-start.29 = (bf16[16,8192]{1,0:T(8,128)(2,1)}, bf16[16,8192]{1,0:T(8,128)(2,1)S(1)}, u32[]{:S(2)}, u32[]{:S(2)}) collective-permute-start(bf16[16,8192]{1,0:T(8,128)(2,1)} %get-tuple-element.82), channel_id=1, source_target_pairs={{0,7},{1,0},{2,1},{3,2},{4,3},{5,4},{6,5},{7,6},{8,15},{9,8},{10,9... | collective-permute-start | bytes 786440 | tf_op jit(solution)/shard_map/ppermute | solution.py:391
  135.8 9.2 %collective-permute-start.27 = (bf16[16,8192]{1,0:T(8,128)(2,1)S(1)}, bf16[16,8192]{1,0:T(8,128)(2,1)S(1)}, u32[]{:S(2)}, u32[]{:S(2)}) collective-permute-start(bf16[16,8192]{1,0:T(8,128)(2,1)S(1)} %add_convert_fusion.9), channel_id=1, source_target_pairs={{0,1},{1,2},{2,3},{3,4},{4,5},{5,6},{6,7},{7,0},{8,9},{9,10},{10,1... | collective-permute-start | bytes 786440 | tf_op jit(solution)/shard_map/ppermute | solution.py:391
  137.0 10.3 %collective-permute-start.30 = (bf16[16,8192]{1,0:T(8,128)(2,1)S(1)}, bf16[16,8192]{1,0:T(8,128)(2,1)S(1)}, u32[]{:S(2)}, u32[]{:S(2)}) collective-permute-start(bf16[16,8192]{1,0:T(8,128)(2,1)S(1)} %add_convert_fusion.7), channel_id=1, source_target_pairs={{0,7},{1,0},{2,1},{3,2},{4,3},{5,4},{6,5},{7,6},{8,15},{9,8},{10,9... | collective-permute-start | bytes 786440 | tf_op jit(solution)/shard_map/ppermute | solution.py:391
  140.8 13.0 %collective-permute-start.35 = (bf16[16,8192]{1,0:T(8,128)(2,1)S(1)}, bf16[16,8192]{1,0:T(8,128)(2,1)S(1)}, u32[]{:S(2)}, u32[]{:S(2)}) collective-permute-start(bf16[16,8192]{1,0:T(8,128)(2,1)S(1)} %add_convert_fusion.4), channel_id=1, source_target_pairs={{0,1},{1,2},{2,3},{3,4},{4,5},{5,6},{6,7},{7,0},{8,9},{9,10},{10,1... | collective-permute-start | bytes 786440 | tf_op jit(solution)/shard_map/ppermute | solution.py:391
  141.0 12.8 %collective-permute-start.37 = (bf16[16,8192]{1,0:T(8,128)(2,1)S(1)}, bf16[16,8192]{1,0:T(8,128)(2,1)S(1)}, u32[]{:S(2)}, u32[]{:S(2)}) collective-permute-start(bf16[16,8192]{1,0:T(8,128)(2,1)S(1)} %add_convert_fusion.2), channel_id=1, source_target_pairs={{0,7},{1,0},{2,1},{3,2},{4,3},{5,4},{6,5},{7,6},{8,15},{9,8},{10,9... | collective-permute-start | bytes 786440 | tf_op jit(solution)/shard_map/ppermute | solution.py:391
  145.1 9.6 %collective-permute-start.28 = (bf16[16,8192]{1,0:T(8,128)(2,1)S(1)}, bf16[16,8192]{1,0:T(8,128)(2,1)S(1)}, u32[]{:S(2)}, u32[]{:S(2)}) collective-permute-start(bf16[16,8192]{1,0:T(8,128)(2,1)S(1)} %add_convert_fusion.8), channel_id=1, source_target_pairs={{0,1},{1,2},{2,3},{3,4},{4,5},{5,6},{6,7},{7,0},{8,9},{9,10},{10,1... | collective-permute-start | bytes 786440 | tf_op jit(solution)/shard_map/ppermute | solution.py:391
  147.4 7.9 %collective-permute-start.31 = (bf16[16,8192]{1,0:T(8,128)(2,1)S(1)}, bf16[16,8192]{1,0:T(8,128)(2,1)S(1)}, u32[]{:S(2)}, u32[]{:S(2)}) collective-permute-start(bf16[16,8192]{1,0:T(8,128)(2,1)S(1)} %add_convert_fusion.6), channel_id=1, source_target_pairs={{0,7},{1,0},{2,1},{3,2},{4,3},{5,4},{6,5},{7,6},{8,15},{9,8},{10,9... | collective-permute-start | bytes 786440 | tf_op jit(solution)/shard_map/ppermute | solution.py:391
  (13 other events, 78.1 us)

commit v5 on v4

--- a/solution.py
+++ b/solution.py
@@ -318,12 +318,13 @@
 
 def finish(parts):
     _, cols, block = parts.shape
-    half = pl.BlockSpec((block, HD), lambda i: (0, 0))
+    n = parts.shape[0]
+    half = pl.BlockSpec((block // 2, HD), lambda i: (i, 0))
     shape = jax.ShapeDtypeStruct((block, HD), F32)
     return pl.pallas_call(
         finish_kernel,
-        grid=(1,),
-        in_specs=[pl.BlockSpec(parts.shape, lambda i: (0, 0, 0))],
+        grid=(2,),
+        in_specs=[pl.BlockSpec((n, cols, block // 2), lambda i: (0, 0, i))],
         out_specs=[half, half],
         out_shape=[shape, shape],
         compiler_params=pltpu.CompilerParams(vmem_limit_bytes=8 * MIB),

time: 158 us -> 158 us (level)
  no operation moved by 1% of the time
where the time goes in v5:
time: 158 us; the launch traced here: 156 us
  starting transfers between devices  70.1 us (44%)
  Pallas kernels  39.6 us (25%)
  waiting for transfers between devices  34 us (22%)
  local copies, waits for them, and re-layouts  6.11 us (4%)
  other arithmetic  5.35 us (3%)
    ppermute x28, starting transfers between devices, shifted(): return lax.ppermute(a, axis, [(i, (i + s) % n) for i in range(n)])  49.4 us
    ppermute x28, waiting for transfers between devices, shifted(): return lax.ppermute(a, axis, [(i, (i + s) % n) for i in range(n)])  19.9 us
    pallas_call x1, Pallas kernels, attention(): pl.pallas_call(attention_kernel, grid_spec=pltpu.PrefetchScalarGridSpec(n...  13 us
    pallas_call x2, Pallas kernels, project(): pl.pallas_call(functools.partial(project_kernel, order, ring, bool(rest))...  12.6 us
    pallas_call x2, Pallas kernels, spread(): pl.pallas_call(functools.partial(spread_kernel, order, ring), grid_spec=p...  6.98 us
    all_to_all x1, starting transfers between devices, on_device(): lax.all_to_all(sums, ('dp', 'y'), 0, 0, tiled=True)  6.96 us
    ppermute x1, waiting for transfers between devices, on_device(): got1 = lax.ppermute(send1, 'y', up1)  5.47 us
    ppermute x1, starting transfers between devices, on_device(): kv2 = lax.ppermute(kv, 'y', down2)  5.11 us
  transfers between devices with their start and end apart: 39, of which 19 were waited for; matrix products, arithmetic and copies ran while one was open for 3% of the time, Pallas kernels for 22%

profile of v5, /device:TPU:2, one launch (start us, length us, event | category | flops | bytes accessed | tf_op | source)
XLA Modules:
  0.0 156.4 jit_solution(12337853693786805380)
XLA Ops:
  0.6 1.1 slice_bitcast_fusion.1
  1.7 2.0 %collective-permute-start.6 = (bf16[16,8192]{1,0:T(8,128)(2,1)S(1)}, bf16[16,8192]{1,0:T(8,128)(2,1)S(1)}, u32[]{:S(2)}, u32[]{:S(2)}) collective-permute-start(bf16[16,8192]{1,0:T(8,128)(2,1)S(1)} %get-tuple-element.101.refs_0_), channel_id=1, source_target_pairs={{0,1},{1,2},{2,3},{3,4},{4,5},{5,6},{6,7},{7,0},{8,9},{9,10},{10,1... | collective-permute-start | bytes 786440 | tf_op jit(solution)/shard_map/ppermute | solution.py:392
  3.7 4.0 %collective-permute-start.10 = (bf16[16,8192]{1,0:T(8,128)(2,1)S(1)}, bf16[16,8192]{1,0:T(8,128)(2,1)S(1)}, u32[]{:S(2)}, u32[]{:S(2)}) collective-permute-start(bf16[16,8192]{1,0:T(8,128)(2,1)S(1)} %get-tuple-element.102.refs_1_), channel_id=1, source_target_pairs={{0,7},{1,0},{2,1},{3,2},{4,3},{5,4},{6,5},{7,6},{8,15},{9,8},{10,9... | collective-permute-start | bytes 786440 | tf_op jit(solution)/shard_map/ppermute | solution.py:392
  7.7 1.9 %collective-permute-start.3 = (bf16[16,8192]{1,0:T(8,128)(2,1)S(1)}, bf16[16,8192]{1,0:T(8,128)(2,1)S(1)}, u32[]{:S(2)}, u32[]{:S(2)}) collective-permute-start(bf16[16,8192]{1,0:T(8,128)(2,1)S(1)} %get-tuple-element.101.refs_0_), channel_id=1, source_target_pairs={{0,7},{1,0},{2,1},{3,2},{4,3},{5,4},{6,5},{7,6},{8,15},{9,8},{10,9... | collective-permute-start | bytes 786440 | tf_op jit(solution)/shard_map/ppermute | solution.py:392
  9.8 5.0 %collective-permute-done.6.refs_2_ = bf16[16,8192]{1,0:T(8,128)(2,1)S(1)} collective-permute-done((bf16[16,8192]{1,0:T(8,128)(2,1)S(1)}, bf16[16,8192]{1,0:T(8,128)(2,1)S(1)}, u32[]{:S(2)}, u32[]{:S(2)}) %collective-permute-start.6) | collective-permute-done | bytes 262176 | tf_op jit(solution)/shard_map/ppermute | solution.py:392
  14.8 3.3 %collective-permute-start.11 = (bf16[16,8192]{1,0:T(8,128)(2,1)S(1)}, bf16[16,8192]{1,0:T(8,128)(2,1)S(1)}, u32[]{:S(2)}, u32[]{:S(2)}) collective-permute-start(bf16[16,8192]{1,0:T(8,128)(2,1)S(1)} %collective-permute-done.10.refs_5_), channel_id=1, source_target_pairs={{0,7},{1,0},{2,1},{3,2},{4,3},{5,4},{6,5},{7,6},{8,15},{9,8},{10,9... | collective-permute-start | bytes 786440 | tf_op jit(solution)/shard_map/ppermute | solution.py:392
  18.2 1.9 %collective-permute-done.3.refs_4_ = bf16[16,8192]{1,0:T(8,128)(2,1)S(1)} collective-permute-done((bf16[16,8192]{1,0:T(8,128)(2,1)S(1)}, bf16[16,8192]{1,0:T(8,128)(2,1)S(1)}, u32[]{:S(2)}, u32[]{:S(2)}) %collective-permute-start.3) | collective-permute-done | bytes 262176 | tf_op jit(solution)/shard_map/ppermute | solution.py:392
  20.1 3.7 %collective-permute-start.4 = (bf16[16,8192]{1,0:T(8,128)(2,1)S(1)}, bf16[16,8192]{1,0:T(8,128)(2,1)S(1)}, u32[]{:S(2)}, u32[]{:S(2)}) collective-permute-start(bf16[16,8192]{1,0:T(8,128)(2,1)S(1)} %collective-permute-done.3.refs_4_), channel_id=1, source_target_pairs={{0,7},{1,0},{2,1},{3,2},{4,3},{5,4},{6,5},{7,6},{8,15},{9,8},{10,9... | collective-permute-start | bytes 786440 | tf_op jit(solution)/shard_map/ppermute | solution.py:392
  23.8 1.4 collective-permute-done.7.refs_6_
  25.7 3.7 %collective-permute-start.12 = (bf16[16,8192]{1,0:T(8,128)(2,1)S(1)}, bf16[16,8192]{1,0:T(8,128)(2,1)}, u32[]{:S(2)}, u32[]{:S(2)}) collective-permute-start(bf16[16,8192]{1,0:T(8,128)(2,1)S(1)} %collective-permute-done.11.refs_9_), channel_id=1, source_target_pairs={{0,7},{1,0},{2,1},{3,2},{4,3},{5,4},{6,5},{7,6},{8,15},{9,8},{10,9... | collective-permute-start | bytes 786440 | tf_op jit(solution)/shard_map/ppermute | solution.py:392
  29.4 1.9 %collective-permute-done.4.refs_8_ = bf16[16,8192]{1,0:T(8,128)(2,1)S(1)} collective-permute-done((bf16[16,8192]{1,0:T(8,128)(2,1)S(1)}, bf16[16,8192]{1,0:T(8,128)(2,1)S(1)}, u32[]{:S(2)}, u32[]{:S(2)}) %collective-permute-start.4) | collective-permute-done | bytes 262176 | tf_op jit(solution)/shard_map/ppermute | solution.py:392
  31.3 3.7 %collective-permute-start.5 = (bf16[16,8192]{1,0:T(8,128)(2,1)S(1)}, bf16[16,8192]{1,0:T(8,128)(2,1)S(1)}, u32[]{:S(2)}, u32[]{:S(2)}) collective-permute-start(bf16[16,8192]{1,0:T(8,128)(2,1)S(1)} %collective-permute-done.4.refs_8_), channel_id=1, source_target_pairs={{0,7},{1,0},{2,1},{3,2},{4,3},{5,4},{6,5},{7,6},{8,15},{9,8},{10,9... | collective-permute-start | bytes 786440 | tf_op jit(solution)/shard_map/ppermute | solution.py:392
  35.0 1.9 %collective-permute-done.8.refs_10_ = bf16[16,8192]{1,0:T(8,128)(2,1)} collective-permute-done((bf16[16,8192]{1,0:T(8,128)(2,1)S(1)}, bf16[16,8192]{1,0:T(8,128)(2,1)}, u32[]{:S(2)}, u32[]{:S(2)}) %collective-permute-start.8) | collective-permute-done | bytes 262176 | tf_op jit(solution)/shard_map/ppermute | solution.py:392
  36.9 3.8 %collective-permute-start.13 = (bf16[16,8192]{1,0:T(8,128)(2,1)}, bf16[16,8192]{1,0:T(8,128)(2,1)S(1)}, u32[]{:S(2)}, u32[]{:S(2)}) collective-permute-start(bf16[16,8192]{1,0:T(8,128)(2,1)} %collective-permute-done.12.refs_11_), channel_id=1, source_target_pairs={{0,7},{1,0},{2,1},{3,2},{4,3},{5,4},{6,5},{7,6},{8,15},{9,8},{10,9... | collective-permute-start | bytes 786440 | tf_op jit(solution)/shard_map/ppermute | solution.py:392
  41.4 6.8 %shard_map.101 = (bf16[192,256]{1,0:T(8,128)(2,1)}, bf16[256,4096]{1,0:T(8,128)(2,1)}, bf16[256,4096]{1,0:T(8,128)(2,1)}) custom-call(s32[4]{0:T(128)} %pad_add_fusion.place_ref, bf16[16,8192]{1,0:T(8,128)(2,1)} %copy-done.9, bf16[16,8192]{1,0:T(8,128)(2,1)} %copy-done.10, bf16[16,8192]{1,0:T(8,128)(2,1)} %copy-done.15, bf16[16,8192]{1,0:T(8,128)(2,1)} %copy-done.18, ...), custom_call_target="tpu_custom_call" | custom-call | flops 805306368 | bytes 8388608 | tf_op jit(solution)/shard_map/pallas_call | solution.py:237
  49.3 5.8 %shard_map.102 = (bf16[272,256]{1,0:T(8,128)(2,1)}, bf16[256,4096]{1,0:T(8,128)(2,1)}, bf16[256,4096]{1,0:T(8,128)(2,1)}) custom-call(s32[4]{0:T(128)} %pad_add_fusion.place_ref, bf16[16,8192]{1,0:T(8,128)(2,1)} %copy-done.12, bf16[16,8192]{1,0:T(8,128)(2,1)} %copy-done.11, ...), custom_call_target="tpu_custom_call", output_to_operand_aliasing={{1}: (9, {}), {2}: (10, {})} | custom-call | flops 268435456 | bytes 8388608 | tf_op jit(solution)/shard_map/pallas_call | solution.py:237
  55.2 5.1 %collective-permute-start.15 = (bf16[272,256]{1,0:T(8,128)(2,1)}, bf16[272,256]{1,0:T(8,128)(2,1)S(1)}, u32[]{:S(2)}, u32[]{:S(2)}) collective-permute-start(bf16[272,256]{1,0:T(8,128)(2,1)} %get-tuple-element.55.kv0), channel_id=1, source_target_pairs={{0,32},{16,48},{1,33},{17,49},{2,34},{18,50},{3,35},{19,51},{4,36}... | collective-permute-start | bytes 417800 | tf_op jit(solution)/shard_map/ppermute | solution.py:411
  60.3 2.6 %collective-permute-start.14 = (bf16[272,256]{1,0:T(8,128)(2,1)}, bf16[272,256]{1,0:T(8,128)(2,1)S(1)}, u32[]{:S(2)}, u32[]{:S(2)}) collective-permute-start(bf16[272,256]{1,0:T(8,128)(2,1)} %get-tuple-element.55.kv0), channel_id=1, source_target_pairs={{0,16},{16,32},{32,48},{1,17},{17,33},{33,49},{2,18},{18,34},{34,5... | collective-permute-start | bytes 417800 | tf_op jit(solution)/shard_map/ppermute | solution.py:410
  62.9 1.8 %collective-permute-start.17 = (bf16[272,256]{1,0:T(8,128)(2,1)}, bf16[272,256]{1,0:T(8,128)(2,1)S(1)}, u32[]{:S(2)}, u32[]{:S(2)}) collective-permute-start(bf16[272,256]{1,0:T(8,128)(2,1)} %get-tuple-element.55.kv0), channel_id=1, source_target_pairs={{0,8},{1,9},{2,10},{3,11},{4,12},{5,13},{6,14},{7,15},{16,24},{17,... | collective-permute-start | bytes 417800 | tf_op jit(solution)/shard_map/ppermute | solution.py:412
  64.8 1.3 collective-permute-start.18
  66.1 1.1 collective-permute-done.14.kv1
  69.4 13.0 %shard_map.103 = (bf16[256,1024]{1,0:T(8,128)(2,1)}, bf16[256,1024]{1,0:T(8,128)(2,1)}, f32[256,256]{1,0:T(8,128)S(1)}, f32[256,256]{1,0:T(8,128)S(1)}, f32[256,...) custom-call(s32[4]{0:T(128)S(1)} %copy-done.5, bf16[272,256]{1,0:T(8,128)(2,1)S(1)} %copy-done.8, ...), custom_call_target="tpu_custom_call" | custom-call | flops 4026531840 | bytes 6291456 | tf_op jit(solution)/shard_map/pallas_call | solution.py:115
  82.6 1.9 %collective-permute-done.19 = f32[2,256,256]{2,1,0:T(8,128)} collective-permute-done((f32[2,256,256]{2,1,0:T(8,128)S(1)}, f32[2,256,256]{2,1,0:T(8,128)}, u32[]{:S(2)}, u32[]{:S(2)}) %collective-permute-start.19) | collective-permute-done | bytes 524320 | tf_op jit(solution)/shard_map/ppermute | solution.py:388
  84.5 1.1 fusion.3
  85.6 1.3 collective-permute-start.20
  86.9 1.3 collective-permute-start.21
  88.2 5.5 %collective-permute-done.20 = bf16[256,256]{1,0:T(8,128)(2,1)S(1)} collective-permute-done((bf16[256,256]{1,0:T(8,128)(2,1)S(1)}, bf16[256,256]{1,0:T(8,128)(2,1)S(1)}, u32[]{:S(2)}, u32[]{:S(2)}) %collective-permute-start.20) | collective-permute-done | bytes 131104 | tf_op jit(solution)/shard_map/ppermute | solution.py:426
  93.7 3.1 %collective-permute-done.21 = bf16[256,256]{1,0:T(8,128)(2,1)S(1)} collective-permute-done((bf16[256,256]{1,0:T(8,128)(2,1)S(1)}, bf16[256,256]{1,0:T(8,128)(2,1)S(1)}, u32[]{:S(2)}, u32[]{:S(2)}) %collective-permute-start.21) | collective-permute-done | bytes 131104 | tf_op jit(solution)/shard_map/ppermute | solution.py:427
  97.8 1.6 %copy-done.2 = bf16[8192,128]{1,0:T(8,128)(2,1)S(1)} copy-done((bf16[8192,128]{1,0:T(8,128)(2,1)S(1)}, bf16[8192,128]{1,0:T(8,128)(2,1)}, u32[]{:S(2)}) %copy-start.2) | copy-done | bytes 2097176
  99.4 3.5 %shard_map.104 = (bf16[16,8192]{1,0:T(8,128)(2,1)S(1)}, bf16[16,8192]{1,0:T(8,128)(2,1)S(1)}, bf16[16,8192]{1,0:T(8,128)(2,1)S(1)}, bf16[16,8192]{1,0:T(8,128)(2...) custom-call(s32[4]{0:T(128)S(1)} %copy-done.5, ...), custom_call_target="tpu_custom_call" | custom-call | flops 536870912 | bytes 6291456 | tf_op jit(solution)/shard_map/pallas_call | solution.py:359
  103.0 3.2 %collective-permute-start.25 = (bf16[16,8192]{1,0:T(8,128)(2,1)S(1)}, bf16[16,8192]{1,0:T(8,128)(2,1)S(1)}, u32[]{:S(2)}, u32[]{:S(2)}) collective-permute-start(bf16[16,8192]{1,0:T(8,128)(2,1)S(1)} %get-tuple-element.66), channel_id=1, source_target_pairs={{0,7},{1,0},{2,1},{3,2},{4,3},{5,4},{6,5},{7,6},{8,15},{9,8},{10,9... | collective-permute-start | bytes 786440 | tf_op jit(solution)/shard_map/ppermute | solution.py:392
  106.2 1.3 collective-permute-done.22.gs_ref
  107.5 1.9 %collective-permute-start.33 = (bf16[16,8192]{1,0:T(8,128)(2,1)S(1)}, bf16[16,8192]{1,0:T(8,128)(2,1)S(1)}, u32[]{:S(2)}, u32[]{:S(2)}) collective-permute-start(bf16[16,8192]{1,0:T(8,128)(2,1)S(1)} %get-tuple-element.67), channel_id=1, source_target_pairs={{0,7},{1,0},{2,1},{3,2},{4,3},{5,4},{6,5},{7,6},{8,15},{9,8},{10,9... | collective-permute-start | bytes 786440 | tf_op jit(solution)/shard_map/ppermute | solution.py:392
  109.4 4.6 %shard_map.105 = bf16[16,256,256]{2,1,0:T(8,128)(2,1)S(1)} custom-call(s32[4]{0:T(128)S(1)} %copy-done.5, bf16[256,256]{1,0:T(8,128)(2,1)S(1)} %fusion.7.g_ref, bf16[256,256]{1,0:T(8,128)(2,1)S(1)} %collective-permute-done.22.gs_ref, bf16[256,4096]{1,0:T(8,128)(2,1)S(1)} %copy-done, bf16[256,4096]{1,0:T(8,128)(2,1)S(1)} %copy-done, ...), custom_call_target="tpu_custom_call" | custom-call | flops 1073741824 | bytes 6291456 | tf_op jit(solution)/shard_map/pallas_call | solution.py:294
  114.1 1.1 add_convert_fusion.10
  115.9 1.4 collective-permute-done.32
  117.5 7.0 %all-to-all-start = ((bf16[16,256,256]{2,1,0:T(8,128)(2,1)}), bf16[16,256,256]{2,1,0:T(8,128)(2,1)}, u32[]{:S(2)}, u32[]{:S(2)}) async-start(bf16[16,256,256]{2,1,0:T(8,128)(2,1)} %copy-done.4), calls=%async_computation | async-start | bytes 4194304 | tf_op jit(solution)/shard_map/all_to_all | solution.py:450
  124.4 3.0 %collective-permute-start.36 = (bf16[16,8192]{1,0:T(8,128)(2,1)S(1)}, bf16[16,8192]{1,0:T(8,128)(2,1)S(1)}, u32[]{:S(2)}, u32[]{:S(2)}) collective-permute-start(bf16[16,8192]{1,0:T(8,128)(2,1)S(1)} %add_convert_fusion.3), channel_id=1, source_target_pairs={{0,7},{1,0},{2,1},{3,2},{4,3},{5,4},{6,5},{7,6},{8,15},{9,8},{10,9... | collective-permute-start | bytes 786440 | tf_op jit(solution)/shard_map/ppermute | solution.py:392
  127.4 3.2 %collective-permute-start.29 = (bf16[16,8192]{1,0:T(8,128)(2,1)}, bf16[16,8192]{1,0:T(8,128)(2,1)S(1)}, u32[]{:S(2)}, u32[]{:S(2)}) collective-permute-start(bf16[16,8192]{1,0:T(8,128)(2,1)} %get-tuple-element.82), channel_id=1, source_target_pairs={{0,7},{1,0},{2,1},{3,2},{4,3},{5,4},{6,5},{7,6},{8,15},{9,8},{10,9... | collective-permute-start | bytes 786440 | tf_op jit(solution)/shard_map/ppermute | solution.py:392
  130.6 1.6 %copy-done.3 = bf16[8192,128]{1,0:T(8,128)(2,1)S(1)} copy-done((bf16[8192,128]{1,0:T(8,128)(2,1)S(1)}, bf16[8192,128]{1,0:T(8,128)(2,1)}, u32[]{:S(2)}) %copy-start.3) | copy-done | bytes 2097176
  132.2 3.5 %shard_map.106 = (bf16[16,8192]{1,0:T(8,128)(2,1)S(1)}, bf16[16,8192]{1,0:T(8,128)(2,1)S(1)}, bf16[16,8192]{1,0:T(8,128)(2,1)S(1)}, bf16[16,8192]{1,0:T(8,128)(2...) custom-call(s32[4]{0:T(128)S(1)} %copy-done.5, ...), custom_call_target="tpu_custom_call" | custom-call | flops 536870912 | bytes 6291456 | tf_op jit(solution)/shard_map/pallas_call | solution.py:359
  135.9 1.1 collective-permute-done.29
  137.0 3.7 %collective-permute-start.30 = (bf16[16,8192]{1,0:T(8,128)(2,1)S(1)}, bf16[16,8192]{1,0:T(8,128)(2,1)S(1)}, u32[]{:S(2)}, u32[]{:S(2)}) collective-permute-start(bf16[16,8192]{1,0:T(8,128)(2,1)S(1)} %add_convert_fusion.7), channel_id=1, source_target_pairs={{0,7},{1,0},{2,1},{3,2},{4,3},{5,4},{6,5},{7,6},{8,15},{9,8},{10,9... | collective-permute-start | bytes 786440 | tf_op jit(solution)/shard_map/ppermute | solution.py:392
  141.0 3.3 %collective-permute-start.37 = (bf16[16,8192]{1,0:T(8,128)(2,1)S(1)}, bf16[16,8192]{1,0:T(8,128)(2,1)S(1)}, u32[]{:S(2)}, u32[]{:S(2)}) collective-permute-start(bf16[16,8192]{1,0:T(8,128)(2,1)S(1)} %add_convert_fusion.2), channel_id=1, source_target_pairs={{0,7},{1,0},{2,1},{3,2},{4,3},{5,4},{6,5},{7,6},{8,15},{9,8},{10,9... | collective-permute-start | bytes 786440 | tf_op jit(solution)/shard_map/ppermute | solution.py:392
  145.1 2.2 %collective-permute-done.30 = bf16[16,8192]{1,0:T(8,128)(2,1)S(1)} collective-permute-done((bf16[16,8192]{1,0:T(8,128)(2,1)S(1)}, bf16[16,8192]{1,0:T(8,128)(2,1)S(1)}, u32[]{:S(2)}, u32[]{:S(2)}) %collective-permute-start.30) | collective-permute-done | bytes 262176 | tf_op jit(solution)/shard_map/ppermute | solution.py:392
  147.4 3.8 %collective-permute-start.31 = (bf16[16,8192]{1,0:T(8,128)(2,1)S(1)}, bf16[16,8192]{1,0:T(8,128)(2,1)S(1)}, u32[]{:S(2)}, u32[]{:S(2)}) collective-permute-start(bf16[16,8192]{1,0:T(8,128)(2,1)S(1)} %add_convert_fusion.6), channel_id=1, source_target_pairs={{0,7},{1,0},{2,1},{3,2},{4,3},{5,4},{6,5},{7,6},{8,15},{9,8},{10,9... | collective-permute-start | bytes 786440 | tf_op jit(solution)/shard_map/ppermute | solution.py:392
  151.2 2.4 %shard_map.107 = (f32[256,128]{1,0:T(8,128)}, f32[256,128]{1,0:T(8,128)}) custom-call(bf16[16,256,256]{2,1,0:T(8,128)(2,1)} %all-to-all-done.parts), custom_call_target="tpu_custom_call" | custom-call | tf_op jit(solution)/shard_map/pallas_call | solution.py:324
  153.6 1.1 collective-permute-done.28
  (97 shorter events, 9.8 us)
Async XLA Ops:
  1.7 39.7 %copy-start.9 = (bf16[16,8192]{1,0:T(8,128)(2,1)}, bf16[16,8192]{1,0:T(8,128)(2,1)S(1)}, u32[]{:S(2)}) copy-start(bf16[16,8192]{1,0:T(8,128)(2,1)S(1)} %get-tuple-element.101.refs_0_) | copy-start | bytes 786436
  1.7 39.7 %copy-start.10 = (bf16[16,8192]{1,0:T(8,128)(2,1)}, bf16[16,8192]{1,0:T(8,128)(2,1)S(1)}, u32[]{:S(2)}) copy-start(bf16[16,8192]{1,0:T(8,128)(2,1)S(1)} %get-tuple-element.102.refs_1_) | copy-start | bytes 786436
  1.7 13.1 %collective-permute-start.6 = (bf16[16,8192]{1,0:T(8,128)(2,1)S(1)}, bf16[16,8192]{1,0:T(8,128)(2,1)S(1)}, u32[]{:S(2)}, u32[]{:S(2)}) collective-permute-start(bf16[16,8192]{1,0:T(8,128)(2,1)S(1)} %get-tuple-element.101.refs_0_), channel_id=1, source_target_pairs={{0,1},{1,2},{2,3},{3,4},{4,5},{5,6},{6,7},{7,0},{8,9},{9,10},{10,1... | collective-permute-start | bytes 786440 | tf_op jit(solution)/shard_map/ppermute | solution.py:392
  3.7 11.1 %collective-permute-start.10 = (bf16[16,8192]{1,0:T(8,128)(2,1)S(1)}, bf16[16,8192]{1,0:T(8,128)(2,1)S(1)}, u32[]{:S(2)}, u32[]{:S(2)}) collective-permute-start(bf16[16,8192]{1,0:T(8,128)(2,1)S(1)} %get-tuple-element.102.refs_1_), channel_id=1, source_target_pairs={{0,7},{1,0},{2,1},{3,2},{4,3},{5,4},{6,5},{7,6},{8,15},{9,8},{10,9... | collective-permute-start | bytes 786440 | tf_op jit(solution)/shard_map/ppermute | solution.py:392
  7.7 12.3 %collective-permute-start.3 = (bf16[16,8192]{1,0:T(8,128)(2,1)S(1)}, bf16[16,8192]{1,0:T(8,128)(2,1)S(1)}, u32[]{:S(2)}, u32[]{:S(2)}) collective-permute-start(bf16[16,8192]{1,0:T(8,128)(2,1)S(1)} %get-tuple-element.101.refs_0_), channel_id=1, source_target_pairs={{0,7},{1,0},{2,1},{3,2},{4,3},{5,4},{6,5},{7,6},{8,15},{9,8},{10,9... | collective-permute-start | bytes 786440 | tf_op jit(solution)/shard_map/ppermute | solution.py:392
  9.7 14.1 %collective-permute-start = (bf16[16,8192]{1,0:T(8,128)(2,1)S(1)}, bf16[16,8192]{1,0:T(8,128)(2,1)S(1)}, u32[]{:S(2)}, u32[]{:S(2)}) collective-permute-start(bf16[16,8192]{1,0:T(8,128)(2,1)S(1)} %get-tuple-element.102.refs_1_), channel_id=1, source_target_pairs={{0,1},{1,2},{2,3},{3,4},{4,5},{5,6},{6,7},{7,0},{8,9},{9,10},{10,1... | collective-permute-start | bytes 786440 | tf_op jit(solution)/shard_map/ppermute | solution.py:392
  14.8 26.6 %copy-start.15 = (bf16[16,8192]{1,0:T(8,128)(2,1)}, bf16[16,8192]{1,0:T(8,128)(2,1)S(1)}, u32[]{:S(2)}) copy-start(bf16[16,8192]{1,0:T(8,128)(2,1)S(1)} %collective-permute-done.6.refs_2_) | copy-start | bytes 786436
  14.8 10.4 %collective-permute-start.7 = (bf16[16,8192]{1,0:T(8,128)(2,1)S(1)}, bf16[16,8192]{1,0:T(8,128)(2,1)S(1)}, u32[]{:S(2)}, u32[]{:S(2)}) collective-permute-start(bf16[16,8192]{1,0:T(8,128)(2,1)S(1)} %collective-permute-done.6.refs_2_), channel_id=1, source_target_pairs={{0,1},{1,2},{2,3},{3,4},{4,5},{5,6},{6,7},{7,0},{8,9},{9,10},{10,1... | collective-permute-start | bytes 786440 | tf_op jit(solution)/shard_map/ppermute | solution.py:392
  14.8 26.6 %copy-start.16 = (bf16[16,8192]{1,0:T(8,128)(2,1)}, bf16[16,8192]{1,0:T(8,128)(2,1)S(1)}, u32[]{:S(2)}) copy-start(bf16[16,8192]{1,0:T(8,128)(2,1)S(1)} %collective-permute-done.10.refs_5_) | copy-start | bytes 786436
  14.8 10.9 %collective-permute-start.11 = (bf16[16,8192]{1,0:T(8,128)(2,1)S(1)}, bf16[16,8192]{1,0:T(8,128)(2,1)S(1)}, u32[]{:S(2)}, u32[]{:S(2)}) collective-permute-start(bf16[16,8192]{1,0:T(8,128)(2,1)S(1)} %collective-permute-done.10.refs_5_), channel_id=1, source_target_pairs={{0,7},{1,0},{2,1},{3,2},{4,3},{5,4},{6,5},{7,6},{8,15},{9,8},{10,9... | collective-permute-start | bytes 786440 | tf_op jit(solution)/shard_map/ppermute | solution.py:392
  20.1 21.3 %copy-start.17 = (bf16[16,8192]{1,0:T(8,128)(2,1)}, bf16[16,8192]{1,0:T(8,128)(2,1)S(1)}, u32[]{:S(2)}) copy-start(bf16[16,8192]{1,0:T(8,128)(2,1)S(1)} %collective-permute-done.3.refs_4_) | copy-start | bytes 786436
  20.1 11.2 %collective-permute-start.4 = (bf16[16,8192]{1,0:T(8,128)(2,1)S(1)}, bf16[16,8192]{1,0:T(8,128)(2,1)S(1)}, u32[]{:S(2)}, u32[]{:S(2)}) collective-permute-start(bf16[16,8192]{1,0:T(8,128)(2,1)S(1)} %collective-permute-done.3.refs_4_), channel_id=1, source_target_pairs={{0,7},{1,0},{2,1},{3,2},{4,3},{5,4},{6,5},{7,6},{8,15},{9,8},{10,9... | collective-permute-start | bytes 786440 | tf_op jit(solution)/shard_map/ppermute | solution.py:392
  23.8 17.6 %copy-start.18 = (bf16[16,8192]{1,0:T(8,128)(2,1)}, bf16[16,8192]{1,0:T(8,128)(2,1)S(1)}, u32[]{:S(2)}) copy-start(bf16[16,8192]{1,0:T(8,128)(2,1)S(1)} %collective-permute-done.refs_3_) | copy-start | bytes 786436
  23.8 11.2 %collective-permute-start.1 = (bf16[16,8192]{1,0:T(8,128)(2,1)S(1)}, bf16[16,8192]{1,0:T(8,128)(2,1)}, u32[]{:S(2)}, u32[]{:S(2)}) collective-permute-start(bf16[16,8192]{1,0:T(8,128)(2,1)S(1)} %collective-permute-done.refs_3_), channel_id=1, source_target_pairs={{0,1},{1,2},{2,3},{3,4},{4,5},{5,6},{6,7},{7,0},{8,9},{9,10},{10,1... | collective-permute-start | bytes 786440 | tf_op jit(solution)/shard_map/ppermute | solution.py:392
  25.2 11.7 %collective-permute-start.8 = (bf16[16,8192]{1,0:T(8,128)(2,1)S(1)}, bf16[16,8192]{1,0:T(8,128)(2,1)}, u32[]{:S(2)}, u32[]{:S(2)}) collective-permute-start(bf16[16,8192]{1,0:T(8,128)(2,1)S(1)} %collective-permute-done.7.refs_6_), channel_id=1, source_target_pairs={{0,1},{1,2},{2,3},{3,4},{4,5},{5,6},{6,7},{7,0},{8,9},{9,10},{10,1... | collective-permute-start | bytes 786440 | tf_op jit(solution)/shard_map/ppermute | solution.py:392
  25.7 11.2 %collective-permute-start.12 = (bf16[16,8192]{1,0:T(8,128)(2,1)S(1)}, bf16[16,8192]{1,0:T(8,128)(2,1)}, u32[]{:S(2)}, u32[]{:S(2)}) collective-permute-start(bf16[16,8192]{1,0:T(8,128)(2,1)S(1)} %collective-permute-done.11.refs_9_), channel_id=1, source_target_pairs={{0,7},{1,0},{2,1},{3,2},{4,3},{5,4},{6,5},{7,6},{8,15},{9,8},{10,9... | collective-permute-start | bytes 786440 | tf_op jit(solution)/shard_map/ppermute | solution.py:392
  31.3 17.0 %collective-permute-start.5 = (bf16[16,8192]{1,0:T(8,128)(2,1)S(1)}, bf16[16,8192]{1,0:T(8,128)(2,1)S(1)}, u32[]{:S(2)}, u32[]{:S(2)}) collective-permute-start(bf16[16,8192]{1,0:T(8,128)(2,1)S(1)} %collective-permute-done.4.refs_8_), channel_id=1, source_target_pairs={{0,7},{1,0},{2,1},{3,2},{4,3},{5,4},{6,5},{7,6},{8,15},{9,8},{10,9... | collective-permute-start | bytes 786440 | tf_op jit(solution)/shard_map/ppermute | solution.py:392
  35.0 13.3 %collective-permute-start.2 = (bf16[16,8192]{1,0:T(8,128)(2,1)}, bf16[16,8192]{1,0:T(8,128)(2,1)S(1)}, u32[]{:S(2)}, u32[]{:S(2)}) collective-permute-start(bf16[16,8192]{1,0:T(8,128)(2,1)} %collective-permute-done.1.refs_7_), channel_id=1, source_target_pairs={{0,1},{1,2},{2,3},{3,4},{4,5},{5,6},{6,7},{7,0},{8,9},{9,10},{10,1... | collective-permute-start | bytes 786440 | tf_op jit(solution)/shard_map/ppermute | solution.py:392
  36.9 11.4 %collective-permute-start.9 = (bf16[16,8192]{1,0:T(8,128)(2,1)}, bf16[16,8192]{1,0:T(8,128)(2,1)S(1)}, u32[]{:S(2)}, u32[]{:S(2)}) collective-permute-start(bf16[16,8192]{1,0:T(8,128)(2,1)} %collective-permute-done.8.refs_10_), channel_id=1, source_target_pairs={{0,1},{1,2},{2,3},{3,4},{4,5},{5,6},{6,7},{7,0},{8,9},{9,10},{10,1... | collective-permute-start | bytes 786440 | tf_op jit(solution)/shard_map/ppermute | solution.py:392
  36.9 11.4 %collective-permute-start.13 = (bf16[16,8192]{1,0:T(8,128)(2,1)}, bf16[16,8192]{1,0:T(8,128)(2,1)S(1)}, u32[]{:S(2)}, u32[]{:S(2)}) collective-permute-start(bf16[16,8192]{1,0:T(8,128)(2,1)} %collective-permute-done.12.refs_11_), channel_id=1, source_target_pairs={{0,7},{1,0},{2,1},{3,2},{4,3},{5,4},{6,5},{7,6},{8,15},{9,8},{10,9... | collective-permute-start | bytes 786440 | tf_op jit(solution)/shard_map/ppermute | solution.py:392
  49.3 19.2 %copy-start.5 = (s32[4]{0:T(128)S(1)}, s32[4]{0:T(128)}, u32[]{:S(2)}) copy-start(s32[4]{0:T(128)} %pad_add_fusion.place_ref) | copy-start | bytes 52
  49.3 19.2 %copy-start.6 = (bf16[1,256,1024]{2,1,0:T(8,128)(2,1)S(1)}, bf16[1,256,1024]{2,1,0:T(8,128)(2,1)}, u32[]{:S(2)}) copy-start(bf16[1,256,1024]{2,1,0:T(8,128)(2,1)} %param.9) | copy-start | bytes 1572868
  49.3 19.2 %copy-start.7 = (bf16[1,256,1024]{2,1,0:T(8,128)(2,1)S(1)}, bf16[1,256,1024]{2,1,0:T(8,128)(2,1)}, u32[]{:S(2)}) copy-start(bf16[1,256,1024]{2,1,0:T(8,128)(2,1)} %param.10) | copy-start | bytes 1572868
  55.1 54.3 %collective-permute-start.23 = (bf16[256,4096]{1,0:T(8,128)(2,1)}, bf16[256,4096]{1,0:T(8,128)(2,1)}, u32[]{:S(2)}, u32[]{:S(2)}) collective-permute-start(bf16[256,4096]{1,0:T(8,128)(2,1)} %get-tuple-element.72), channel_id=1, source_target_pairs={{0,8},{8,0},{1,9},{9,1},{2,10},{10,2},{3,11},{11,3},{4,12},{12,4},... | collective-permute-start | bytes 6291464 | tf_op jit(solution)/shard_map/ppermute | solution.py:388
  55.2 9.6 %collective-permute-start.15 = (bf16[272,256]{1,0:T(8,128)(2,1)}, bf16[272,256]{1,0:T(8,128)(2,1)S(1)}, u32[]{:S(2)}, u32[]{:S(2)}) collective-permute-start(bf16[272,256]{1,0:T(8,128)(2,1)} %get-tuple-element.55.kv0), channel_id=1, source_target_pairs={{0,32},{16,48},{1,33},{17,49},{2,34},{18,50},{3,35},{19,51},{4,36}... | collective-permute-start | bytes 417800 | tf_op jit(solution)/shard_map/ppermute | solution.py:411
  60.3 6.9 %collective-permute-start.14 = (bf16[272,256]{1,0:T(8,128)(2,1)}, bf16[272,256]{1,0:T(8,128)(2,1)S(1)}, u32[]{:S(2)}, u32[]{:S(2)}) collective-permute-start(bf16[272,256]{1,0:T(8,128)(2,1)} %get-tuple-element.55.kv0), channel_id=1, source_target_pairs={{0,16},{16,32},{32,48},{1,17},{17,33},{33,49},{2,18},{18,34},{34,5... | collective-permute-start | bytes 417800 | tf_op jit(solution)/shard_map/ppermute | solution.py:410
  62.9 4.4 %collective-permute-start.17 = (bf16[272,256]{1,0:T(8,128)(2,1)}, bf16[272,256]{1,0:T(8,128)(2,1)S(1)}, u32[]{:S(2)}, u32[]{:S(2)}) collective-permute-start(bf16[272,256]{1,0:T(8,128)(2,1)} %get-tuple-element.55.kv0), channel_id=1, source_target_pairs={{0,8},{1,9},{2,10},{3,11},{4,12},{5,13},{6,14},{7,15},{16,24},{17,... | collective-permute-start | bytes 417800 | tf_op jit(solution)/shard_map/ppermute | solution.py:412
  64.8 3.3 %collective-permute-start.18 = (bf16[272,256]{1,0:T(8,128)(2,1)S(1)}, bf16[272,256]{1,0:T(8,128)(2,1)S(1)}, u32[]{:S(2)}, u32[]{:S(2)}) collective-permute-start(bf16[272,256]{1,0:T(8,128)(2,1)S(1)} %collective-permute-done.15.kv2), channel_id=1, source_target_pairs={{8,0},{9,1},{10,2},{11,3},{12,4},{13,5},{14,6},{15,7},{24,16},{25,... | collective-permute-start | bytes 417800 | tf_op jit(solution)/shard_map/ppermute | solution.py:414
  67.2 1.4 collective-permute-start.16
  82.5 2.0 %collective-permute-start.19 = (f32[2,256,256]{2,1,0:T(8,128)S(1)}, f32[2,256,256]{2,1,0:T(8,128)}, u32[]{:S(2)}, u32[]{:S(2)}) collective-permute-start(f32[2,256,256]{2,1,0:T(8,128)S(1)} %get-tuple-element.59), channel_id=1, source_target_pairs={{0,8},{8,0},{1,9},{9,1},{2,10},{10,2},{3,11},{11,3},{4,12},{12,4},... | collective-permute-start | bytes 1572872 | tf_op jit(solution)/shard_map/ppermute | solution.py:388
  85.6 8.1 %collective-permute-start.20 = (bf16[256,256]{1,0:T(8,128)(2,1)S(1)}, bf16[256,256]{1,0:T(8,128)(2,1)S(1)}, u32[]{:S(2)}, u32[]{:S(2)}) collective-permute-start(bf16[256,256]{1,0:T(8,128)(2,1)S(1)} %get-tuple-element.99), channel_id=1, source_target_pairs={{16,0},{32,16},{48,32},{17,1},{33,17},{49,33},{18,2},{34,18},{50,3... | collective-permute-start | bytes 393224 | tf_op jit(solution)/shard_map/ppermute | solution.py:426
  86.9 9.8 %collective-permute-start.21 = (bf16[256,256]{1,0:T(8,128)(2,1)S(1)}, bf16[256,256]{1,0:T(8,128)(2,1)S(1)}, u32[]{:S(2)}, u32[]{:S(2)}) collective-permute-start(bf16[256,256]{1,0:T(8,128)(2,1)S(1)} %get-tuple-element.100), channel_id=1, source_target_pairs={{32,0},{48,16},{33,1},{49,17},{34,2},{50,18},{35,3},{51,19},{36,4}... | collective-permute-start | bytes 393224 | tf_op jit(solution)/shard_map/ppermute | solution.py:427
  102.9 11.2 %collective-permute-start.24 = (bf16[16,8192]{1,0:T(8,128)(2,1)S(1)}, bf16[16,8192]{1,0:T(8,128)(2,1)S(1)}, u32[]{:S(2)}, u32[]{:S(2)}) collective-permute-start(bf16[16,8192]{1,0:T(8,128)(2,1)S(1)} %get-tuple-element.65), channel_id=1, source_target_pairs={{0,1},{1,2},{2,3},{3,4},{4,5},{5,6},{6,7},{7,0},{8,9},{9,10},{10,1... | collective-permute-start | bytes 786440 | tf_op jit(solution)/shard_map/ppermute | solution.py:392
  103.0 11.1 %collective-permute-start.25 = (bf16[16,8192]{1,0:T(8,128)(2,1)S(1)}, bf16[16,8192]{1,0:T(8,128)(2,1)S(1)}, u32[]{:S(2)}, u32[]{:S(2)}) collective-permute-start(bf16[16,8192]{1,0:T(8,128)(2,1)S(1)} %get-tuple-element.66), channel_id=1, source_target_pairs={{0,7},{1,0},{2,1},{3,2},{4,3},{5,4},{6,5},{7,6},{8,15},{9,8},{10,9... | collective-permute-start | bytes 786440 | tf_op jit(solution)/shard_map/ppermute | solution.py:392
  106.2 1.3 collective-permute-start.22
  106.2 11.1 %collective-permute-start.32 = (bf16[16,8192]{1,0:T(8,128)(2,1)S(1)}, bf16[16,8192]{1,0:T(8,128)(2,1)S(1)}, u32[]{:S(2)}, u32[]{:S(2)}) collective-permute-start(bf16[16,8192]{1,0:T(8,128)(2,1)S(1)} %get-tuple-element.64), channel_id=1, source_target_pairs={{0,1},{1,2},{2,3},{3,4},{4,5},{5,6},{6,7},{7,0},{8,9},{9,10},{10,1... | collective-permute-start | bytes 786440 | tf_op jit(solution)/shard_map/ppermute | solution.py:392
  107.5 9.8 %collective-permute-start.33 = (bf16[16,8192]{1,0:T(8,128)(2,1)S(1)}, bf16[16,8192]{1,0:T(8,128)(2,1)S(1)}, u32[]{:S(2)}, u32[]{:S(2)}) collective-permute-start(bf16[16,8192]{1,0:T(8,128)(2,1)S(1)} %get-tuple-element.67), channel_id=1, source_target_pairs={{0,7},{1,0},{2,1},{3,2},{4,3},{5,4},{6,5},{7,6},{8,15},{9,8},{10,9... | collective-permute-start | bytes 786440 | tf_op jit(solution)/shard_map/ppermute | solution.py:392
  115.1 20.6 %collective-permute-start.26 = (bf16[16,8192]{1,0:T(8,128)(2,1)}, bf16[16,8192]{1,0:T(8,128)(2,1)S(1)}, u32[]{:S(2)}, u32[]{:S(2)}) collective-permute-start(bf16[16,8192]{1,0:T(8,128)(2,1)} %get-tuple-element.79), channel_id=1, source_target_pairs={{0,1},{1,2},{2,3},{3,4},{4,5},{5,6},{6,7},{7,0},{8,9},{9,10},{10,1... | collective-permute-start | bytes 786440 | tf_op jit(solution)/shard_map/ppermute | solution.py:392
  117.5 33.7 %all-to-all-start = ((bf16[16,256,256]{2,1,0:T(8,128)(2,1)}), bf16[16,256,256]{2,1,0:T(8,128)(2,1)}, u32[]{:S(2)}, u32[]{:S(2)}) async-start(bf16[16,256,256]{2,1,0:T(8,128)(2,1)} %copy-done.4), calls=%async_computation | async-start | bytes 4194304 | tf_op jit(solution)/shard_map/all_to_all | solution.py:450
  124.4 16.5 %collective-permute-start.36 = (bf16[16,8192]{1,0:T(8,128)(2,1)S(1)}, bf16[16,8192]{1,0:T(8,128)(2,1)S(1)}, u32[]{:S(2)}, u32[]{:S(2)}) collective-permute-start(bf16[16,8192]{1,0:T(8,128)(2,1)S(1)} %add_convert_fusion.3), channel_id=1, source_target_pairs={{0,7},{1,0},{2,1},{3,2},{4,3},{5,4},{6,5},{7,6},{8,15},{9,8},{10,9... | collective-permute-start | bytes 786440 | tf_op jit(solution)/shard_map/ppermute | solution.py:392
  127.4 13.3 %collective-permute-start.34 = (bf16[16,8192]{1,0:T(8,128)(2,1)S(1)}, bf16[16,8192]{1,0:T(8,128)(2,1)S(1)}, u32[]{:S(2)}, u32[]{:S(2)}) collective-permute-start(bf16[16,8192]{1,0:T(8,128)(2,1)S(1)} %add_convert_fusion.5), channel_id=1, source_target_pairs={{0,1},{1,2},{2,3},{3,4},{4,5},{5,6},{6,7},{7,0},{8,9},{9,10},{10,1... | collective-permute-start | bytes 786440 | tf_op jit(solution)/shard_map/ppermute | solution.py:392
  127.4 9.6 %collective-permute-start.29 = (bf16[16,8192]{1,0:T(8,128)(2,1)}, bf16[16,8192]{1,0:T(8,128)(2,1)S(1)}, u32[]{:S(2)}, u32[]{:S(2)}) collective-permute-start(bf16[16,8192]{1,0:T(8,128)(2,1)} %get-tuple-element.82), channel_id=1, source_target_pairs={{0,7},{1,0},{2,1},{3,2},{4,3},{5,4},{6,5},{7,6},{8,15},{9,8},{10,9... | collective-permute-start | bytes 786440 | tf_op jit(solution)/shard_map/ppermute | solution.py:392
  135.8 9.2 %collective-permute-start.27 = (bf16[16,8192]{1,0:T(8,128)(2,1)S(1)}, bf16[16,8192]{1,0:T(8,128)(2,1)S(1)}, u32[]{:S(2)}, u32[]{:S(2)}) collective-permute-start(bf16[16,8192]{1,0:T(8,128)(2,1)S(1)} %add_convert_fusion.9), channel_id=1, source_target_pairs={{0,1},{1,2},{2,3},{3,4},{4,5},{5,6},{6,7},{7,0},{8,9},{9,10},{10,1... | collective-permute-start | bytes 786440 | tf_op jit(solution)/shard_map/ppermute | solution.py:392
  137.0 10.3 %collective-permute-start.30 = (bf16[16,8192]{1,0:T(8,128)(2,1)S(1)}, bf16[16,8192]{1,0:T(8,128)(2,1)S(1)}, u32[]{:S(2)}, u32[]{:S(2)}) collective-permute-start(bf16[16,8192]{1,0:T(8,128)(2,1)S(1)} %add_convert_fusion.7), channel_id=1, source_target_pairs={{0,7},{1,0},{2,1},{3,2},{4,3},{5,4},{6,5},{7,6},{8,15},{9,8},{10,9... | collective-permute-start | bytes 786440 | tf_op jit(solution)/shard_map/ppermute | solution.py:392
  140.8 12.8 %collective-permute-start.35 = (bf16[16,8192]{1,0:T(8,128)(2,1)S(1)}, bf16[16,8192]{1,0:T(8,128)(2,1)S(1)}, u32[]{:S(2)}, u32[]{:S(2)}) collective-permute-start(bf16[16,8192]{1,0:T(8,128)(2,1)S(1)} %add_convert_fusion.4), channel_id=1, source_target_pairs={{0,1},{1,2},{2,3},{3,4},{4,5},{5,6},{6,7},{7,0},{8,9},{9,10},{10,1... | collective-permute-start | bytes 786440 | tf_op jit(solution)/shard_map/ppermute | solution.py:392
  141.0 12.6 %collective-permute-start.37 = (bf16[16,8192]{1,0:T(8,128)(2,1)S(1)}, bf16[16,8192]{1,0:T(8,128)(2,1)S(1)}, u32[]{:S(2)}, u32[]{:S(2)}) collective-permute-start(bf16[16,8192]{1,0:T(8,128)(2,1)S(1)} %add_convert_fusion.2), channel_id=1, source_target_pairs={{0,7},{1,0},{2,1},{3,2},{4,3},{5,4},{6,5},{7,6},{8,15},{9,8},{10,9... | collective-permute-start | bytes 786440 | tf_op jit(solution)/shard_map/ppermute | solution.py:392
  145.1 9.6 %collective-permute-start.28 = (bf16[16,8192]{1,0:T(8,128)(2,1)S(1)}, bf16[16,8192]{1,0:T(8,128)(2,1)S(1)}, u32[]{:S(2)}, u32[]{:S(2)}) collective-permute-start(bf16[16,8192]{1,0:T(8,128)(2,1)S(1)} %add_convert_fusion.8), channel_id=1, source_target_pairs={{0,1},{1,2},{2,3},{3,4},{4,5},{5,6},{6,7},{7,0},{8,9},{9,10},{10,1... | collective-permute-start | bytes 786440 | tf_op jit(solution)/shard_map/ppermute | solution.py:392
  147.4 7.9 %collective-permute-start.31 = (bf16[16,8192]{1,0:T(8,128)(2,1)S(1)}, bf16[16,8192]{1,0:T(8,128)(2,1)S(1)}, u32[]{:S(2)}, u32[]{:S(2)}) collective-permute-start(bf16[16,8192]{1,0:T(8,128)(2,1)S(1)} %add_convert_fusion.6), channel_id=1, source_target_pairs={{0,7},{1,0},{2,1},{3,2},{4,3},{5,4},{6,5},{7,6},{8,15},{9,8},{10,9... | collective-permute-start | bytes 786440 | tf_op jit(solution)/shard_map/ppermute | solution.py:392
  (13 other events, 78.1 us)
